TPU v7x, 32 devices: a whole 2x2x4 slice. The times are simulated.
32 devices in a mesh: grp: 2 (over y), obs: 4 (over z), par: 4 (over x, core).
Axes of the slice: x: 2, y: 2, z: 4, core: 2. Of those that a mesh axis runs over, the one named last changes fastest.
Arguments:
- predicted: bfloat16 [256, 786432], P(None, ('grp', 'obs', 'par')), parts along dimension 1, may hold values from -120 to 120
- observed: float32 [786432], P(('grp', 'obs', 'par')), parts along dimension 0, may hold values from -120 to 120
- band: float32 [8, 786432], P(None, ('grp', 'obs', 'par')), parts along dimension 1, may hold values from -5 to 5
- offsets: int32 [8], replicated, may hold values from -1024 to 1024, as said below
- rows_count: int32 [32], P(('grp', 'obs', 'par')), parts along dimension 0, may hold values from 12288 to 23552, as said below
- params: bfloat16 [16384, 256], P(('grp', 'obs', 'par')), parts along dimension 0, may hold values from -6 to 6
Outputs:
- params_new: float32 [16384, 256], P(('grp', 'obs', 'par')), parts along dimension 0
- whitened_misfit: float32 [786432], P(('grp', 'obs', 'par')), parts along dimension 0
There are 2 independent parts, one for each index of `grp`. A program takes and returns all parts, laid end to end along the dimension named above; an argument that names none is the same for every part. Nothing has to cross between parts.
Inputs may be any that keep to these rules, and one draw needn't show every extreme that they name: offsets[0] is 0, the 8 offsets are distinct, and both -1024 and 1024 are among them. `rows_count`: every shard holds this many strain observations first, then load observations up to its last 1024 observations, which are strain observations again; in every draw some shard holds exactly 23552 leading strain observations and some exactly 12288.
All inputs are finite; a program needn't handle non-finite values.
Results may differ from a plain program's by a relative error of at most 0.0029.
Values may be sent and summed in bfloat16 or wider, within the bound.
No kernel may reach another device: no remote copies, remote signals or barrier semaphores. Data moves between devices by JAX's collectives and lax.ppermute only.
A program may use at most 256 MiB of HBM per device.

v0:
```python
import functools
import math

import jax
import jax.numpy as jnp
from jax import lax
from jax.experimental import pallas as pl
from jax.experimental.pallas import tpu as pltpu
from jax.sharding import PartitionSpec as P

H = 1024
LANE = 128
PACK = 16
BLOCK = 64
PANEL = 8
BF = jnp.bfloat16
F32 = jnp.float32


def local_kernel(edge, columns, obs_total, *refs):
    if edge:
        (off_ref, count_ref, pred_ref, obs_ref, band_ref, left_ref, right_ref, gram_in, misfit_in,
         gram_out, misfit_out, raw, joint, aw_a, aw_b, coef, gram, centre, row_out, slots, sems) = refs
    else:
        (off_ref, count_ref, pred_ref, obs_ref, band_ref,
         gram_out, misfit_out, raw, joint, aw_a, aw_b, coef, gram, centre, slots, sems) = refs
    members = pred_ref.shape[0]
    rows = members + PACK
    terms = band_ref.shape[0]
    chunks = columns // H
    tiles = H // LANE
    slices = 4
    part = H // slices
    row_factor = 1.0 / math.sqrt(obs_total)

    if edge:
        copies = [
            pltpu.make_async_copy(left_ref, raw.at[:, pl.ds(0, H)], sems.at[0]),
            pltpu.make_async_copy(right_ref, raw.at[:, pl.ds(5 * H, H)], sems.at[5]),
        ]
        for place, chunk in ((1, 0), (2, 1), (3, chunks - 2), (4, chunks - 1)):
            copies.append(pltpu.make_async_copy(
                pred_ref.at[:, pl.ds(chunk * H, H)],
                raw.at[pl.ds(0, members), pl.ds(place * H, H)], sems.at[place]))
        for copy in copies:
            copy.start()
    else:
        def chunk_copy(place):
            start = pl.multiple_of(place * H, H)
            return pltpu.make_async_copy(
                pred_ref.at[:, pl.ds(start, H)], raw.at[:, pl.ds(start, H)], sems.at[place])

        for place in range(chunks):
            chunk_copy(place).start()

    slots[0, 0] = 0
    slots[0, 1] = 0
    free = jnp.int32(3)
    for term in range(1, terms):
        offset = off_ref[term]
        whole = (offset == H) | (offset == -H)
        place = jnp.where(offset == -H, 1, jnp.where(offset == H, 2, free))
        place = jnp.minimum(place, terms - 1)
        slots[place, 0] = jnp.int32(term)
        slots[place, 1] = offset
        free = free + jnp.where(whole, 0, 1)

    row_index = lax.broadcasted_iota(jnp.int32, (rows, members), 0)
    col_index = lax.broadcasted_iota(jnp.int32, (rows, members), 1)
    mean_part = 1.0 / members
    centre[...] = jnp.where(
        row_index >= members, mean_part, jnp.where(row_index == col_index, 1.0 - mean_part, -mean_part)
    ).astype(BF)
    if edge:
        gram[...] = jnp.zeros_like(gram)
    else:
        gram[...] = jnp.zeros_like(gram)
        aw_b[...] = jnp.zeros_like(aw_b)

    def anomalies(place, step, obs_row):
        at = pl.multiple_of(place * H + step * part, part)
        wide = jnp.dot(centre[...], raw[pl.ds(0, members), pl.ds(at, part)], preferred_element_type=F32)
        joint[pl.ds(0, members), pl.ds(at, part)] = wide[:members].astype(BF)
        joint[pl.ds(members, PACK), pl.ds(at, part)] = (obs_row - wide[members:]).astype(BF)

    def coefficients(column):
        index = column + lax.broadcasted_iota(jnp.int32, (1, H), 1)
        strained = (index < count_ref[0]) | (index >= columns - H)
        strain = jnp.where(strained, row_factor, 0.0)
        for slot in range(terms):
            term = slots[slot, 0]
            row = band_ref[pl.ds(term, 1), pl.ds(column, H)]
            row = row * (row_factor if slot == 0 else strain)
            coef[pl.ds(slot * 8, 8), :] = jnp.broadcast_to(row, (8, H))

    def whiten_rows(place, at_row):
        lane = lax.broadcasted_iota(jnp.int32, (PACK, LANE), 1)
        acc = [None] * tiles

        def load(tile):
            start = pl.multiple_of(tile * LANE, LANE)
            return joint[pl.ds(at_row, PACK), pl.ds(start, LANE)]

        for slot in range(terms):
            offset = slots[slot, 1]
            if slot < 3:
                first = place * tiles + (0, -tiles, tiles)[slot]
                values = [load(first + t) for t in range(tiles)]
            else:
                turn = lax.rem(offset + 8 * LANE, LANE)
                first = place * tiles + lax.div(offset + 8 * LANE, LANE) - 8
                back = lax.rem(LANE - turn, LANE)
                keep = lane < LANE - turn
                rolled = [pltpu.roll(load(first + t), back, 1) for t in range(tiles + 1)]
                values = [jnp.where(keep, rolled[t], rolled[t + 1]) for t in range(tiles)]
            for t in range(tiles):
                weight = coef[pl.ds(slot * 8, 8), pl.ds(t * LANE, LANE)]
                weight = jnp.concatenate([weight, weight], 0)
                product = values[t].astype(F32) * weight
                acc[t] = product if acc[t] is None else acc[t] + product
        return acc

    def products(aw, step):
        at = step * part if isinstance(step, int) else pl.multiple_of(step * part, part)
        block = aw[:, pl.ds(at, part)]
        gram[...] += lax.dot_general(
            block, block[:members], (((1,), (1,)), ((), ())), preferred_element_type=F32)

    def whiten_chunk(place, column, aw, before, store_misfit, more=None):
        coefficients(column)
        acc = whiten_rows(place, members)
        row = lax.broadcasted_iota(jnp.int32, (PACK, LANE), 0)
        for t in range(tiles):
            wide = acc[t]
            high = wide.astype(BF).astype(F32)
            rest = wide - high
            middle = rest.astype(BF).astype(F32)
            low = rest - middle
            split = jnp.where(row == 0, high, jnp.where(row == 1, middle, jnp.where(row == 2, low, 0.0)))
            aw[pl.ds(members, PACK), pl.ds(t * LANE, LANE)] = split.astype(BF)
            store_misfit(t, wide[0:1] * math.sqrt(members - 1))

        def step_body(step, carry):
            if before is not None:
                products(before, step)
            for piece in range(members // PACK // slices):
                at_row = pl.multiple_of(step * (members // slices) + piece * PACK, PACK)
                out = whiten_rows(place, at_row)
                for t in range(tiles):
                    aw[pl.ds(at_row, PACK), pl.ds(t * LANE, LANE)] = out[t].astype(BF)
            if more is not None:
                more(step)
            return carry

        lax.fori_loop(0, slices, step_body, 0)

    if edge:
        for copy in copies:
            copy.wait()
        for place, chunk in ((0, None), (1, 0), (2, 1), (3, chunks - 2), (4, chunks - 1), (5, None)):
            def edge_step(step, carry):
                if chunk is None:
                    at = pl.multiple_of(place * H + step * part, part)
                    pieces = raw[pl.ds(members, PACK), pl.ds(at, part)].astype(F32)
                    obs_row = pieces[0:1] + pieces[1:2] + pieces[2:3]
                else:
                    obs_row = obs_ref[:, pl.ds(pl.multiple_of(chunk * H + step * part, part), part)]
                anomalies(place, step, obs_row)
                return carry
            lax.fori_loop(0, slices, edge_step, 0)
        for place, chunk, aw, before in ((1, 0, aw_a, None), (4, chunks - 1, aw_b, aw_a)):
            def store_misfit(t, value):
                row_out[:, pl.ds((0 if place == 1 else H) + t * LANE, LANE)] = value
            whiten_chunk(place, chunk * H, aw, before, store_misfit)
        out_copies = [
            pltpu.make_async_copy(row_out.at[:, pl.ds(0, H)], misfit_out.at[:, pl.ds(0, H)], sems.at[0]),
            pltpu.make_async_copy(row_out.at[:, pl.ds(H, H)], misfit_out.at[:, pl.ds(columns - H, H)], sems.at[1]),
        ]
        for copy in out_copies:
            copy.start()
        for step in range(slices):
            products(aw_b, step)
        gram_out[pl.ds(0, members), :] = gram_in[pl.ds(0, members), :] + gram[pl.ds(0, members), :]
        tail = gram[pl.ds(members, 8), :]
        total = tail[0:1] + tail[1:2] + tail[2:3]
        first = lax.broadcasted_iota(jnp.int32, (8, members), 0) == 0
        gram_out[pl.ds(members, 8), :] = gram_in[pl.ds(members, 8), :] + jnp.where(first, total, 0.0)
        for copy in out_copies:
            copy.wait()
    else:
        def make_ready(place, step):
            obs_row = obs_ref[:, pl.ds(pl.multiple_of(place * H + step * part, part), part)]
            anomalies(place, step, obs_row)

        for place in range(3):
            chunk_copy(place).wait()

            def first_step(step, carry, place=place):
                make_ready(place, step)
                return carry
            lax.fori_loop(0, slices, first_step, 0)

        def chunk_step(place, aw, before):
            ahead = jnp.minimum(place + 2, chunks - 1)

            @pl.when(place + 2 < chunks)
            def _():
                chunk_copy(ahead).wait()

            column = pl.multiple_of(place * H, H)

            def store_misfit(t, value):
                misfit_out[:, pl.ds(column + t * LANE, LANE)] = value

            whiten_chunk(place, column, aw, before, store_misfit, lambda step: make_ready(ahead, step))

        def pair(index, carry):
            chunk_step(1 + 2 * index, aw_a, aw_b)
            chunk_step(2 + 2 * index, aw_b, aw_a)
            return carry

        lax.fori_loop(0, (chunks - 2) // 2, pair, 0)
        for step in range(slices):
            products(aw_b, step)
        gram_out[pl.ds(0, members), :] = gram[pl.ds(0, members), :]
        tail = gram[pl.ds(members, 8), :]
        total = tail[0:1] + tail[1:2] + tail[2:3]
        first = lax.broadcasted_iota(jnp.int32, (8, members), 0) == 0
        gram_out[pl.ds(members, 8), :] = jnp.where(first, total, 0.0)


def local_call(edge, obs_total, offsets, rows_count, predicted, observed, band, *more):
    members, columns = predicted.shape
    rows = members + PACK
    places = 6 if edge else columns // H
    vmem = pl.BlockSpec(memory_space=pltpu.VMEM)
    smem = pl.BlockSpec(memory_space=pltpu.SMEM)
    anywhere = pl.BlockSpec(memory_space=pl.ANY)
    in_specs = [smem, smem, anywhere, vmem, vmem]
    out_specs = [vmem, anywhere if edge else vmem]
    if edge:
        in_specs += [anywhere, anywhere, vmem, anywhere]
    scratch = [
        pltpu.VMEM((rows if edge else members, places * H), BF),
        pltpu.VMEM((rows, places * H), BF),
        pltpu.VMEM((rows, H), BF),
        pltpu.VMEM((rows, H), BF),
        pltpu.VMEM((8 * band.shape[0], H), F32),
        pltpu.VMEM((rows, members), F32),
        pltpu.VMEM((rows, members), BF),
    ]
    if edge:
        scratch.append(pltpu.VMEM((1, 2 * H), F32))
    scratch += [pltpu.SMEM((8, 2), jnp.int32), pltpu.SemaphoreType.DMA((places,))]
    work = 2 if edge else places - 2
    return pl.pallas_call(
        functools.partial(local_kernel, edge, columns, obs_total),
        out_shape=(
            jax.ShapeDtypeStruct((members + 8, members), F32),
            jax.ShapeDtypeStruct((1, columns), F32),
        ),
        in_specs=in_specs,
        out_specs=out_specs,
        scratch_shapes=scratch,
        input_output_aliases={8: 1} if edge else {},
        compiler_params=pltpu.CompilerParams(vmem_limit_bytes=50 * 2**20),
        cost_estimate=pl.CostEstimate(
            flops=2 * rows * members * H * work * 2, bytes_accessed=members * H * places * 2, transcendentals=0),
        name="edges" if edge else "inner",
    )(offsets, rows_count, predicted, observed, band, *more)


def update_kernel(sum_ref, params_ref, out_ref, work):
    members = params_ref.shape[1]
    highest = lax.Precision.HIGHEST
    row_index = lax.broadcasted_iota(jnp.int32, (members, members), 0)
    col_index = lax.broadcasted_iota(jnp.int32, (members, members), 1)
    identity = jnp.where(row_index == col_index, 1.0, 0.0).astype(F32)
    work[:, pl.ds(0, members)] = sum_ref[pl.ds(0, members), :] + identity
    work[:, pl.ds(members, members)] = identity
    panels = BLOCK // PANEL
    sub = lax.broadcasted_iota(jnp.int32, (PANEL, LANE), 0)
    eye = identity[:BLOCK, :BLOCK]

    def across(tile, column):
        return jnp.broadcast_to(tile[:, column:column + 1], (PANEL, LANE))

    def down(tile, row):
        return jnp.broadcast_to(tile[row:row + 1, :], (PANEL, LANE))

    for block in range(members // BLOCK):
        r0 = block * BLOCK
        start = jnp.concatenate([work[pl.ds(r0, BLOCK), pl.ds(r0, BLOCK)], eye], axis=1)
        tiles = [start[PANEL * t:PANEL * (t + 1)] for t in range(panels)]
        done = []
        for p in range(panels):
            c0 = PANEL * p
            tile = tiles[p]
            upper = tile
            full = tile
            cols = [across(tile, c0 + j) for j in range(PANEL)]
            full_cols = list(cols)
            scale = jnp.zeros((PANEL, LANE), F32)
            for k in range(PANEL):
                pivot = down(cols[k], k)
                inverse = 1.0 / pivot
                scale = jnp.where(sub == k, pivot, scale)
                below = jnp.where(sub > k, cols[k] * inverse, 0.0)

                def clear(values):
                    row = down(values, k) * inverse
                    return jnp.where(sub == k, row, values - full_cols[k] * row)

                for j in range(k + 1, PANEL):
                    cols[j] = cols[j] - below * down(cols[j], k)
                    full_cols[j] = clear(full_cols[j])
                upper = upper - below * down(upper, k)
                full = clear(full)
            done.append(upper * lax.rsqrt(scale))
            rows_of = [down(full, k) for k in range(PANEL)]
            for t in range(p + 1, panels):
                tile_t = tiles[t]
                change = [across(tile_t, c0 + k) * rows_of[k] for k in range(PANEL)]
                while len(change) > 1:
                    change = [a + b for a, b in zip(change[::2], change[1::2])]
                tiles[t] = tile_t - change[0]
        lower_inverse = jnp.concatenate(done, axis=0)[:, BLOCK:2 * BLOCK]
        solved = jnp.dot(lower_inverse, work[pl.ds(r0, BLOCK), :], precision=highest, preferred_element_type=F32)
        work[pl.ds(r0, BLOCK), :] = solved
        if r0 + BLOCK < members:
            rest = members - r0 - BLOCK
            factor = solved[:, r0 + BLOCK:members]
            work[pl.ds(r0 + BLOCK, rest), :] = work[pl.ds(r0 + BLOCK, rest), :] - lax.dot_general(
                factor, solved, (((0,), (0,)), ((), ())), precision=highest, preferred_element_type=F32)

    inverse = jnp.where(row_index >= col_index, work[:, pl.ds(members, members)], 0.0)
    projection = sum_ref[pl.ds(members, 1), :]
    half = jnp.sum(inverse * projection, axis=1, keepdims=True)
    weights = jnp.sum(inverse * half, axis=0, keepdims=True)
    turned = inverse + weights
    turned = turned - jnp.mean(turned, axis=1, keepdims=True) + 1.0 / members
    high = turned.astype(BF)
    rest = turned - high.astype(F32)
    middle = rest.astype(BF)
    low = (rest - middle.astype(F32)).astype(BF)
    params = params_ref[...]

    def times(part):
        return lax.dot_general(params, part, (((1,), (1,)), ((), ())), preferred_element_type=F32)

    out_ref[...] = times(high) + (times(middle) + times(low))


def update(total, params):
    members = params.shape[1]
    vmem = pl.BlockSpec(memory_space=pltpu.VMEM)
    return pl.pallas_call(
        update_kernel,
        out_shape=jax.ShapeDtypeStruct(params.shape, F32),
        in_specs=[vmem, vmem],
        out_specs=vmem,
        scratch_shapes=[pltpu.VMEM((members, 2 * members), F32)],
        compiler_params=pltpu.CompilerParams(vmem_limit_bytes=32 * 2**20),
        name="update",
    )(total, params)


def halo_block(predicted, observed):
    high = lax.reduce_precision(observed, 8, 7)
    rest = observed - high
    middle = lax.reduce_precision(rest, 8, 7)
    low = rest - middle
    pieces = jnp.concatenate(
        [high[None], middle[None], low[None], jnp.zeros((PACK - 3, observed.shape[0]), F32)], 0)
    return jnp.concatenate([predicted, pieces.astype(BF)], 0)


def body(predicted, observed, band, offsets, rows_count, params):
    columns = predicted.shape[1]
    axes = ("obs", "par")
    shards = lax.axis_size(axes)
    obs_total = columns * shards
    up = [(i, i + 1) for i in range(shards - 1)]
    down = [(j, i) for i, j in up]
    left = lax.ppermute(halo_block(predicted[:, columns - H:], observed[columns - H:]), axes, up)
    right = lax.ppermute(halo_block(predicted[:, :H], observed[:H]), axes, down)
    obs_row = observed[None, :]
    gram, misfit = local_call(False, obs_total, offsets, rows_count, predicted, obs_row, band)
    gram, misfit = local_call(
        True, obs_total, offsets, rows_count, predicted, obs_row, band, left, right, gram, misfit)
    total = lax.psum(gram, axes)
    return (update(total, params), misfit[0])


def solution(mesh):
    in_specs = (
        P(None, ("grp", "obs", "par")),
        P(("grp", "obs", "par")),
        P(None, ("grp", "obs", "par")),
        P(),
        P(("grp", "obs", "par")),
        P(("grp", "obs", "par"), None),
    )
    out_specs = (P(("grp", "obs", "par"), None), P(("grp", "obs", "par")))
    return jax.shard_map(body, mesh=mesh, in_specs=in_specs, out_specs=out_specs, check_vma=False)
```

profile of v0, /device:TPU:0, one launch (start us, length us, event | category | flops | bytes accessed | tf_op | source)
XLA Modules:
  0.0 204.9 jit_solution(16392940568153790793)
XLA Ops:
  7.2 0.0 all-reduce.2.cloned.1.call-start
  7.2 0.7 fusion.1
  8.0 1.3 fusion.2
  9.2 0.3 concatenate.13
  9.6 1.3 collective-permute-start.1
  10.9 0.3 concatenate.12
  11.3 3.1 %collective-permute-start = (bf16[272,1024]{1,0:T(8,128)(2,1)S(1)}, bf16[272,1024]{1,0:T(8,128)(2,1)S(1)}, u32[]{:S(2)}, u32[]{:S(2)}) collective-permute-start(bf16[272,1024]{1,0:T(8,128)(2,1)S(1)} %concatenate.12), channel_id=1, source_target_pairs={{0,1},{1,2},{2,3},{3,4},{4,5},{5,6},{6,7},{7,8},{8,9},{9,10},{10,1... | collective-permute-start | bytes 1671176 | tf_op jit(solution)/shard_map/ppermute | solution.py:385
  15.0 0.0 copy-start
  15.0 1.1 copy-done
  16.1 0.0 copy-start.3
  16.1 0.9 copy-done.3
  17.0 0.0 copy-start.4
  17.0 0.7 copy-done.4
  17.7 62.3 %inner.1 = (f32[264,256]{1,0:T(8,128)S(1)}, f32[1,24576]{1,0:T(1,128)}) custom-call(s32[8]{0:T(128)S(1)} %copy-done.4, s32[1]{0:T(128)S(6)} %copy.11.refs_1_, bf16[256,24576]{1,0:T(8,128)(2,1)} %refs_2_.3, f32[1,24576]{1,0:T(1,128)S(1)} %bitcast.2, f32[8,24576]{1,0:T(8,128)S(1)} %copy-done), custom_call_target="tpu_custom_call" | custom-call | flops 6274678784 | bytes 12582912 | tf_op jit(solution)/shard_map/inner/pallas_call | solution.py:256
  80.0 0.0 copy-start.2
  80.0 0.0 collective-permute-done.1.refs_6_
  80.1 0.0 collective-permute-done.refs_5_
  80.1 12.2 %edges.1 = (f32[264,256]{1,0:T(8,128)}, f32[1,24576]{1,0:T(1,128)}) custom-call(s32[8]{0:T(128)S(1)} %copy-done.4, s32[1]{0:T(128)S(6)} %copy.11.refs_1_, bf16[256,24576]{1,0:T(8,128)(2,1)} %refs_2_.3, f32[1,24576]{1,0:T(1,128)S(1)} %bitcast.3, f32[8,24576]{1,0:T(8,128)S(1)} %copy-done, ...), custom_call_target="tpu_custom_call", output_to_operand_aliasing={{1}: (8, {})} | custom-call | flops 570425344 | bytes 3145728 | tf_op jit(solution)/shard_map/edges/pallas_call | solution.py:256
  92.2 0.0 all-reduce.2.cloned.1.call-update
  92.2 92.4 %all-reduce.2.cloned.1.call-done.sum_ref = f32[264,256]{1,0:T(8,128)} async-done(((f32[264,256]{1,0:T(8,128)}), f32[264,256]{1,0:T(8,128)}) %all-reduce.2.cloned.1.call-update) | async-done | bytes 270352 | tf_op jit(solution)/shard_map/psum | solution.py:391
  184.6 0.0 copy-done.2
  184.6 0.0 copy-start.1
  184.6 1.0 copy-done.1
  185.6 12.4 %update.1 = f32[512,256]{1,0:T(8,128)} custom-call(f32[264,256]{1,0:T(8,128)S(1)} %copy-done.1, bf16[512,256]{1,0:T(8,128)(2,1)S(1)} %copy-done.2), custom_call_target="tpu_custom_call" | custom-call | tf_op jit(solution)/shard_map/update/pallas_call | solution.py:357
  (7 shorter events, 0.0 us)
Async XLA Ops:
  7.2 177.5 %all-reduce.2.cloned.1.call-start = ((), (), s32[]{:S(2)}) async-start(), calls=%async_computation | async-start | bytes 540672 | tf_op jit(solution)/shard_map/psum | solution.py:391
  9.6 70.5 %collective-permute-start.1 = (bf16[272,1024]{1,0:T(8,128)(2,1)S(1)}, bf16[272,1024]{1,0:T(8,128)(2,1)S(1)}, u32[]{:S(2)}, u32[]{:S(2)}) collective-permute-start(bf16[272,1024]{1,0:T(8,128)(2,1)S(1)} %concatenate.13), channel_id=1, source_target_pairs={{1,0},{2,1},{3,2},{4,3},{5,4},{6,5},{7,6},{8,7},{9,8},{10,9},{11,1... | collective-permute-start | bytes 1671176 | tf_op jit(solution)/shard_map/ppermute | solution.py:386
  11.3 68.8 %collective-permute-start = (bf16[272,1024]{1,0:T(8,128)(2,1)S(1)}, bf16[272,1024]{1,0:T(8,128)(2,1)S(1)}, u32[]{:S(2)}, u32[]{:S(2)}) collective-permute-start(bf16[272,1024]{1,0:T(8,128)(2,1)S(1)} %concatenate.12), channel_id=1, source_target_pairs={{0,1},{1,2},{2,3},{3,4},{4,5},{5,6},{6,7},{7,8},{8,9},{9,10},{10,1... | collective-permute-start | bytes 1671176 | tf_op jit(solution)/shard_map/ppermute | solution.py:385
  15.0 1.1 copy-start
  16.1 0.9 copy-start.3
  17.0 0.7 copy-start.4
  80.0 104.6 %copy-start.2 = (bf16[512,256]{1,0:T(8,128)(2,1)S(1)}, bf16[512,256]{1,0:T(8,128)(2,1)}, u32[]{:S(2)}) copy-start(bf16[512,256]{1,0:T(8,128)(2,1)} %params_ref.1) | copy-start | bytes 786436
  184.6 1.0 copy-start.1
Sparse Core Ops, SparseCore 0:
  92.4 92.2 all-reduce.1
where the time goes:
time: 205 us
  waiting for transfers between devices  92.4 us (45%)
  Pallas kernels  86.9 us (42%)
  between operations  14.8 us (7%)
  local copies, waits for them, and re-layouts  5.62 us (3%)
  starting transfers between devices  4.39 us (2%)
    psum x1, waiting for transfers between devices, body(): total = lax.psum(gram, axes)  92.4 us
    pallas_call x2, Pallas kernels, local_call(): pl.pallas_call(functools.partial(local_kernel, edge, columns, obs_total),...  74.5 us
    pallas_call x1, Pallas kernels, update(): pl.pallas_call(update_kernel, out_shape=jax.ShapeDtypeStruct(params.shape...  12.4 us
  transfers between devices with their start and end apart: 3, of which 1 were waited for; matrix products, arithmetic and copies ran while one was open for 0% of the time, Pallas kernels for 30%

commit v1 on v0

v1 whole, which is shorter than its diff:
```python
import functools
import math

import jax
import jax.numpy as jnp
from jax import lax
from jax.experimental import pallas as pl
from jax.experimental.pallas import tpu as pltpu
from jax.sharding import PartitionSpec as P

H = 1024
LANE = 128
PACK = 16
BLOCK = 64
PANEL = 8
BF = jnp.bfloat16
F32 = jnp.float32


def local_kernel(edge, columns, obs_total, *refs):
    if edge:
        (off_ref, count_ref, pred_ref, obs_ref, band_ref, left_ref, right_ref, gram_in, misfit_in,
         gram_out, misfit_out, raw, joint, fresh, aw_a, aw_b, coef, gram, centre, obs, band, row_out, slots,
         sems) = refs
    else:
        (off_ref, count_ref, pred_ref, obs_ref, band_ref,
         gram_out, misfit_out, raw, joint, fresh, aw_a, aw_b, coef, gram, centre, obs, band, row_out, slots,
         sems) = refs
    members = pred_ref.shape[0]
    terms = band_ref.shape[0]
    chunks = columns // H
    tiles = H // LANE
    half = members // 2
    row_factor = 1.0 / math.sqrt(obs_total)

    if edge:
        copies = [
            pltpu.make_async_copy(left_ref, raw.at[:, pl.ds(0, H)], sems.at[0]),
            pltpu.make_async_copy(right_ref, raw.at[:, pl.ds(5 * H, H)], sems.at[5]),
        ]
        for place, chunk in ((1, 0), (2, 1), (3, chunks - 2), (4, chunks - 1)):
            copies.append(pltpu.make_async_copy(
                pred_ref.at[:, pl.ds(chunk * H, H)],
                raw.at[pl.ds(0, members), pl.ds(place * H, H)], sems.at[place]))
        for which in range(2):
            there = which * (columns - 2 * H)
            copies.append(pltpu.make_async_copy(
                obs_ref.at[:, pl.ds(there, 2 * H)], obs.at[:, pl.ds(which * 2 * H, 2 * H)], sems.at[6 + which]))
            there = which * (columns - H)
            copies.append(pltpu.make_async_copy(
                band_ref.at[:, pl.ds(there, H)], band.at[:, pl.ds(which * H, H)], sems.at[8 + which]))
        for copy in copies:
            copy.start()
    else:
        def chunk_copy(place):
            start = pl.multiple_of(place * H, H)
            return pltpu.make_async_copy(
                pred_ref.at[:, pl.ds(start, H)], raw.at[:, pl.ds(start, H)], sems.at[place])

        copies = [
            pltpu.make_async_copy(obs_ref, obs, sems.at[chunks]),
            pltpu.make_async_copy(band_ref, band, sems.at[chunks + 1]),
        ]
        for place in range(chunks):
            chunk_copy(place).start()
            if place == 2:
                for copy in copies:
                    copy.start()

    slots[0, 0] = 0
    slots[0, 1] = 0
    free = jnp.int32(3)
    for term in range(1, terms):
        offset = off_ref[term]
        whole = (offset == H) | (offset == -H)
        place = jnp.where(offset == -H, 1, jnp.where(offset == H, 2, free))
        place = jnp.minimum(place, terms - 1)
        slots[place, 0] = jnp.int32(term)
        slots[place, 1] = offset
        free = free + jnp.where(whole, 0, 1)

    rows = members + PACK
    row_index = lax.broadcasted_iota(jnp.int32, (rows, members), 0)
    col_index = lax.broadcasted_iota(jnp.int32, (rows, members), 1)
    mean_part = 1.0 / members
    centre[...] = jnp.where(
        row_index >= members, mean_part, jnp.where(row_index == col_index, 1.0 - mean_part, -mean_part)
    ).astype(BF)
    gram[...] = jnp.zeros_like(gram)
    if not edge:
        aw_b[...] = jnp.zeros_like(aw_b)

    def anomalies(place, obs_row, target, at):
        wide = jnp.dot(
            centre[...], raw[pl.ds(0, members), pl.ds(pl.multiple_of(place * H, H), H)],
            preferred_element_type=F32)
        target[pl.ds(0, members), pl.ds(at, H)] = wide[:members].astype(BF)
        target[pl.ds(members, PACK), pl.ds(at, H)] = (obs_row - wide[members:]).astype(BF)

    def coefficients(column, at):
        index = column + lax.broadcasted_iota(jnp.int32, (1, H), 1)
        strained = (index < count_ref[0]) | (index >= columns - H)
        strain = jnp.where(strained, row_factor, 0.0)
        for slot in range(terms):
            term = slots[slot, 0]
            row = band[pl.ds(term, 1), pl.ds(at, H)]
            row = row * (row_factor if slot == 0 else strain)
            coef[pl.ds(slot * 8, 8), :] = jnp.broadcast_to(row, (8, H))

    def plan(place):
        lane = lax.broadcasted_iota(jnp.int32, (PACK, LANE), 1)
        steps = []
        for slot in range(terms):
            if slot < 3:
                steps.append((place * tiles + (0, -tiles, tiles)[slot], None, None))
            else:
                offset = slots[slot, 1] + 8 * LANE
                turn = lax.rem(offset, LANE)
                first = place * tiles + lax.div(offset, LANE) - 8
                steps.append((first, lax.rem(LANE - turn, LANE), lane < LANE - turn))
        return steps

    def whiten_rows(steps, starts, low, width):
        acc = [[None] * width for _ in starts]
        for slot, (first, back, keep) in enumerate(steps):
            weights = []
            for t in range(width):
                weight = coef[pl.ds(slot * 8, 8), pl.ds((low + t) * LANE, LANE)]
                weights.append(jnp.concatenate([weight, weight], 0))
            for r, at_row in enumerate(starts):
                def load(t):
                    start = pl.multiple_of((first + low + t) * LANE, LANE)
                    return joint[pl.ds(at_row, PACK), pl.ds(start, LANE)]

                if back is None:
                    values = [load(t) for t in range(width)]
                else:
                    rolled = [pltpu.roll(load(t), back, 1) for t in range(width + 1)]
                    values = [jnp.where(keep, rolled[t], rolled[t + 1]) for t in range(width)]
                for t in range(width):
                    product = values[t].astype(F32) * weights[t]
                    acc[r][t] = product if acc[r][t] is None else acc[r][t] + product
        return acc

    def products(aw):
        gram[...] += lax.dot_general(
            aw[...], aw[pl.ds(0, members), :], (((1,), (1,)), ((), ())), preferred_element_type=F32)

    def whiten_chunk(place, column, at, aw, out_at):
        coefficients(column, at)
        steps = plan(place)
        acc = whiten_rows(steps, [members], 0, tiles)[0]
        row = lax.broadcasted_iota(jnp.int32, (PACK, LANE), 0)
        for t in range(tiles):
            wide = acc[t]
            high = wide.astype(BF).astype(F32)
            rest = wide - high
            middle = rest.astype(BF).astype(F32)
            low = rest - middle
            split = jnp.where(row == 0, high, jnp.where(row == 1, middle, jnp.where(row == 2, low, 0.0)))
            aw[pl.ds(members, PACK), pl.ds(t * LANE, LANE)] = split.astype(BF)
            row_out[:, pl.ds(out_at + t * LANE, LANE)] = wide[0:1] * math.sqrt(members - 1)
        width = tiles // 2
        for group in range(members // (2 * PACK)):
            starts = [group * 2 * PACK, group * 2 * PACK + PACK]
            for low in (0, width):
                acc = whiten_rows(steps, starts, low, width)
                for r, at_row in enumerate(starts):
                    for t in range(width):
                        aw[pl.ds(at_row, PACK), pl.ds((low + t) * LANE, LANE)] = acc[r][t].astype(BF)

    if edge:
        for copy in copies:
            copy.wait()
        for place in range(6):
            if place in (0, 5):
                pieces = raw[pl.ds(members, PACK), pl.ds(place * H, H)].astype(F32)
                obs_row = pieces[0:1] + pieces[1:2] + pieces[2:3]
            else:
                obs_row = obs[:, pl.ds((place - 1) * H, H)]
            anomalies(place, obs_row, joint, place * H)
        whiten_chunk(1, 0, 0, aw_a, 0)
        products(aw_a)
        whiten_chunk(4, columns - H, H, aw_b, H)
        out_copies = [
            pltpu.make_async_copy(row_out.at[:, pl.ds(0, H)], misfit_out.at[:, pl.ds(0, H)], sems.at[0]),
            pltpu.make_async_copy(row_out.at[:, pl.ds(H, H)], misfit_out.at[:, pl.ds(columns - H, H)], sems.at[1]),
        ]
        for copy in out_copies:
            copy.start()
        products(aw_b)
    else:
        def ready(place, target, at):
            anomalies(place, obs[:, pl.ds(pl.multiple_of(place * H, H), H)], target, at)

        for copy in copies:
            copy.wait()
        for place in range(3):
            chunk_copy(place).wait()
            ready(place, *((joint, place * H) if place < 2 else (fresh, 0)))

        def chunk_step(place, aw, before):
            ahead = jnp.minimum(place + 2, chunks - 1)

            @pl.when(place + 2 < chunks)
            def _():
                chunk_copy(ahead).wait()

            column = pl.multiple_of(place * H, H)
            joint[:, pl.ds(pl.multiple_of(column + H, H), H)] = fresh[...]
            products(before)
            whiten_chunk(place, column, column, aw, column)
            ready(ahead, fresh, 0)

        def pair(index, carry):
            chunk_step(1 + 2 * index, aw_a, aw_b)
            chunk_step(2 + 2 * index, aw_b, aw_a)
            return carry

        lax.fori_loop(0, (chunks - 2) // 2, pair, 0)
        inside = pl.ds(H, columns - 2 * H)
        out_copies = [pltpu.make_async_copy(row_out.at[:, inside], misfit_out.at[:, inside], sems.at[0])]
        for copy in out_copies:
            copy.start()
        products(aw_b)

    tail = gram[pl.ds(members, 8), :]
    total = tail[0:1] + tail[1:2] + tail[2:3]
    both = gram[pl.ds(0, members), :]
    top = lax.broadcasted_iota(jnp.int32, (half, half), 0)
    corner = jnp.where(top == 0, total[:, :half], jnp.where(top == 1, total[:, half:], 0.0))
    upper = jnp.concatenate([both[:half, :half], corner], 1)
    lower = both[half:]
    if edge:
        upper = upper + gram_in[pl.ds(0, half), :]
        lower = lower + gram_in[pl.ds(half, half), :]
    gram_out[pl.ds(0, half), :] = upper
    gram_out[pl.ds(half, half), :] = lower
    for copy in out_copies:
        copy.wait()


def local_call(edge, obs_total, offsets, rows_count, predicted, observed, band, *more):
    members, columns = predicted.shape
    terms = band.shape[0]
    rows = members + PACK
    places = 6 if edge else columns // H
    vmem = pl.BlockSpec(memory_space=pltpu.VMEM)
    smem = pl.BlockSpec(memory_space=pltpu.SMEM)
    anywhere = pl.BlockSpec(memory_space=pl.ANY)
    in_specs = [smem, smem, anywhere, anywhere, anywhere]
    if edge:
        in_specs += [anywhere, anywhere, vmem, anywhere]
    scratch = [
        pltpu.VMEM((rows if edge else members, places * H), BF),
        pltpu.VMEM((rows, places * H), BF),
        pltpu.VMEM((rows, H), BF),
        pltpu.VMEM((rows, H), BF),
        pltpu.VMEM((rows, H), BF),
        pltpu.VMEM((8 * terms, H), F32),
        pltpu.VMEM((rows, members), F32),
        pltpu.VMEM((rows, members), BF),
        pltpu.VMEM((1, 4 * H if edge else columns), F32),
        pltpu.VMEM((terms, 2 * H if edge else columns), F32),
        pltpu.VMEM((1, 2 * H if edge else columns), F32),
        pltpu.SMEM((8, 2), jnp.int32),
        pltpu.SemaphoreType.DMA((places + 4,)),
    ]
    work = 2 if edge else places - 2
    return pl.pallas_call(
        functools.partial(local_kernel, edge, columns, obs_total),
        out_shape=(
            jax.ShapeDtypeStruct((members, members), F32),
            jax.ShapeDtypeStruct((1, columns), F32),
        ),
        in_specs=in_specs,
        out_specs=[vmem, anywhere],
        scratch_shapes=scratch,
        input_output_aliases={8: 1} if edge else {},
        compiler_params=pltpu.CompilerParams(vmem_limit_bytes=50 * 2**20),
        cost_estimate=pl.CostEstimate(
            flops=2 * rows * members * H * work * 2, bytes_accessed=members * H * places * 2, transcendentals=0),
        name="edges" if edge else "inner",
    )(offsets, rows_count, predicted, observed, band, *more)


def update_kernel(sum_ref, params_ref, out_ref, work):
    members = params_ref.shape[1]
    highest = lax.Precision.HIGHEST
    row_index = lax.broadcasted_iota(jnp.int32, (members, members), 0)
    col_index = lax.broadcasted_iota(jnp.int32, (members, members), 1)
    identity = jnp.where(row_index == col_index, 1.0, 0.0).astype(F32)
    half = members // 2
    work[:, pl.ds(0, half)] = sum_ref[:, pl.ds(0, half)] + identity[:, :half]
    work[pl.ds(0, half), pl.ds(half, half)] = sum_ref[pl.ds(half, half), pl.ds(0, half)].T
    work[pl.ds(half, half), pl.ds(half, half)] = sum_ref[pl.ds(half, half), pl.ds(half, half)] + identity[half:, half:]
    work[:, pl.ds(members, members)] = identity
    panels = BLOCK // PANEL
    sub = lax.broadcasted_iota(jnp.int32, (PANEL, LANE), 0)
    eye = identity[:BLOCK, :BLOCK]

    def across(tile, column):
        return jnp.broadcast_to(tile[:, column:column + 1], (PANEL, LANE))

    def down(tile, row):
        return jnp.broadcast_to(tile[row:row + 1, :], (PANEL, LANE))

    for block in range(members // BLOCK):
        r0 = block * BLOCK
        start = jnp.concatenate([work[pl.ds(r0, BLOCK), pl.ds(r0, BLOCK)], eye], axis=1)
        tiles = [start[PANEL * t:PANEL * (t + 1)] for t in range(panels)]
        done = []
        for p in range(panels):
            c0 = PANEL * p
            tile = tiles[p]
            upper = tile
            full = tile
            cols = [across(tile, c0 + j) for j in range(PANEL)]
            full_cols = list(cols)
            scale = jnp.zeros((PANEL, LANE), F32)
            for k in range(PANEL):
                pivot = down(cols[k], k)
                inverse = 1.0 / pivot
                scale = jnp.where(sub == k, pivot, scale)
                below = jnp.where(sub > k, cols[k] * inverse, 0.0)

                def clear(values):
                    row = down(values, k) * inverse
                    return jnp.where(sub == k, row, values - full_cols[k] * row)

                for j in range(k + 1, PANEL):
                    cols[j] = cols[j] - below * down(cols[j], k)
                    full_cols[j] = clear(full_cols[j])
                upper = upper - below * down(upper, k)
                full = clear(full)
            done.append(upper * lax.rsqrt(scale))
            rows_of = [down(full, k) for k in range(PANEL)]
            for t in range(p + 1, panels):
                tile_t = tiles[t]
                change = [across(tile_t, c0 + k) * rows_of[k] for k in range(PANEL)]
                while len(change) > 1:
                    change = [a + b for a, b in zip(change[::2], change[1::2])]
                tiles[t] = tile_t - change[0]
        lower_inverse = jnp.concatenate(done, axis=0)[:, BLOCK:2 * BLOCK]
        solved = jnp.dot(lower_inverse, work[pl.ds(r0, BLOCK), :], precision=highest, preferred_element_type=F32)
        work[pl.ds(r0, BLOCK), :] = solved
        if r0 + BLOCK < members:
            rest = members - r0 - BLOCK
            factor = solved[:, r0 + BLOCK:members]
            work[pl.ds(r0 + BLOCK, rest), :] = work[pl.ds(r0 + BLOCK, rest), :] - lax.dot_general(
                factor, solved, (((0,), (0,)), ((), ())), precision=highest, preferred_element_type=F32)

    inverse = jnp.where(row_index >= col_index, work[:, pl.ds(members, members)], 0.0)
    projection = jnp.concatenate([sum_ref[pl.ds(r, 1), pl.ds(half, half)] for r in range(2)], 1)
    solved = jnp.sum(inverse * projection, axis=1, keepdims=True)
    weights = jnp.sum(inverse * solved, axis=0, keepdims=True)
    turned = inverse + weights
    turned = turned - jnp.mean(turned, axis=1, keepdims=True) + 1.0 / members
    high = turned.astype(BF)
    rest = turned - high.astype(F32)
    middle = rest.astype(BF)
    low = (rest - middle.astype(F32)).astype(BF)
    params = params_ref[...]

    def times(part):
        return lax.dot_general(params, part, (((1,), (1,)), ((), ())), preferred_element_type=F32)

    out_ref[...] = times(high) + (times(middle) + times(low))


def update(total, params):
    members = params.shape[1]
    vmem = pl.BlockSpec(memory_space=pltpu.VMEM)
    return pl.pallas_call(
        update_kernel,
        out_shape=jax.ShapeDtypeStruct(params.shape, F32),
        in_specs=[vmem, vmem],
        out_specs=vmem,
        scratch_shapes=[pltpu.VMEM((members, 2 * members), F32)],
        compiler_params=pltpu.CompilerParams(vmem_limit_bytes=32 * 2**20),
        name="update",
    )(total, params)


def halo_block(predicted, observed):
    high = lax.reduce_precision(observed, 8, 7)
    rest = observed - high
    middle = lax.reduce_precision(rest, 8, 7)
    low = rest - middle
    pieces = jnp.concatenate(
        [high[None], middle[None], low[None], jnp.zeros((PACK - 3, observed.shape[0]), F32)], 0)
    return jnp.concatenate([predicted, pieces.astype(BF)], 0)


def sum_over(values, axes):
    shards = lax.axis_size(axes)
    rows, width = values.shape
    parts = lax.all_to_all(values, axes, 0, 0, tiled=True)
    own = jnp.sum(parts.reshape(shards, rows // shards, width), axis=0)
    copies = jnp.broadcast_to(own[None], (shards, rows // shards, width)).reshape(rows, width)
    return lax.all_to_all(copies, axes, 0, 0, tiled=True)


def body(predicted, observed, band, offsets, rows_count, params):
    columns = predicted.shape[1]
    axes = ("obs", "par")
    shards = lax.axis_size(axes)
    obs_total = columns * shards
    up = [(i, i + 1) for i in range(shards - 1)]
    down = [(j, i) for i, j in up]
    left = lax.ppermute(halo_block(predicted[:, columns - H:], observed[columns - H:]), axes, up)
    right = lax.ppermute(halo_block(predicted[:, :H], observed[:H]), axes, down)
    obs_row = observed[None, :]
    gram, misfit = local_call(False, obs_total, offsets, rows_count, predicted, obs_row, band)
    gram, misfit = local_call(
        True, obs_total, offsets, rows_count, predicted, obs_row, band, left, right, gram, misfit)
    total = sum_over(gram, axes)
    return (update(total, params), misfit[0])


def solution(mesh):
    in_specs = (
        P(None, ("grp", "obs", "par")),
        P(("grp", "obs", "par")),
        P(None, ("grp", "obs", "par")),
        P(),
        P(("grp", "obs", "par")),
        P(("grp", "obs", "par"), None),
    )
    out_specs = (P(("grp", "obs", "par"), None), P(("grp", "obs", "par")))
    return jax.shard_map(body, mesh=mesh, in_specs=in_specs, out_specs=out_specs, check_vma=False)
```

time: 205 us -> 105 us (0.51)
  waiting for transfers between devices: 92.4 us -> 0.01 us
  blocking collectives: 0 us -> 30.6 us
  Pallas kernels: 86.9 us -> 62.4 us
  between operations: 14.8 us -> 1.42 us
    psum x1 -> x0, waiting for transfers between devices: 92.4 us -> none  [body(): total = lax.psum(gram, axes)]
    all_to_all x0 -> x2, blocking collectives: none -> 30.6 us  [the longest x1 17.7 us: sum_over(): parts = lax.all_to_all(values, axes, 0, 0, tiled=True)]
    pallas_call x2, Pallas kernels: 74.5 us -> 50 us  [local_call(): pl.pallas_call(functools.partial(local_kernel, edge, columns, obs_total),...]
  transfers between devices with their start and end apart: 3 -> 2, of which waited for: 1 -> 0; matrix products, arithmetic and copies ran while one was open for 0% -> 0% of each run, Pallas kernels for 30% -> 41%
where the time goes in v1:
time: 105 us; the launch traced here: 104 us
  Pallas kernels  62.4 us (59%)
  blocking collectives  30.6 us (29%)
  local copies, waits for them, and re-layouts  4.68 us (4%)
  starting transfers between devices  4.36 us (4%)
  between operations  1.42 us (1%)
    pallas_call x2, Pallas kernels, local_call(): pl.pallas_call(functools.partial(local_kernel, edge, columns, obs_total),...  50 us
    all_to_all x1, blocking collectives, sum_over(): parts = lax.all_to_all(values, axes, 0, 0, tiled=True)  17.7 us
    all_to_all x1, blocking collectives, sum_over(): return lax.all_to_all(copies, axes, 0, 0, tiled=True)  12.8 us
    pallas_call x1, Pallas kernels, update(): pl.pallas_call(update_kernel, out_shape=jax.ShapeDtypeStruct(params.shape...  12.4 us
    ppermute x1, starting transfers between devices, body(): lax.ppermute(halo_block(predicted[:, columns - H:], observed[columns - H:...  3.07 us
    unnamed x8, local copies, waits for them, and re-layouts  2.68 us
  transfers between devices with their start and end apart: 2, of which 0 were waited for; matrix products, arithmetic and copies ran while one was open for 0% of the time, Pallas kernels for 41%

profile of v1, /device:TPU:0, one launch (start us, length us, event | category | flops | bytes accessed | tf_op | source)
XLA Modules:
  0.0 104.2 jit_solution(6589883780334616522)
XLA Ops:
  0.6 0.7 fusion.1
  1.4 1.3 %fusion.2 = (bf16[256,1024]{1,0:T(8,128)(2,1)S(1)}, bf16[256,1024]{1,0:T(8,128)(2,1)S(1)}) fusion(bf16[256,24576]{1,0:T(8,128)(2,1)} %refs_2_.3), kind=kLoop, calls=%fused_computation.10 | loop fusion | bytes 2097152 | tf_op jit(solution)/shard_map/slice | solution.py:412
  2.7 0.3 concatenate.13
  3.0 1.3 %collective-permute-start.1 = (bf16[272,1024]{1,0:T(8,128)(2,1)S(1)}, bf16[272,1024]{1,0:T(8,128)(2,1)S(1)}, u32[]{:S(2)}, u32[]{:S(2)}) collective-permute-start(bf16[272,1024]{1,0:T(8,128)(2,1)S(1)} %concatenate.13), channel_id=1, source_target_pairs={{1,0},{2,1},{3,2},{4,3},{5,4},{6,5},{7,6},{8,7},{9,8},{10,9},{11,1... | collective-permute-start | bytes 1671176 | tf_op jit(solution)/shard_map/ppermute | solution.py:412
  4.3 0.3 concatenate.12
  4.7 3.1 %collective-permute-start = (bf16[272,1024]{1,0:T(8,128)(2,1)S(1)}, bf16[272,1024]{1,0:T(8,128)(2,1)S(1)}, u32[]{:S(2)}, u32[]{:S(2)}) collective-permute-start(bf16[272,1024]{1,0:T(8,128)(2,1)S(1)} %concatenate.12), channel_id=1, source_target_pairs={{0,1},{1,2},{2,3},{3,4},{4,5},{5,6},{6,7},{7,8},{8,9},{9,10},{10,1... | collective-permute-start | bytes 1671176 | tf_op jit(solution)/shard_map/ppermute | solution.py:411
  8.4 0.0 copy-start
  8.4 1.1 %copy-done = f32[8,24576]{1,0:T(8,128)S(1)} copy-done((f32[8,24576]{1,0:T(8,128)S(1)}, f32[8,24576]{1,0:T(8,128)}, u32[]{:S(2)}) %copy-start) | copy-done | bytes 786456
  9.6 0.0 copy-start.2
  9.6 0.9 copy-done.2
  10.4 0.0 copy-start.3
  10.4 0.7 copy-done.3
  11.1 42.9 %inner.1 = (f32[256,256]{1,0:T(8,128)S(1)}, f32[1,24576]{1,0:T(1,128)}) custom-call(s32[8]{0:T(128)S(1)} %copy-done.3, s32[1]{0:T(128)S(6)} %copy.10.refs_1_, bf16[256,24576]{1,0:T(8,128)(2,1)} %refs_2_.3, f32[1,24576]{1,0:T(1,128)S(1)} %bitcast.6, f32[8,24576]{1,0:T(8,128)S(1)} %copy-done), custom_call_target="tpu_custom_call" | custom-call | flops 6274678784 | bytes 12582912 | tf_op jit(solution)/shard_map/inner/pallas_call | solution.py:270
  54.0 0.0 copy-start.1
  54.0 0.0 collective-permute-done.1.refs_6_
  54.1 0.0 collective-permute-done.refs_5_
  54.1 7.0 %edges.1 = (f32[256,256]{1,0:T(8,128)S(1)}, f32[1,24576]{1,0:T(1,128)}) custom-call(s32[8]{0:T(128)S(1)} %copy-done.3, s32[1]{0:T(128)S(6)} %copy.10.refs_1_, bf16[256,24576]{1,0:T(8,128)(2,1)} %refs_2_.3, f32[1,24576]{1,0:T(1,128)S(1)} %bitcast.7, f32[8,24576]{1,0:T(8,128)S(1)} %copy-done, ...), custom_call_target="tpu_custom_call", output_to_operand_aliasing={{1}: (8, {})} | custom-call | flops 570425344 | bytes 3145728 | tf_op jit(solution)/shard_map/edges/pallas_call | solution.py:270
  61.1 17.7 %all_to_all.17 = f32[16,16,256]{2,1,0:T(8,128)S(1)} all-to-all(f32[16,16,256]{2,1,0:T(8,128)S(1)} %bitcast.5), channel_id=1, replica_groups=mesh['grp'=2,'obs'=4,'par'=4] {'obs','par'}, dimensions={0} | all-to-all | bytes 524288 | tf_op jit(solution)/shard_map/all_to_all | solution.py:398
  78.9 12.8 %all_to_all.18 = f32[16,16,256]{2,1,0:T(8,128)S(1)} all-to-all(f32[16,16,256]{2,1,0:T(8,128)S(1)} %broadcast_in_dim.40), channel_id=1, replica_groups=mesh['grp'=2,'obs'=4,'par'=4] {'obs','par'}, dimensions={0} | all-to-all | bytes 524288 | tf_op jit(solution)/shard_map/all_to_all | solution.py:401
  91.7 0.0 copy-done.1
  91.7 12.4 %update.1 = f32[512,256]{1,0:T(8,128)} custom-call(f32[256,256]{1,0:T(8,128)S(1)} %bitcast.4, bf16[512,256]{1,0:T(8,128)(2,1)S(1)} %copy-done.1), custom_call_target="tpu_custom_call" | custom-call | tf_op jit(solution)/shard_map/update/pallas_call | solution.py:374
  (9 shorter events, 0.1 us)
Async XLA Ops:
  3.0 51.0 %collective-permute-start.1 = (bf16[272,1024]{1,0:T(8,128)(2,1)S(1)}, bf16[272,1024]{1,0:T(8,128)(2,1)S(1)}, u32[]{:S(2)}, u32[]{:S(2)}) collective-permute-start(bf16[272,1024]{1,0:T(8,128)(2,1)S(1)} %concatenate.13), channel_id=1, source_target_pairs={{1,0},{2,1},{3,2},{4,3},{5,4},{6,5},{7,6},{8,7},{9,8},{10,9},{11,1... | collective-permute-start | bytes 1671176 | tf_op jit(solution)/shard_map/ppermute | solution.py:412
  4.7 49.4 %collective-permute-start = (bf16[272,1024]{1,0:T(8,128)(2,1)S(1)}, bf16[272,1024]{1,0:T(8,128)(2,1)S(1)}, u32[]{:S(2)}, u32[]{:S(2)}) collective-permute-start(bf16[272,1024]{1,0:T(8,128)(2,1)S(1)} %concatenate.12), channel_id=1, source_target_pairs={{0,1},{1,2},{2,3},{3,4},{4,5},{5,6},{6,7},{7,8},{8,9},{9,10},{10,1... | collective-permute-start | bytes 1671176 | tf_op jit(solution)/shard_map/ppermute | solution.py:411
  8.4 1.1 %copy-start = (f32[8,24576]{1,0:T(8,128)S(1)}, f32[8,24576]{1,0:T(8,128)}, u32[]{:S(2)}) copy-start(f32[8,24576]{1,0:T(8,128)} %refs_4_.3) | copy-start | bytes 2359300
  9.6 0.9 copy-start.2
  10.4 0.7 copy-start.3
  54.0 37.7 %copy-start.1 = (bf16[512,256]{1,0:T(8,128)(2,1)S(1)}, bf16[512,256]{1,0:T(8,128)(2,1)}, u32[]{:S(2)}) copy-start(bf16[512,256]{1,0:T(8,128)(2,1)} %params_ref.1) | copy-start | bytes 786436

commit v2 on v1

--- a/solution.py
+++ b/solution.py
@@ -10,9 +10,11 @@
 
 H = 1024
 LANE = 128
+SUB = 8
 PACK = 16
 BLOCK = 64
 PANEL = 8
+VMEM = 64 * 2**20
 BF = jnp.bfloat16
 F32 = jnp.float32
 
@@ -94,21 +96,23 @@
         wide = jnp.dot(
             centre[...], raw[pl.ds(0, members), pl.ds(pl.multiple_of(place * H, H), H)],
             preferred_element_type=F32)
-        target[pl.ds(0, members), pl.ds(at, H)] = wide[:members].astype(BF)
-        target[pl.ds(members, PACK), pl.ds(at, H)] = (obs_row - wide[members:]).astype(BF)
+        target[pl.ds(0, members), pl.ds(at, H)] = wide[:members]
+        innovation = obs_row - wide[members:members + SUB]
+        target[pl.ds(members, SUB), pl.ds(at, H)] = innovation.astype(BF).astype(F32)
 
     def coefficients(column, at):
         index = column + lax.broadcasted_iota(jnp.int32, (1, H), 1)
         strained = (index < count_ref[0]) | (index >= columns - H)
-        strain = jnp.where(strained, row_factor, 0.0)
+        strain = jnp.where(strained, 1.0, 0.0)
         for slot in range(terms):
             term = slots[slot, 0]
             row = band[pl.ds(term, 1), pl.ds(at, H)]
-            row = row * (row_factor if slot == 0 else strain)
-            coef[pl.ds(slot * 8, 8), :] = jnp.broadcast_to(row, (8, H))
+            if slot > 0:
+                row = row * strain
+            coef[pl.ds(slot * SUB, SUB), :] = jnp.broadcast_to(row, (SUB, H))
 
     def plan(place):
-        lane = lax.broadcasted_iota(jnp.int32, (PACK, LANE), 1)
+        lane = lax.broadcasted_iota(jnp.int32, (SUB, LANE), 1)
         steps = []
         for slot in range(terms):
             if slot < 3:
@@ -120,25 +124,22 @@
                 steps.append((first, lax.rem(LANE - turn, LANE), lane < LANE - turn))
         return steps
 
-    def whiten_rows(steps, starts, low, width):
-        acc = [[None] * width for _ in starts]
+    def whiten_rows(steps, starts):
+        acc = [[None] * tiles for _ in starts]
         for slot, (first, back, keep) in enumerate(steps):
-            weights = []
-            for t in range(width):
-                weight = coef[pl.ds(slot * 8, 8), pl.ds((low + t) * LANE, LANE)]
-                weights.append(jnp.concatenate([weight, weight], 0))
+            weights = [coef[pl.ds(slot * SUB, SUB), pl.ds(t * LANE, LANE)] for t in range(tiles)]
             for r, at_row in enumerate(starts):
                 def load(t):
-                    start = pl.multiple_of((first + low + t) * LANE, LANE)
-                    return joint[pl.ds(at_row, PACK), pl.ds(start, LANE)]
+                    start = pl.multiple_of((first + t) * LANE, LANE)
+                    return joint[pl.ds(at_row, SUB), pl.ds(start, LANE)]
 
                 if back is None:
-                    values = [load(t) for t in range(width)]
+                    values = [load(t) for t in range(tiles)]
                 else:
-                    rolled = [pltpu.roll(load(t), back, 1) for t in range(width + 1)]
-                    values = [jnp.where(keep, rolled[t], rolled[t + 1]) for t in range(width)]
-                for t in range(width):
-                    product = values[t].astype(F32) * weights[t]
+                    rolled = [pltpu.roll(load(t), back, 1) for t in range(tiles + 1)]
+                    values = [jnp.where(keep, rolled[t], rolled[t + 1]) for t in range(tiles)]
+                for t in range(tiles):
+                    product = values[t] * weights[t]
                     acc[r][t] = product if acc[r][t] is None else acc[r][t] + product
         return acc
 
@@ -149,25 +150,22 @@
     def whiten_chunk(place, column, at, aw, out_at):
         coefficients(column, at)
         steps = plan(place)
-        acc = whiten_rows(steps, [members], 0, tiles)[0]
+        acc = whiten_rows(steps, [members])[0]
         row = lax.broadcasted_iota(jnp.int32, (PACK, LANE), 0)
         for t in range(tiles):
-            wide = acc[t]
+            row_out[:, pl.ds(out_at + t * LANE, LANE)] = acc[t][0:1] * (math.sqrt(members - 1) * row_factor)
+            wide = jnp.concatenate([acc[t], acc[t]], 0)
             high = wide.astype(BF).astype(F32)
             rest = wide - high
             middle = rest.astype(BF).astype(F32)
             low = rest - middle
             split = jnp.where(row == 0, high, jnp.where(row == 1, middle, jnp.where(row == 2, low, 0.0)))
             aw[pl.ds(members, PACK), pl.ds(t * LANE, LANE)] = split.astype(BF)
-            row_out[:, pl.ds(out_at + t * LANE, LANE)] = wide[0:1] * math.sqrt(members - 1)
-        width = tiles // 2
-        for group in range(members // (2 * PACK)):
-            starts = [group * 2 * PACK, group * 2 * PACK + PACK]
-            for low in (0, width):
-                acc = whiten_rows(steps, starts, low, width)
-                for r, at_row in enumerate(starts):
-                    for t in range(width):
-                        aw[pl.ds(at_row, PACK), pl.ds((low + t) * LANE, LANE)] = acc[r][t].astype(BF)
+        for group in range(members // PACK):
+            low, high = whiten_rows(steps, [group * PACK, group * PACK + SUB])
+            for t in range(tiles):
+                aw[pl.ds(group * PACK, PACK), pl.ds(t * LANE, LANE)] = jnp.concatenate(
+                    [low[t], high[t]], 0).astype(BF)
 
     if edge:
         for copy in copies:
@@ -231,6 +229,8 @@
     corner = jnp.where(top == 0, total[:, :half], jnp.where(top == 1, total[:, half:], 0.0))
     upper = jnp.concatenate([both[:half, :half], corner], 1)
     lower = both[half:]
+    upper = upper * (1.0 / obs_total)
+    lower = lower * (1.0 / obs_total)
     if edge:
         upper = upper + gram_in[pl.ds(0, half), :]
         lower = lower + gram_in[pl.ds(half, half), :]
@@ -247,17 +247,17 @@
     places = 6 if edge else columns // H
     vmem = pl.BlockSpec(memory_space=pltpu.VMEM)
     smem = pl.BlockSpec(memory_space=pltpu.SMEM)
-    anywhere = pl.BlockSpec(memory_space=pl.ANY)
-    in_specs = [smem, smem, anywhere, anywhere, anywhere]
+    far = pl.BlockSpec(memory_space=pltpu.HBM)
+    in_specs = [smem, smem, far, far, far]
     if edge:
-        in_specs += [anywhere, anywhere, vmem, anywhere]
+        in_specs += [far, far, vmem, far]
     scratch = [
         pltpu.VMEM((rows if edge else members, places * H), BF),
-        pltpu.VMEM((rows, places * H), BF),
+        pltpu.VMEM((members + SUB, places * H), F32),
+        pltpu.VMEM((members + SUB, H), F32),
         pltpu.VMEM((rows, H), BF),
         pltpu.VMEM((rows, H), BF),
-        pltpu.VMEM((rows, H), BF),
-        pltpu.VMEM((8 * terms, H), F32),
+        pltpu.VMEM((SUB * terms, H), F32),
         pltpu.VMEM((rows, members), F32),
         pltpu.VMEM((rows, members), BF),
         pltpu.VMEM((1, 4 * H if edge else columns), F32),
@@ -274,10 +274,10 @@
             jax.ShapeDtypeStruct((1, columns), F32),
         ),
         in_specs=in_specs,
-        out_specs=[vmem, anywhere],
+        out_specs=[vmem, far],
         scratch_shapes=scratch,
         input_output_aliases={8: 1} if edge else {},
-        compiler_params=pltpu.CompilerParams(vmem_limit_bytes=50 * 2**20),
+        compiler_params=pltpu.CompilerParams(vmem_limit_bytes=VMEM),
         cost_estimate=pl.CostEstimate(
             flops=2 * rows * members * H * work * 2, bytes_accessed=members * H * places * 2, transcendentals=0),
         name="edges" if edge else "inner",
@@ -377,19 +377,56 @@
         in_specs=[vmem, vmem],
         out_specs=vmem,
         scratch_shapes=[pltpu.VMEM((members, 2 * members), F32)],
-        compiler_params=pltpu.CompilerParams(vmem_limit_bytes=32 * 2**20),
+        compiler_params=pltpu.CompilerParams(vmem_limit_bytes=VMEM),
         name="update",
     )(total, params)
 
 
-def halo_block(predicted, observed):
-    high = lax.reduce_precision(observed, 8, 7)
-    rest = observed - high
-    middle = lax.reduce_precision(rest, 8, 7)
+def halo_kernel(columns, pred_ref, obs_ref, first_ref, last_ref, obs, pieces, sems):
+    members = pred_ref.shape[0]
+    copies = []
+    for side, (out, at) in enumerate(((first_ref, 0), (last_ref, columns - H))):
+        copies.append(pltpu.make_async_copy(
+            pred_ref.at[:, pl.ds(at, H)], out.at[pl.ds(0, members), :], sems.at[side]))
+        copies.append(pltpu.make_async_copy(
+            obs_ref.at[:, pl.ds(at, H)], obs.at[:, pl.ds(side * H, H)], sems.at[2 + side]))
+    for copy in copies:
+        copy.start()
+    for copy in copies[1::2]:
+        copy.wait()
+    wide = jnp.broadcast_to(obs[...], (PACK, 2 * H))
+    high = wide.astype(BF).astype(F32)
+    rest = wide - high
+    middle = rest.astype(BF).astype(F32)
     low = rest - middle
-    pieces = jnp.concatenate(
-        [high[None], middle[None], low[None], jnp.zeros((PACK - 3, observed.shape[0]), F32)], 0)
-    return jnp.concatenate([predicted, pieces.astype(BF)], 0)
+    row = lax.broadcasted_iota(jnp.int32, (PACK, 2 * H), 0)
+    split = jnp.where(row == 0, high, jnp.where(row == 1, middle, jnp.where(row == 2, low, 0.0)))
+    pieces[...] = split.astype(BF)
+    ends = [
+        pltpu.make_async_copy(
+            pieces.at[:, pl.ds(side * H, H)], out.at[pl.ds(members, PACK), :], sems.at[4 + side])
+        for side, out in enumerate((first_ref, last_ref))
+    ]
+    for copy in ends:
+        copy.start()
+    for copy in copies[0::2] + ends:
+        copy.wait()
+
+
+def halo_blocks(predicted, observed):
+    members, columns = predicted.shape
+    far = pl.BlockSpec(memory_space=pltpu.HBM)
+    block = jax.ShapeDtypeStruct((members + PACK, H), BF)
+    return pl.pallas_call(
+        functools.partial(halo_kernel, columns),
+        out_shape=(block, block),
+        in_specs=[far, far],
+        out_specs=[far, far],
+        scratch_shapes=[
+            pltpu.VMEM((1, 2 * H), F32), pltpu.VMEM((PACK, 2 * H), BF), pltpu.SemaphoreType.DMA((6,))],
+        compiler_params=pltpu.CompilerParams(vmem_limit_bytes=VMEM),
+        name="halos",
+    )(predicted, observed)
 
 
 def sum_over(values, axes):
@@ -408,9 +445,10 @@
     obs_total = columns * shards
     up = [(i, i + 1) for i in range(shards - 1)]
     down = [(j, i) for i, j in up]
-    left = lax.ppermute(halo_block(predicted[:, columns - H:], observed[columns - H:]), axes, up)
-    right = lax.ppermute(halo_block(predicted[:, :H], observed[:H]), axes, down)
     obs_row = observed[None, :]
+    first, last = halo_blocks(predicted, obs_row)
+    left = lax.ppermute(last, axes, up)
+    right = lax.ppermute(first, axes, down)
     gram, misfit = local_call(False, obs_total, offsets, rows_count, predicted, obs_row, band)
     gram, misfit = local_call(
         True, obs_total, offsets, rows_count, predicted, obs_row, band, left, right, gram, misfit)

time: 105 us -> 145 us (1.38)
  Pallas kernels: 62.4 us -> 107 us
  local copies, waits for them, and re-layouts: 4.68 us -> 0.02 us
    pallas_call x0 -> x1, Pallas kernels: none -> 32.9 us  [halo_blocks(): pl.pallas_call(functools.partial(halo_kernel, columns), out_shape=(block,...]
    pallas_call x2, Pallas kernels: 50 us -> 60.9 us  [local_call(): pl.pallas_call(functools.partial(local_kernel, edge, columns, obs_total),...]
    unnamed x8 -> x0, local copies, waits for them, and re-layouts: 2.68 us -> none
  transfers between devices with their start and end apart: 2 -> 2, of which waited for: 0 -> 0; matrix products, arithmetic and copies ran while one was open for 0% -> 0% of each run, Pallas kernels for 41% -> 36%
where the time goes in v2:
time: 145 us
  Pallas kernels  107 us (74%)
  blocking collectives  31.9 us (22%)
  starting transfers between devices  4.45 us (3%)
    pallas_call x2, Pallas kernels, local_call(): pl.pallas_call(functools.partial(local_kernel, edge, columns, obs_total),...  60.9 us
    pallas_call x1, Pallas kernels, halo_blocks(): pl.pallas_call(functools.partial(halo_kernel, columns), out_shape=(block,...  32.9 us
    all_to_all x1, blocking collectives, sum_over(): parts = lax.all_to_all(values, axes, 0, 0, tiled=True)  18.5 us
    pallas_call x1, Pallas kernels, update(): pl.pallas_call(update_kernel, out_shape=jax.ShapeDtypeStruct(params.shape...  13.5 us
    all_to_all x1, blocking collectives, sum_over(): return lax.all_to_all(copies, axes, 0, 0, tiled=True)  13.3 us
    ppermute x1, starting transfers between devices, body(): left = lax.ppermute(last, axes, up)  3.17 us
  transfers between devices with their start and end apart: 2, of which 0 were waited for; matrix products, arithmetic and copies ran while one was open for 0% of the time, Pallas kernels for 36%

profile of v2, /device:TPU:0, one launch (start us, length us, event | category | flops | bytes accessed | tf_op | source)
XLA Modules:
  0.0 145.0 jit_solution(13553977457916656682)
XLA Ops:
  0.6 32.9 %halos.1 = (bf16[272,1024]{1,0:T(8,128)(2,1)}, bf16[272,1024]{1,0:T(8,128)(2,1)}) custom-call(bf16[256,24576]{1,0:T(8,128)(2,1)} %refs_2_.3, f32[1,24576]{1,0:T(1,128)} %bitcast.5), custom_call_target="tpu_custom_call" | custom-call | tf_op jit(solution)/shard_map/halos/pallas_call | solution.py:420
  33.6 3.2 %collective-permute-start = (bf16[272,1024]{1,0:T(8,128)(2,1)}, bf16[272,1024]{1,0:T(8,128)(2,1)}, u32[]{:S(2)}, u32[]{:S(2)}) collective-permute-start(bf16[272,1024]{1,0:T(8,128)(2,1)} %get-tuple-element.8), channel_id=1, source_target_pairs={{0,1},{1,2},{2,3},{3,4},{4,5},{5,6},{6,7},{7,8},{8,9},{9,10},{10,1... | collective-permute-start | bytes 1671176 | tf_op jit(solution)/shard_map/ppermute | solution.py:450
  36.7 1.3 collective-permute-start.1
  38.7 51.9 %inner.1 = (f32[256,256]{1,0:T(8,128)}, f32[1,24576]{1,0:T(1,128)}) custom-call(s32[8]{0:T(128)} %refs_0_.3, s32[1]{0:T(128)S(6)} %copy.10.refs_1_, bf16[256,24576]{1,0:T(8,128)(2,1)} %refs_2_.3, f32[1,24576]{1,0:T(1,128)} %bitcast.6, f32[8,24576]{1,0:T(8,128)} %refs_4_.3), custom_call_target="tpu_custom_call" | custom-call | flops 6274678784 | bytes 12582912 | tf_op jit(solution)/shard_map/inner/pallas_call | solution.py:270
  90.6 0.0 collective-permute-done.refs_5_
  90.6 0.0 collective-permute-done.1.refs_6_
  90.6 9.0 %edges.1 = (f32[256,256]{1,0:T(8,128)}, f32[1,24576]{1,0:T(1,128)}) custom-call(s32[8]{0:T(128)} %refs_0_.3, s32[1]{0:T(128)S(6)} %copy.10.refs_1_, bf16[256,24576]{1,0:T(8,128)(2,1)} %refs_2_.3, f32[1,24576]{1,0:T(1,128)} %bitcast.7, f32[8,24576]{1,0:T(8,128)} %refs_4_.3, ...), custom_call_target="tpu_custom_call", output_to_operand_aliasing={{1}: (8, {})} | custom-call | flops 570425344 | bytes 3145728 | tf_op jit(solution)/shard_map/edges/pallas_call | solution.py:270
  99.6 18.5 %all_to_all.17 = f32[16,16,256]{2,1,0:T(8,128)S(1)} all-to-all(f32[16,16,256]{2,1,0:T(8,128)} %bitcast.8), channel_id=1, replica_groups=mesh['grp'=2,'obs'=4,'par'=4] {'obs','par'}, dimensions={0} | all-to-all | bytes 524288 | tf_op jit(solution)/shard_map/all_to_all | solution.py:435
  118.2 13.3 %all_to_all.18 = f32[16,16,256]{2,1,0:T(8,128)} all-to-all(f32[16,16,256]{2,1,0:T(8,128)S(1)} %broadcast_in_dim.10), channel_id=1, replica_groups=mesh['grp'=2,'obs'=4,'par'=4] {'obs','par'}, dimensions={0} | all-to-all | bytes 524288 | tf_op jit(solution)/shard_map/all_to_all | solution.py:438
  131.5 13.5 %update.1 = f32[512,256]{1,0:T(8,128)} custom-call(f32[256,256]{1,0:T(8,128)} %bitcast.4, bf16[512,256]{1,0:T(8,128)(2,1)} %params_ref.1), custom_call_target="tpu_custom_call" | custom-call | tf_op jit(solution)/shard_map/update/pallas_call | solution.py:374
  (2 shorter events, 0.0 us)
Async XLA Ops:
  33.6 57.0 %collective-permute-start = (bf16[272,1024]{1,0:T(8,128)(2,1)}, bf16[272,1024]{1,0:T(8,128)(2,1)}, u32[]{:S(2)}, u32[]{:S(2)}) collective-permute-start(bf16[272,1024]{1,0:T(8,128)(2,1)} %get-tuple-element.8), channel_id=1, source_target_pairs={{0,1},{1,2},{2,3},{3,4},{4,5},{5,6},{6,7},{7,8},{8,9},{9,10},{10,1... | collective-permute-start | bytes 1671176 | tf_op jit(solution)/shard_map/ppermute | solution.py:450
  36.7 53.9 %collective-permute-start.1 = (bf16[272,1024]{1,0:T(8,128)(2,1)}, bf16[272,1024]{1,0:T(8,128)(2,1)}, u32[]{:S(2)}, u32[]{:S(2)}) collective-permute-start(bf16[272,1024]{1,0:T(8,128)(2,1)} %get-tuple-element.9), channel_id=1, source_target_pairs={{1,0},{2,1},{3,2},{4,3},{5,4},{6,5},{7,6},{8,7},{9,8},{10,9},{11,1... | collective-permute-start | bytes 1671176 | tf_op jit(solution)/shard_map/ppermute | solution.py:451

commit v3 on v2

--- a/solution.py
+++ b/solution.py
@@ -12,6 +12,7 @@
 LANE = 128
 SUB = 8
 PACK = 16
+GROUP = 64
 BLOCK = 64
 PANEL = 8
 VMEM = 64 * 2**20
@@ -22,11 +23,11 @@
 def local_kernel(edge, columns, obs_total, *refs):
     if edge:
         (off_ref, count_ref, pred_ref, obs_ref, band_ref, left_ref, right_ref, gram_in, misfit_in,
-         gram_out, misfit_out, raw, joint, fresh, aw_a, aw_b, coef, gram, centre, obs, band, row_out, slots,
+         gram_out, misfit_out, raw, joint, aw, coef, gram, centre, obs, band, row_out, slots,
          sems) = refs
     else:
         (off_ref, count_ref, pred_ref, obs_ref, band_ref,
-         gram_out, misfit_out, raw, joint, fresh, aw_a, aw_b, coef, gram, centre, obs, band, row_out, slots,
+         gram_out, misfit_out, raw, joint, aw, coef, gram, centre, obs, band, row_out, slots,
          sems) = refs
     members = pred_ref.shape[0]
     terms = band_ref.shape[0]
@@ -47,7 +48,7 @@
         for which in range(2):
             there = which * (columns - 2 * H)
             copies.append(pltpu.make_async_copy(
-                obs_ref.at[:, pl.ds(there, 2 * H)], obs.at[:, pl.ds(which * 2 * H, 2 * H)], sems.at[6 + which]))
+                obs_ref.at[:, pl.ds(there, 2 * H)], obs.at[:, pl.ds((1 + which * 2) * H, 2 * H)], sems.at[6 + which]))
             there = which * (columns - H)
             copies.append(pltpu.make_async_copy(
                 band_ref.at[:, pl.ds(there, H)], band.at[:, pl.ds(which * H, H)], sems.at[8 + which]))
@@ -89,16 +90,14 @@
         row_index >= members, mean_part, jnp.where(row_index == col_index, 1.0 - mean_part, -mean_part)
     ).astype(BF)
     gram[...] = jnp.zeros_like(gram)
-    if not edge:
-        aw_b[...] = jnp.zeros_like(aw_b)
-
-    def anomalies(place, obs_row, target, at):
-        wide = jnp.dot(
-            centre[...], raw[pl.ds(0, members), pl.ds(pl.multiple_of(place * H, H), H)],
-            preferred_element_type=F32)
-        target[pl.ds(0, members), pl.ds(at, H)] = wide[:members]
-        innovation = obs_row - wide[members:members + SUB]
-        target[pl.ds(members, SUB), pl.ds(at, H)] = innovation.astype(BF).astype(F32)
+    aw[...] = jnp.zeros_like(aw)
+
+    def anomalies(place):
+        at = pl.ds(pl.multiple_of(place * H, H), H)
+        wide = jnp.dot(centre[...], raw[pl.ds(0, members), at], preferred_element_type=F32)
+        joint[pl.ds(0, members), at] = wide[:members]
+        innovation = obs[:, at] - wide[members:members + SUB]
+        joint[pl.ds(members, SUB), at] = innovation.astype(BF).astype(F32)
 
     def coefficients(column, at):
         index = column + lax.broadcasted_iota(jnp.int32, (1, H), 1)
@@ -143,17 +142,17 @@
                     acc[r][t] = product if acc[r][t] is None else acc[r][t] + product
         return acc
 
-    def products(aw):
+    def products():
         gram[...] += lax.dot_general(
             aw[...], aw[pl.ds(0, members), :], (((1,), (1,)), ((), ())), preferred_element_type=F32)
 
-    def whiten_chunk(place, column, at, aw, out_at):
+    def whiten_chunk(place, column, at):
         coefficients(column, at)
         steps = plan(place)
         acc = whiten_rows(steps, [members])[0]
         row = lax.broadcasted_iota(jnp.int32, (PACK, LANE), 0)
         for t in range(tiles):
-            row_out[:, pl.ds(out_at + t * LANE, LANE)] = acc[t][0:1] * (math.sqrt(members - 1) * row_factor)
+            row_out[:, pl.ds(at + t * LANE, LANE)] = acc[t][0:1] * (math.sqrt(members - 1) * row_factor)
             wide = jnp.concatenate([acc[t], acc[t]], 0)
             high = wide.astype(BF).astype(F32)
             rest = wide - high
@@ -161,66 +160,66 @@
             low = rest - middle
             split = jnp.where(row == 0, high, jnp.where(row == 1, middle, jnp.where(row == 2, low, 0.0)))
             aw[pl.ds(members, PACK), pl.ds(t * LANE, LANE)] = split.astype(BF)
-        for group in range(members // PACK):
-            low, high = whiten_rows(steps, [group * PACK, group * PACK + SUB])
-            for t in range(tiles):
-                aw[pl.ds(group * PACK, PACK), pl.ds(t * LANE, LANE)] = jnp.concatenate(
-                    [low[t], high[t]], 0).astype(BF)
+
+        def group(index, carry):
+            for pair in range(GROUP // PACK):
+                at_row = pl.multiple_of(index * GROUP + pair * PACK, PACK)
+                low, high = whiten_rows(steps, [at_row, pl.multiple_of(at_row + SUB, SUB)])
+                for t in range(tiles):
+                    aw[pl.ds(at_row, PACK), pl.ds(t * LANE, LANE)] = jnp.concatenate(
+                        [low[t], high[t]], 0).astype(BF)
+            return carry
+
+        lax.fori_loop(0, members // GROUP, group, 0)
 
     if edge:
         for copy in copies:
             copy.wait()
-        for place in range(6):
-            if place in (0, 5):
-                pieces = raw[pl.ds(members, PACK), pl.ds(place * H, H)].astype(F32)
-                obs_row = pieces[0:1] + pieces[1:2] + pieces[2:3]
-            else:
-                obs_row = obs[:, pl.ds((place - 1) * H, H)]
-            anomalies(place, obs_row, joint, place * H)
-        whiten_chunk(1, 0, 0, aw_a, 0)
-        products(aw_a)
-        whiten_chunk(4, columns - H, H, aw_b, H)
+        for place in (0, 5):
+            pieces = raw[pl.ds(members, PACK), pl.ds(place * H, H)].astype(F32)
+            obs[:, pl.ds(place * H, H)] = pieces[0:1] + pieces[1:2] + pieces[2:3]
+
+        def centre_step(place, carry):
+            anomalies(place)
+            return carry
+
+        lax.fori_loop(0, 6, centre_step, 0)
+
+        def chunk_step(which, carry):
+            products()
+            whiten_chunk(1 + 3 * which, which * (columns - H), pl.multiple_of(which * H, H))
+            return carry
+
+        lax.fori_loop(0, 2, chunk_step, 0)
         out_copies = [
             pltpu.make_async_copy(row_out.at[:, pl.ds(0, H)], misfit_out.at[:, pl.ds(0, H)], sems.at[0]),
             pltpu.make_async_copy(row_out.at[:, pl.ds(H, H)], misfit_out.at[:, pl.ds(columns - H, H)], sems.at[1]),
         ]
-        for copy in out_copies:
-            copy.start()
-        products(aw_b)
     else:
-        def ready(place, target, at):
-            anomalies(place, obs[:, pl.ds(pl.multiple_of(place * H, H), H)], target, at)
-
         for copy in copies:
             copy.wait()
-        for place in range(3):
+
+        def centre_step(place, carry):
             chunk_copy(place).wait()
-            ready(place, *((joint, place * H) if place < 2 else (fresh, 0)))
-
-        def chunk_step(place, aw, before):
-            ahead = jnp.minimum(place + 2, chunks - 1)
-
-            @pl.when(place + 2 < chunks)
-            def _():
-                chunk_copy(ahead).wait()
-
+            anomalies(place)
+            return carry
+
+        lax.fori_loop(0, 2, centre_step, 0)
+
+        def chunk_step(place, carry):
+            chunk_copy(place + 1).wait()
+            products()
+            anomalies(place + 1)
             column = pl.multiple_of(place * H, H)
-            joint[:, pl.ds(pl.multiple_of(column + H, H), H)] = fresh[...]
-            products(before)
-            whiten_chunk(place, column, column, aw, column)
-            ready(ahead, fresh, 0)
-
-        def pair(index, carry):
-            chunk_step(1 + 2 * index, aw_a, aw_b)
-            chunk_step(2 + 2 * index, aw_b, aw_a)
+            whiten_chunk(place, column, column)
             return carry
 
-        lax.fori_loop(0, (chunks - 2) // 2, pair, 0)
+        lax.fori_loop(1, chunks - 1, chunk_step, 0)
         inside = pl.ds(H, columns - 2 * H)
         out_copies = [pltpu.make_async_copy(row_out.at[:, inside], misfit_out.at[:, inside], sems.at[0])]
-        for copy in out_copies:
-            copy.start()
-        products(aw_b)
+    for copy in out_copies:
+        copy.start()
+    products()
 
     tail = gram[pl.ds(members, 8), :]
     total = tail[0:1] + tail[1:2] + tail[2:3]
@@ -254,13 +253,11 @@
     scratch = [
         pltpu.VMEM((rows if edge else members, places * H), BF),
         pltpu.VMEM((members + SUB, places * H), F32),
-        pltpu.VMEM((members + SUB, H), F32),
-        pltpu.VMEM((rows, H), BF),
         pltpu.VMEM((rows, H), BF),
         pltpu.VMEM((SUB * terms, H), F32),
         pltpu.VMEM((rows, members), F32),
         pltpu.VMEM((rows, members), BF),
-        pltpu.VMEM((1, 4 * H if edge else columns), F32),
+        pltpu.VMEM((1, places * H), F32),
         pltpu.VMEM((terms, 2 * H if edge else columns), F32),
         pltpu.VMEM((1, 2 * H if edge else columns), F32),
         pltpu.SMEM((8, 2), jnp.int32),
@@ -382,7 +379,7 @@
     )(total, params)
 
 
-def halo_kernel(columns, pred_ref, obs_ref, first_ref, last_ref, obs, pieces, sems):
+def halo_kernel(columns, pred_ref, obs_ref, first_ref, last_ref, obs, sems):
     members = pred_ref.shape[0]
     copies = []
     for side, (out, at) in enumerate(((first_ref, 0), (last_ref, columns - H))):
@@ -394,36 +391,30 @@
         copy.start()
     for copy in copies[1::2]:
         copy.wait()
-    wide = jnp.broadcast_to(obs[...], (PACK, 2 * H))
-    high = wide.astype(BF).astype(F32)
-    rest = wide - high
-    middle = rest.astype(BF).astype(F32)
-    low = rest - middle
-    row = lax.broadcasted_iota(jnp.int32, (PACK, 2 * H), 0)
-    split = jnp.where(row == 0, high, jnp.where(row == 1, middle, jnp.where(row == 2, low, 0.0)))
-    pieces[...] = split.astype(BF)
-    ends = [
-        pltpu.make_async_copy(
-            pieces.at[:, pl.ds(side * H, H)], out.at[pl.ds(members, PACK), :], sems.at[4 + side])
-        for side, out in enumerate((first_ref, last_ref))
-    ]
-    for copy in ends:
-        copy.start()
-    for copy in copies[0::2] + ends:
+    row = lax.broadcasted_iota(jnp.int32, (PACK, H), 0)
+    for side, out in enumerate((first_ref, last_ref)):
+        wide = jnp.broadcast_to(obs[:, pl.ds(side * H, H)], (PACK, H))
+        high = wide.astype(BF).astype(F32)
+        rest = wide - high
+        middle = rest.astype(BF).astype(F32)
+        low = rest - middle
+        split = jnp.where(row == 0, high, jnp.where(row == 1, middle, jnp.where(row == 2, low, 0.0)))
+        out[pl.ds(members, PACK), :] = split.astype(BF)
+    for copy in copies[0::2]:
         copy.wait()
 
 
 def halo_blocks(predicted, observed):
     members, columns = predicted.shape
     far = pl.BlockSpec(memory_space=pltpu.HBM)
+    near = pl.BlockSpec(memory_space=pltpu.VMEM)
     block = jax.ShapeDtypeStruct((members + PACK, H), BF)
     return pl.pallas_call(
         functools.partial(halo_kernel, columns),
         out_shape=(block, block),
         in_specs=[far, far],
-        out_specs=[far, far],
-        scratch_shapes=[
-            pltpu.VMEM((1, 2 * H), F32), pltpu.VMEM((PACK, 2 * H), BF), pltpu.SemaphoreType.DMA((6,))],
+        out_specs=[near, near],
+        scratch_shapes=[pltpu.VMEM((1, 2 * H), F32), pltpu.SemaphoreType.DMA((4,))],
         compiler_params=pltpu.CompilerParams(vmem_limit_bytes=VMEM),
         name="halos",
     )(predicted, observed)

time: 145 us -> 148 us (1.021)
  Pallas kernels: 107 us -> 110 us
    pallas_call x2, Pallas kernels: 60.9 us -> 94.6 us  [local_call(): pl.pallas_call(functools.partial(local_kernel, edge, columns, obs_total),...]
    pallas_call x1, Pallas kernels: 32.9 us -> 2.29 us  [halo_blocks(): pl.pallas_call(functools.partial(halo_kernel, columns), out_shape=(block,...]
  transfers between devices with their start and end apart: 2 -> 2, of which waited for: 0 -> 0; matrix products, arithmetic and copies ran while one was open for 0% -> 0% of each run, Pallas kernels for 36% -> 55%
where the time goes in v3:
time: 148 us
  Pallas kernels  110 us (74%)
  blocking collectives  31.9 us (22%)
  starting transfers between devices  4.45 us (3%)
    pallas_call x2, Pallas kernels, local_call(): pl.pallas_call(functools.partial(local_kernel, edge, columns, obs_total),...  94.6 us
    all_to_all x1, blocking collectives, sum_over(): parts = lax.all_to_all(values, axes, 0, 0, tiled=True)  18.5 us
    pallas_call x1, Pallas kernels, update(): pl.pallas_call(update_kernel, out_shape=jax.ShapeDtypeStruct(params.shape...  13.5 us
    all_to_all x1, blocking collectives, sum_over(): return lax.all_to_all(copies, axes, 0, 0, tiled=True)  13.3 us
    ppermute x1, starting transfers between devices, body(): left = lax.ppermute(last, axes, up)  3.17 us
  transfers between devices with their start and end apart: 2, of which 0 were waited for; matrix products, arithmetic and copies ran while one was open for 0% of the time, Pallas kernels for 55%

profile of v3, /device:TPU:0, one launch (start us, length us, event | category | flops | bytes accessed | tf_op | source)
XLA Modules:
  0.0 148.1 jit_solution(3678996331375839573)
XLA Ops:
  0.6 2.3 %halos.1 = (bf16[272,1024]{1,0:T(8,128)(2,1)}, bf16[272,1024]{1,0:T(8,128)(2,1)}) custom-call(bf16[256,24576]{1,0:T(8,128)(2,1)} %refs_2_.3, f32[1,24576]{1,0:T(1,128)} %bitcast.5), custom_call_target="tpu_custom_call" | custom-call | tf_op jit(solution)/shard_map/halos/pallas_call | solution.py:412
  2.9 3.2 %collective-permute-start = (bf16[272,1024]{1,0:T(8,128)(2,1)}, bf16[272,1024]{1,0:T(8,128)(2,1)}, u32[]{:S(2)}, u32[]{:S(2)}) collective-permute-start(bf16[272,1024]{1,0:T(8,128)(2,1)} %get-tuple-element.8), channel_id=1, source_target_pairs={{0,1},{1,2},{2,3},{3,4},{4,5},{5,6},{6,7},{7,8},{8,9},{9,10},{10,1... | collective-permute-start | bytes 1671176 | tf_op jit(solution)/shard_map/ppermute | solution.py:441
  6.1 1.3 collective-permute-start.1
  8.0 82.0 %inner.1 = (f32[256,256]{1,0:T(8,128)}, f32[1,24576]{1,0:T(1,128)}) custom-call(s32[8]{0:T(128)} %refs_0_.3, s32[1]{0:T(128)S(6)} %copy.10.refs_1_, bf16[256,24576]{1,0:T(8,128)(2,1)} %refs_2_.3, f32[1,24576]{1,0:T(1,128)} %bitcast.6, f32[8,24576]{1,0:T(8,128)} %refs_4_.3), custom_call_target="tpu_custom_call" | custom-call | flops 6274678784 | bytes 12582912 | tf_op jit(solution)/shard_map/inner/pallas_call | solution.py:267
  90.0 0.0 collective-permute-done.refs_5_
  90.0 0.0 collective-permute-done.1.refs_6_
  90.0 12.6 %edges.1 = (f32[256,256]{1,0:T(8,128)}, f32[1,24576]{1,0:T(1,128)}) custom-call(s32[8]{0:T(128)} %refs_0_.3, s32[1]{0:T(128)S(6)} %copy.10.refs_1_, bf16[256,24576]{1,0:T(8,128)(2,1)} %refs_2_.3, f32[1,24576]{1,0:T(1,128)} %bitcast.7, f32[8,24576]{1,0:T(8,128)} %refs_4_.3, ...), custom_call_target="tpu_custom_call", output_to_operand_aliasing={{1}: (8, {})} | custom-call | flops 570425344 | bytes 3145728 | tf_op jit(solution)/shard_map/edges/pallas_call | solution.py:267
  102.7 18.5 %all_to_all.17 = f32[16,16,256]{2,1,0:T(8,128)S(1)} all-to-all(f32[16,16,256]{2,1,0:T(8,128)} %bitcast.8), channel_id=1, replica_groups=mesh['grp'=2,'obs'=4,'par'=4] {'obs','par'}, dimensions={0} | all-to-all | bytes 524288 | tf_op jit(solution)/shard_map/all_to_all | solution.py:426
  121.3 13.3 %all_to_all.18 = f32[16,16,256]{2,1,0:T(8,128)} all-to-all(f32[16,16,256]{2,1,0:T(8,128)S(1)} %broadcast_in_dim.10), channel_id=1, replica_groups=mesh['grp'=2,'obs'=4,'par'=4] {'obs','par'}, dimensions={0} | all-to-all | bytes 524288 | tf_op jit(solution)/shard_map/all_to_all | solution.py:429
  134.6 13.5 %update.1 = f32[512,256]{1,0:T(8,128)} custom-call(f32[256,256]{1,0:T(8,128)} %bitcast.4, bf16[512,256]{1,0:T(8,128)(2,1)} %params_ref.1), custom_call_target="tpu_custom_call" | custom-call | tf_op jit(solution)/shard_map/update/pallas_call | solution.py:371
  (2 shorter events, 0.0 us)
Async XLA Ops:
  2.9 87.1 %collective-permute-start = (bf16[272,1024]{1,0:T(8,128)(2,1)}, bf16[272,1024]{1,0:T(8,128)(2,1)}, u32[]{:S(2)}, u32[]{:S(2)}) collective-permute-start(bf16[272,1024]{1,0:T(8,128)(2,1)} %get-tuple-element.8), channel_id=1, source_target_pairs={{0,1},{1,2},{2,3},{3,4},{4,5},{5,6},{6,7},{7,8},{8,9},{9,10},{10,1... | collective-permute-start | bytes 1671176 | tf_op jit(solution)/shard_map/ppermute | solution.py:441
  6.1 83.9 %collective-permute-start.1 = (bf16[272,1024]{1,0:T(8,128)(2,1)}, bf16[272,1024]{1,0:T(8,128)(2,1)}, u32[]{:S(2)}, u32[]{:S(2)}) collective-permute-start(bf16[272,1024]{1,0:T(8,128)(2,1)} %get-tuple-element.9), channel_id=1, source_target_pairs={{1,0},{2,1},{3,2},{4,3},{5,4},{6,5},{7,6},{8,7},{9,8},{10,9},{11,1... | collective-permute-start | bytes 1671176 | tf_op jit(solution)/shard_map/ppermute | solution.py:442

commit v4 on v3

--- a/solution.py
+++ b/solution.py
@@ -12,7 +12,7 @@
 LANE = 128
 SUB = 8
 PACK = 16
-GROUP = 64
+LATE = 2
 BLOCK = 64
 PANEL = 8
 VMEM = 64 * 2**20
@@ -149,28 +149,36 @@
     def whiten_chunk(place, column, at):
         coefficients(column, at)
         steps = plan(place)
+        pending = []
+
+        def store_oldest():
+            at_row, values = pending.pop(0)
+            for t in range(tiles):
+                aw[pl.ds(at_row, PACK), pl.ds(t * LANE, LANE)] = values[t]
+
         acc = whiten_rows(steps, [members])[0]
         row = lax.broadcasted_iota(jnp.int32, (PACK, LANE), 0)
+        parts = []
         for t in range(tiles):
-            row_out[:, pl.ds(at + t * LANE, LANE)] = acc[t][0:1] * (math.sqrt(members - 1) * row_factor)
             wide = jnp.concatenate([acc[t], acc[t]], 0)
             high = wide.astype(BF).astype(F32)
             rest = wide - high
             middle = rest.astype(BF).astype(F32)
             low = rest - middle
             split = jnp.where(row == 0, high, jnp.where(row == 1, middle, jnp.where(row == 2, low, 0.0)))
-            aw[pl.ds(members, PACK), pl.ds(t * LANE, LANE)] = split.astype(BF)
-
-        def group(index, carry):
-            for pair in range(GROUP // PACK):
-                at_row = pl.multiple_of(index * GROUP + pair * PACK, PACK)
-                low, high = whiten_rows(steps, [at_row, pl.multiple_of(at_row + SUB, SUB)])
-                for t in range(tiles):
-                    aw[pl.ds(at_row, PACK), pl.ds(t * LANE, LANE)] = jnp.concatenate(
-                        [low[t], high[t]], 0).astype(BF)
-            return carry
-
-        lax.fori_loop(0, members // GROUP, group, 0)
+            parts.append(split.astype(BF))
+        pending.append((members, parts))
+        scale = math.sqrt(members - 1) * row_factor
+        misfit = [acc[t][0:1] * scale for t in range(tiles)]
+        for group in range(members // PACK):
+            low, high = whiten_rows(steps, [group * PACK, group * PACK + SUB])
+            pending.append((group * PACK, [jnp.concatenate([low[t], high[t]], 0).astype(BF) for t in range(tiles)]))
+            if len(pending) > LATE:
+                store_oldest()
+        while pending:
+            store_oldest()
+        for t in range(tiles):
+            row_out[:, pl.ds(at + t * LANE, LANE)] = misfit[t]
 
     if edge:
         for copy in copies:

time: 148 us -> 125 us (0.84)
  Pallas kernels: 110 us -> 86.6 us
    pallas_call x2, Pallas kernels: 94.6 us -> 70.8 us  [local_call(): pl.pallas_call(functools.partial(local_kernel, edge, columns, obs_total),...]
  transfers between devices with their start and end apart: 2 -> 2, of which waited for: 0 -> 0; matrix products, arithmetic and copies ran while one was open for 0% -> 0% of each run, Pallas kernels for 55% -> 49%
where the time goes in v4:
time: 125 us; the launch traced here: 124 us
  Pallas kernels  86.6 us (69%)
  blocking collectives  31.9 us (26%)
  starting transfers between devices  4.45 us (4%)
  between operations  1.34 us (1%)
    pallas_call x2, Pallas kernels, local_call(): pl.pallas_call(functools.partial(local_kernel, edge, columns, obs_total),...  70.8 us
    all_to_all x1, blocking collectives, sum_over(): parts = lax.all_to_all(values, axes, 0, 0, tiled=True)  18.5 us
    pallas_call x1, Pallas kernels, update(): pl.pallas_call(update_kernel, out_shape=jax.ShapeDtypeStruct(params.shape...  13.5 us
    all_to_all x1, blocking collectives, sum_over(): return lax.all_to_all(copies, axes, 0, 0, tiled=True)  13.3 us
    ppermute x1, starting transfers between devices, body(): left = lax.ppermute(last, axes, up)  3.17 us
  transfers between devices with their start and end apart: 2, of which 0 were waited for; matrix products, arithmetic and copies ran while one was open for 0% of the time, Pallas kernels for 49%

profile of v4, /device:TPU:0, one launch (start us, length us, event | category | flops | bytes accessed | tf_op | source)
XLA Modules:
  0.0 124.3 jit_solution(8254761881457274555)
XLA Ops:
  0.6 2.3 %halos.1 = (bf16[272,1024]{1,0:T(8,128)(2,1)}, bf16[272,1024]{1,0:T(8,128)(2,1)}) custom-call(bf16[256,24576]{1,0:T(8,128)(2,1)} %refs_2_.3, f32[1,24576]{1,0:T(1,128)} %bitcast.5), custom_call_target="tpu_custom_call" | custom-call | tf_op jit(solution)/shard_map/halos/pallas_call | solution.py:420
  2.9 3.2 %collective-permute-start = (bf16[272,1024]{1,0:T(8,128)(2,1)}, bf16[272,1024]{1,0:T(8,128)(2,1)}, u32[]{:S(2)}, u32[]{:S(2)}) collective-permute-start(bf16[272,1024]{1,0:T(8,128)(2,1)} %get-tuple-element.8), channel_id=1, source_target_pairs={{0,1},{1,2},{2,3},{3,4},{4,5},{5,6},{6,7},{7,8},{8,9},{9,10},{10,1... | collective-permute-start | bytes 1671176 | tf_op jit(solution)/shard_map/ppermute | solution.py:449
  6.1 1.3 %collective-permute-start.1 = (bf16[272,1024]{1,0:T(8,128)(2,1)}, bf16[272,1024]{1,0:T(8,128)(2,1)}, u32[]{:S(2)}, u32[]{:S(2)}) collective-permute-start(bf16[272,1024]{1,0:T(8,128)(2,1)} %get-tuple-element.9), channel_id=1, source_target_pairs={{1,0},{2,1},{3,2},{4,3},{5,4},{6,5},{7,6},{8,7},{9,8},{10,9},{11,1... | collective-permute-start | bytes 1671176 | tf_op jit(solution)/shard_map/ppermute | solution.py:450
  8.0 60.8 %inner.1 = (f32[256,256]{1,0:T(8,128)}, f32[1,24576]{1,0:T(1,128)}) custom-call(s32[8]{0:T(128)} %refs_0_.3, s32[1]{0:T(128)S(6)} %copy.10.refs_1_, bf16[256,24576]{1,0:T(8,128)(2,1)} %refs_2_.3, f32[1,24576]{1,0:T(1,128)} %bitcast.6, f32[8,24576]{1,0:T(8,128)} %refs_4_.3), custom_call_target="tpu_custom_call" | custom-call | flops 6274678784 | bytes 12582912 | tf_op jit(solution)/shard_map/inner/pallas_call | solution.py:275
  68.8 0.0 collective-permute-done.refs_5_
  68.8 0.0 collective-permute-done.1.refs_6_
  68.8 10.1 %edges.1 = (f32[256,256]{1,0:T(8,128)}, f32[1,24576]{1,0:T(1,128)}) custom-call(s32[8]{0:T(128)} %refs_0_.3, s32[1]{0:T(128)S(6)} %copy.10.refs_1_, bf16[256,24576]{1,0:T(8,128)(2,1)} %refs_2_.3, f32[1,24576]{1,0:T(1,128)} %bitcast.7, f32[8,24576]{1,0:T(8,128)} %refs_4_.3, ...), custom_call_target="tpu_custom_call", output_to_operand_aliasing={{1}: (8, {})} | custom-call | flops 570425344 | bytes 3145728 | tf_op jit(solution)/shard_map/edges/pallas_call | solution.py:275
  78.9 18.5 %all_to_all.17 = f32[16,16,256]{2,1,0:T(8,128)S(1)} all-to-all(f32[16,16,256]{2,1,0:T(8,128)} %bitcast.8), channel_id=1, replica_groups=mesh['grp'=2,'obs'=4,'par'=4] {'obs','par'}, dimensions={0} | all-to-all | bytes 524288 | tf_op jit(solution)/shard_map/all_to_all | solution.py:434
  97.5 13.3 %all_to_all.18 = f32[16,16,256]{2,1,0:T(8,128)} all-to-all(f32[16,16,256]{2,1,0:T(8,128)S(1)} %broadcast_in_dim.10), channel_id=1, replica_groups=mesh['grp'=2,'obs'=4,'par'=4] {'obs','par'}, dimensions={0} | all-to-all | bytes 524288 | tf_op jit(solution)/shard_map/all_to_all | solution.py:437
  110.8 13.5 %update.1 = f32[512,256]{1,0:T(8,128)} custom-call(f32[256,256]{1,0:T(8,128)} %bitcast.4, bf16[512,256]{1,0:T(8,128)(2,1)} %params_ref.1), custom_call_target="tpu_custom_call" | custom-call | tf_op jit(solution)/shard_map/update/pallas_call | solution.py:379
  (2 shorter events, 0.0 us)
Async XLA Ops:
  2.9 65.9 %collective-permute-start = (bf16[272,1024]{1,0:T(8,128)(2,1)}, bf16[272,1024]{1,0:T(8,128)(2,1)}, u32[]{:S(2)}, u32[]{:S(2)}) collective-permute-start(bf16[272,1024]{1,0:T(8,128)(2,1)} %get-tuple-element.8), channel_id=1, source_target_pairs={{0,1},{1,2},{2,3},{3,4},{4,5},{5,6},{6,7},{7,8},{8,9},{9,10},{10,1... | collective-permute-start | bytes 1671176 | tf_op jit(solution)/shard_map/ppermute | solution.py:449
  6.1 62.7 %collective-permute-start.1 = (bf16[272,1024]{1,0:T(8,128)(2,1)}, bf16[272,1024]{1,0:T(8,128)(2,1)}, u32[]{:S(2)}, u32[]{:S(2)}) collective-permute-start(bf16[272,1024]{1,0:T(8,128)(2,1)} %get-tuple-element.9), channel_id=1, source_target_pairs={{1,0},{2,1},{3,2},{4,3},{5,4},{6,5},{7,6},{8,7},{9,8},{10,9},{11,1... | collective-permute-start | bytes 1671176 | tf_op jit(solution)/shard_map/ppermute | solution.py:450

commit v5 on v4

--- a/solution.py
+++ b/solution.py
@@ -23,11 +23,11 @@
 def local_kernel(edge, columns, obs_total, *refs):
     if edge:
         (off_ref, count_ref, pred_ref, obs_ref, band_ref, left_ref, right_ref, gram_in, misfit_in,
-         gram_out, misfit_out, raw, joint, aw, coef, gram, centre, obs, band, row_out, slots,
+         gram_out, misfit_out, raw, joint, aw, coef, gram, obs, band, row_out, slots,
          sems) = refs
     else:
         (off_ref, count_ref, pred_ref, obs_ref, band_ref,
-         gram_out, misfit_out, raw, joint, aw, coef, gram, centre, obs, band, row_out, slots,
+         gram_out, misfit_out, raw, joint, aw, coef, gram, obs, band, row_out, slots,
          sems) = refs
     members = pred_ref.shape[0]
     terms = band_ref.shape[0]
@@ -82,22 +82,19 @@
         slots[place, 1] = offset
         free = free + jnp.where(whole, 0, 1)
 
-    rows = members + PACK
-    row_index = lax.broadcasted_iota(jnp.int32, (rows, members), 0)
-    col_index = lax.broadcasted_iota(jnp.int32, (rows, members), 1)
-    mean_part = 1.0 / members
-    centre[...] = jnp.where(
-        row_index >= members, mean_part, jnp.where(row_index == col_index, 1.0 - mean_part, -mean_part)
-    ).astype(BF)
     gram[...] = jnp.zeros_like(gram)
     aw[...] = jnp.zeros_like(aw)
 
     def anomalies(place):
-        at = pl.ds(pl.multiple_of(place * H, H), H)
-        wide = jnp.dot(centre[...], raw[pl.ds(0, members), at], preferred_element_type=F32)
-        joint[pl.ds(0, members), at] = wide[:members]
-        innovation = obs[:, at] - wide[members:members + SUB]
-        joint[pl.ds(members, SUB), at] = innovation.astype(BF).astype(F32)
+        columns_of = [pl.ds(pl.multiple_of(place * H + t * LANE, LANE), LANE) for t in range(tiles)]
+        means = []
+        for at in columns_of:
+            wide = raw[pl.ds(0, members), at].astype(F32)
+            means.append(jnp.sum(wide, axis=0, keepdims=True) * (1.0 / members))
+        for at, mean in zip(columns_of, means):
+            joint[pl.ds(0, members), at] = (raw[pl.ds(0, members), at].astype(F32) - mean).astype(BF)
+            innovation = jnp.broadcast_to(obs[:, at] - mean, (PACK, LANE))
+            joint[pl.ds(members, PACK), at] = innovation.astype(BF)
 
     def coefficients(column, at):
         index = column + lax.broadcasted_iota(jnp.int32, (1, H), 1)
@@ -111,7 +108,7 @@
             coef[pl.ds(slot * SUB, SUB), :] = jnp.broadcast_to(row, (SUB, H))
 
     def plan(place):
-        lane = lax.broadcasted_iota(jnp.int32, (SUB, LANE), 1)
+        lane = lax.broadcasted_iota(jnp.int32, (PACK, LANE), 1)
         steps = []
         for slot in range(terms):
             if slot < 3:
@@ -123,27 +120,30 @@
                 steps.append((first, lax.rem(LANE - turn, LANE), lane < LANE - turn))
         return steps
 
-    def whiten_rows(steps, starts):
-        acc = [[None] * tiles for _ in starts]
+    def whiten_rows(steps, starts, low, width):
+        acc = [[None] * width for _ in starts]
         for slot, (first, back, keep) in enumerate(steps):
-            weights = [coef[pl.ds(slot * SUB, SUB), pl.ds(t * LANE, LANE)] for t in range(tiles)]
+            weights = []
+            for t in range(width):
+                weight = coef[pl.ds(slot * SUB, SUB), pl.ds((low + t) * LANE, LANE)]
+                weights.append(jnp.concatenate([weight, weight], 0))
             for r, at_row in enumerate(starts):
                 def load(t):
-                    start = pl.multiple_of((first + t) * LANE, LANE)
-                    return joint[pl.ds(at_row, SUB), pl.ds(start, LANE)]
+                    start = pl.multiple_of((first + low + t) * LANE, LANE)
+                    return joint[pl.ds(at_row, PACK), pl.ds(start, LANE)]
 
                 if back is None:
-                    values = [load(t) for t in range(tiles)]
+                    values = [load(t) for t in range(width)]
                 else:
-                    rolled = [pltpu.roll(load(t), back, 1) for t in range(tiles + 1)]
-                    values = [jnp.where(keep, rolled[t], rolled[t + 1]) for t in range(tiles)]
-                for t in range(tiles):
-                    product = values[t] * weights[t]
+                    rolled = [pltpu.roll(load(t), back, 1) for t in range(width + 1)]
+                    values = [jnp.where(keep, rolled[t], rolled[t + 1]) for t in range(width)]
+                for t in range(width):
+                    product = values[t].astype(F32) * weights[t]
                     acc[r][t] = product if acc[r][t] is None else acc[r][t] + product
         return acc
 
     def products():
-        gram[...] += lax.dot_general(
+        return lax.dot_general(
             aw[...], aw[pl.ds(0, members), :], (((1,), (1,)), ((), ())), preferred_element_type=F32)
 
     def whiten_chunk(place, column, at):
@@ -152,29 +152,33 @@
         pending = []
 
         def store_oldest():
-            at_row, values = pending.pop(0)
-            for t in range(tiles):
-                aw[pl.ds(at_row, PACK), pl.ds(t * LANE, LANE)] = values[t]
-
-        acc = whiten_rows(steps, [members])[0]
+            for at_row, tile, value in pending.pop(0):
+                aw[pl.ds(at_row, PACK), pl.ds(tile * LANE, LANE)] = value
+
+        acc = whiten_rows(steps, [members], 0, tiles)[0]
         row = lax.broadcasted_iota(jnp.int32, (PACK, LANE), 0)
         parts = []
         for t in range(tiles):
-            wide = jnp.concatenate([acc[t], acc[t]], 0)
+            wide = acc[t]
             high = wide.astype(BF).astype(F32)
             rest = wide - high
             middle = rest.astype(BF).astype(F32)
             low = rest - middle
             split = jnp.where(row == 0, high, jnp.where(row == 1, middle, jnp.where(row == 2, low, 0.0)))
-            parts.append(split.astype(BF))
-        pending.append((members, parts))
+            parts.append((members, t, split.astype(BF)))
+        pending.append(parts)
         scale = math.sqrt(members - 1) * row_factor
         misfit = [acc[t][0:1] * scale for t in range(tiles)]
-        for group in range(members // PACK):
-            low, high = whiten_rows(steps, [group * PACK, group * PACK + SUB])
-            pending.append((group * PACK, [jnp.concatenate([low[t], high[t]], 0).astype(BF) for t in range(tiles)]))
-            if len(pending) > LATE:
-                store_oldest()
+        width = tiles // 2
+        for group in range(members // (2 * PACK)):
+            starts = [group * 2 * PACK, group * 2 * PACK + PACK]
+            for first in (0, width):
+                out = whiten_rows(steps, starts, first, width)
+                pending.append([
+                    (at_row, first + t, out[r][t].astype(BF))
+                    for r, at_row in enumerate(starts) for t in range(width)])
+                if len(pending) > LATE:
+                    store_oldest()
         while pending:
             store_oldest()
         for t in range(tiles):
@@ -194,8 +198,9 @@
         lax.fori_loop(0, 6, centre_step, 0)
 
         def chunk_step(which, carry):
-            products()
+            added = products()
             whiten_chunk(1 + 3 * which, which * (columns - H), pl.multiple_of(which * H, H))
+            gram[...] += added
             return carry
 
         lax.fori_loop(0, 2, chunk_step, 0)
@@ -216,10 +221,11 @@
 
         def chunk_step(place, carry):
             chunk_copy(place + 1).wait()
-            products()
+            added = products()
             anomalies(place + 1)
             column = pl.multiple_of(place * H, H)
             whiten_chunk(place, column, column)
+            gram[...] += added
             return carry
 
         lax.fori_loop(1, chunks - 1, chunk_step, 0)
@@ -227,7 +233,7 @@
         out_copies = [pltpu.make_async_copy(row_out.at[:, inside], misfit_out.at[:, inside], sems.at[0])]
     for copy in out_copies:
         copy.start()
-    products()
+    gram[...] += products()
 
     tail = gram[pl.ds(members, 8), :]
     total = tail[0:1] + tail[1:2] + tail[2:3]
@@ -260,11 +266,10 @@
         in_specs += [far, far, vmem, far]
     scratch = [
         pltpu.VMEM((rows if edge else members, places * H), BF),
-        pltpu.VMEM((members + SUB, places * H), F32),
+        pltpu.VMEM((rows, places * H), BF),
         pltpu.VMEM((rows, H), BF),
         pltpu.VMEM((SUB * terms, H), F32),
         pltpu.VMEM((rows, members), F32),
-        pltpu.VMEM((rows, members), BF),
         pltpu.VMEM((1, places * H), F32),
         pltpu.VMEM((terms, 2 * H if edge else columns), F32),
         pltpu.VMEM((1, 2 * H if edge else columns), F32),
@@ -428,13 +433,22 @@
     )(predicted, observed)
 
 
+def scatter_sum(values, axis):
+    size, (rows, width) = lax.axis_size(axis), values.shape
+    parts = lax.all_to_all(values, axis, 0, 0, tiled=True)
+    return jnp.sum(parts.reshape(size, rows // size, width), axis=0)
+
+
+def gather_rows(values, axis):
+    size, (rows, width) = lax.axis_size(axis), values.shape
+    copies = jnp.broadcast_to(values[None], (size, rows, width)).reshape(size * rows, width)
+    return lax.all_to_all(copies, axis, 0, 0, tiled=True)
+
+
 def sum_over(values, axes):
-    shards = lax.axis_size(axes)
-    rows, width = values.shape
-    parts = lax.all_to_all(values, axes, 0, 0, tiled=True)
-    own = jnp.sum(parts.reshape(shards, rows // shards, width), axis=0)
-    copies = jnp.broadcast_to(own[None], (shards, rows // shards, width)).reshape(rows, width)
-    return lax.all_to_all(copies, axes, 0, 0, tiled=True)
+    outer, inner = axes
+    own = scatter_sum(scatter_sum(values, inner), outer)
+    return gather_rows(gather_rows(own, outer), inner)
 
 
 def body(predicted, observed, band, offsets, rows_count, params):

time: 125 us -> 122 us (0.976)
  Pallas kernels: 86.6 us -> 75.2 us
  blocking collectives: 31.9 us -> 40.5 us
    pallas_call x2, Pallas kernels: 70.8 us -> 59.4 us  [local_call(): pl.pallas_call(functools.partial(local_kernel, edge, columns, obs_total),...]
    all_to_all x2 -> x4, blocking collectives: 31.9 us -> 40.5 us  [the longest x2 23.3 us: scatter_sum(): parts = lax.all_to_all(values, axis, 0, 0, tiled=True)]
  transfers between devices with their start and end apart: 2 -> 2, of which waited for: 0 -> 0; matrix products, arithmetic and copies ran while one was open for 0% -> 0% of each run, Pallas kernels for 49% -> 41%
where the time goes in v5:
time: 122 us
  Pallas kernels  75.2 us (62%)
  blocking collectives  40.5 us (33%)
  starting transfers between devices  4.43 us (4%)
  between operations  1.34 us (1%)
    pallas_call x2, Pallas kernels, local_call(): pl.pallas_call(functools.partial(local_kernel, edge, columns, obs_total),...  59.4 us
    all_to_all x2, blocking collectives, scatter_sum(): parts = lax.all_to_all(values, axis, 0, 0, tiled=True)  23.3 us
    all_to_all x2, blocking collectives, gather_rows(): return lax.all_to_all(copies, axis, 0, 0, tiled=True)  17.2 us
    pallas_call x1, Pallas kernels, update(): pl.pallas_call(update_kernel, out_shape=jax.ShapeDtypeStruct(params.shape...  13.5 us
    ppermute x1, starting transfers between devices, body(): left = lax.ppermute(last, axes, up)  3.15 us
  transfers between devices with their start and end apart: 2, of which 0 were waited for; matrix products, arithmetic and copies ran while one was open for 0% of the time, Pallas kernels for 41%

profile of v5, /device:TPU:0, one launch (start us, length us, event | category | flops | bytes accessed | tf_op | source)
XLA Modules:
  0.0 121.6 jit_solution(919114683490102214)
XLA Ops:
  0.6 2.3 %halos.1 = (bf16[272,1024]{1,0:T(8,128)(2,1)}, bf16[272,1024]{1,0:T(8,128)(2,1)}) custom-call(bf16[256,24576]{1,0:T(8,128)(2,1)} %refs_2_.3, f32[1,24576]{1,0:T(1,128)} %bitcast.7), custom_call_target="tpu_custom_call" | custom-call | tf_op jit(solution)/shard_map/halos/pallas_call | solution.py:425
  2.9 3.2 %collective-permute-start = (bf16[272,1024]{1,0:T(8,128)(2,1)}, bf16[272,1024]{1,0:T(8,128)(2,1)}, u32[]{:S(2)}, u32[]{:S(2)}) collective-permute-start(bf16[272,1024]{1,0:T(8,128)(2,1)} %get-tuple-element.8), channel_id=1, source_target_pairs={{0,1},{1,2},{2,3},{3,4},{4,5},{5,6},{6,7},{7,8},{8,9},{9,10},{10,1... | collective-permute-start | bytes 1671176 | tf_op jit(solution)/shard_map/ppermute | solution.py:463
  6.1 1.3 %collective-permute-start.1 = (bf16[272,1024]{1,0:T(8,128)(2,1)}, bf16[272,1024]{1,0:T(8,128)(2,1)}, u32[]{:S(2)}, u32[]{:S(2)}) collective-permute-start(bf16[272,1024]{1,0:T(8,128)(2,1)} %get-tuple-element.9), channel_id=1, source_target_pairs={{1,0},{2,1},{3,2},{4,3},{5,4},{6,5},{7,6},{8,7},{9,8},{10,9},{11,1... | collective-permute-start | bytes 1671176 | tf_op jit(solution)/shard_map/ppermute | solution.py:464
  8.0 49.7 %inner.1 = (f32[256,256]{1,0:T(8,128)}, f32[1,24576]{1,0:T(1,128)}) custom-call(s32[8]{0:T(128)} %refs_0_.3, s32[1]{0:T(128)S(6)} %copy.10.refs_1_, bf16[256,24576]{1,0:T(8,128)(2,1)} %refs_2_.3, f32[1,24576]{1,0:T(1,128)} %bitcast.8, f32[8,24576]{1,0:T(8,128)} %refs_4_.3), custom_call_target="tpu_custom_call" | custom-call | flops 6274678784 | bytes 12582912 | tf_op jit(solution)/shard_map/inner/pallas_call | solution.py:280
  57.7 0.0 collective-permute-done.refs_5_
  57.7 0.0 collective-permute-done.1.refs_6_
  57.8 9.7 %edges.1 = (f32[256,256]{1,0:T(8,128)}, f32[1,24576]{1,0:T(1,128)}) custom-call(s32[8]{0:T(128)} %refs_0_.3, s32[1]{0:T(128)S(6)} %copy.10.refs_1_, bf16[256,24576]{1,0:T(8,128)(2,1)} %refs_2_.3, f32[1,24576]{1,0:T(1,128)} %bitcast.9, f32[8,24576]{1,0:T(8,128)} %refs_4_.3, ...), custom_call_target="tpu_custom_call", output_to_operand_aliasing={{1}: (8, {})} | custom-call | flops 570425344 | bytes 3145728 | tf_op jit(solution)/shard_map/edges/pallas_call | solution.py:280
  67.5 11.4 %all_to_all.32 = f32[4,64,256]{2,1,0:T(8,128)S(1)} all-to-all(f32[4,64,256]{2,1,0:T(8,128)} %bitcast.12), channel_id=1, replica_groups=mesh['grp'=2,'obs'=4,'par'=4] {'par'}, dimensions={0} | all-to-all | bytes 524288 | tf_op jit(solution)/shard_map/all_to_all | solution.py:438
  78.9 11.9 %all_to_all.33 = f32[4,16,256]{2,1,0:T(8,128)S(1)} all-to-all(f32[4,16,256]{2,1,0:T(8,128)S(1)} %bitcast.10), channel_id=1, replica_groups=mesh['grp'=2,'obs'=4,'par'=4] {'obs'}, dimensions={0} | all-to-all | bytes 131072 | tf_op jit(solution)/shard_map/all_to_all | solution.py:438
  90.9 8.1 %all_to_all.34 = f32[4,16,256]{2,1,0:T(8,128)S(1)} all-to-all(f32[4,16,256]{2,1,0:T(8,128)S(1)} %broadcast_in_dim.18), channel_id=1, replica_groups=mesh['grp'=2,'obs'=4,'par'=4] {'obs'}, dimensions={0} | all-to-all | bytes 131072 | tf_op jit(solution)/shard_map/all_to_all | solution.py:445
  99.0 9.1 %all_to_all.35 = f32[4,64,256]{2,1,0:T(8,128)} all-to-all(f32[4,64,256]{2,1,0:T(8,128)S(1)} %broadcast_in_dim.20), channel_id=1, replica_groups=mesh['grp'=2,'obs'=4,'par'=4] {'par'}, dimensions={0} | all-to-all | bytes 524288 | tf_op jit(solution)/shard_map/all_to_all | solution.py:445
  108.1 13.5 %update.1 = f32[512,256]{1,0:T(8,128)} custom-call(f32[256,256]{1,0:T(8,128)} %bitcast.6, bf16[512,256]{1,0:T(8,128)(2,1)} %params_ref.1), custom_call_target="tpu_custom_call" | custom-call | tf_op jit(solution)/shard_map/update/pallas_call | solution.py:384
  (4 shorter events, 0.0 us)
Async XLA Ops:
  2.9 54.8 %collective-permute-start = (bf16[272,1024]{1,0:T(8,128)(2,1)}, bf16[272,1024]{1,0:T(8,128)(2,1)}, u32[]{:S(2)}, u32[]{:S(2)}) collective-permute-start(bf16[272,1024]{1,0:T(8,128)(2,1)} %get-tuple-element.8), channel_id=1, source_target_pairs={{0,1},{1,2},{2,3},{3,4},{4,5},{5,6},{6,7},{7,8},{8,9},{9,10},{10,1... | collective-permute-start | bytes 1671176 | tf_op jit(solution)/shard_map/ppermute | solution.py:463
  6.1 51.7 %collective-permute-start.1 = (bf16[272,1024]{1,0:T(8,128)(2,1)}, bf16[272,1024]{1,0:T(8,128)(2,1)}, u32[]{:S(2)}, u32[]{:S(2)}) collective-permute-start(bf16[272,1024]{1,0:T(8,128)(2,1)} %get-tuple-element.9), channel_id=1, source_target_pairs={{1,0},{2,1},{3,2},{4,3},{5,4},{6,5},{7,6},{8,7},{9,8},{10,9},{11,1... | collective-permute-start | bytes 1671176 | tf_op jit(solution)/shard_map/ppermute | solution.py:464

commit v6 on v5

--- a/solution.py
+++ b/solution.py
@@ -13,6 +13,7 @@
 SUB = 8
 PACK = 16
 LATE = 2
+AHEAD = 5
 BLOCK = 64
 PANEL = 8
 VMEM = 64 * 2**20
@@ -36,15 +37,22 @@
     half = members // 2
     row_factor = 1.0 / math.sqrt(obs_total)
 
+    def tile_copies(source, column, place, height):
+        for t in range(tiles):
+            pltpu.make_async_copy(
+                source.at[:, pl.ds(column + t * LANE, LANE)],
+                raw.at[place * tiles + t, pl.ds(0, height), :], sems.at[place]).start()
+
+    def tile_wait(place, height):
+        whole = raw.at[pl.ds(place * tiles, tiles), pl.ds(0, height), :]
+        pltpu.make_async_copy(whole, whole, sems.at[place]).wait()
+
     if edge:
-        copies = [
-            pltpu.make_async_copy(left_ref, raw.at[:, pl.ds(0, H)], sems.at[0]),
-            pltpu.make_async_copy(right_ref, raw.at[:, pl.ds(5 * H, H)], sems.at[5]),
-        ]
+        tile_copies(left_ref, 0, 0, members + PACK)
         for place, chunk in ((1, 0), (2, 1), (3, chunks - 2), (4, chunks - 1)):
-            copies.append(pltpu.make_async_copy(
-                pred_ref.at[:, pl.ds(chunk * H, H)],
-                raw.at[pl.ds(0, members), pl.ds(place * H, H)], sems.at[place]))
+            tile_copies(pred_ref, chunk * H, place, members)
+        tile_copies(right_ref, 0, 5, members + PACK)
+        copies = []
         for which in range(2):
             there = which * (columns - 2 * H)
             copies.append(pltpu.make_async_copy(
@@ -52,23 +60,15 @@
             there = which * (columns - H)
             copies.append(pltpu.make_async_copy(
                 band_ref.at[:, pl.ds(there, H)], band.at[:, pl.ds(which * H, H)], sems.at[8 + which]))
-        for copy in copies:
-            copy.start()
     else:
-        def chunk_copy(place):
-            start = pl.multiple_of(place * H, H)
-            return pltpu.make_async_copy(
-                pred_ref.at[:, pl.ds(start, H)], raw.at[:, pl.ds(start, H)], sems.at[place])
-
         copies = [
             pltpu.make_async_copy(obs_ref, obs, sems.at[chunks]),
             pltpu.make_async_copy(band_ref, band, sems.at[chunks + 1]),
         ]
-        for place in range(chunks):
-            chunk_copy(place).start()
-            if place == 2:
-                for copy in copies:
-                    copy.start()
+        for place in range(AHEAD):
+            tile_copies(pred_ref, place * H, place, members)
+    for copy in copies:
+        copy.start()
 
     slots[0, 0] = 0
     slots[0, 1] = 0
@@ -86,15 +86,16 @@
     aw[...] = jnp.zeros_like(aw)
 
     def anomalies(place):
-        columns_of = [pl.ds(pl.multiple_of(place * H + t * LANE, LANE), LANE) for t in range(tiles)]
         means = []
-        for at in columns_of:
-            wide = raw[pl.ds(0, members), at].astype(F32)
+        for t in range(tiles):
+            wide = raw[place * tiles + t, pl.ds(0, members), :].astype(F32)
             means.append(jnp.sum(wide, axis=0, keepdims=True) * (1.0 / members))
-        for at, mean in zip(columns_of, means):
-            joint[pl.ds(0, members), at] = (raw[pl.ds(0, members), at].astype(F32) - mean).astype(BF)
-            innovation = jnp.broadcast_to(obs[:, at] - mean, (PACK, LANE))
-            joint[pl.ds(members, PACK), at] = innovation.astype(BF)
+        for t, mean in enumerate(means):
+            tile = place * tiles + t
+            joint[tile, pl.ds(0, members), :] = (
+                raw[tile, pl.ds(0, members), :].astype(F32) - mean).astype(BF)
+            seen = obs[:, pl.ds(pl.multiple_of(place * H + t * LANE, LANE), LANE)]
+            joint[tile, pl.ds(members, PACK), :] = jnp.broadcast_to(seen - mean, (PACK, LANE)).astype(BF)
 
     def coefficients(column, at):
         index = column + lax.broadcasted_iota(jnp.int32, (1, H), 1)
@@ -129,8 +130,7 @@
                 weights.append(jnp.concatenate([weight, weight], 0))
             for r, at_row in enumerate(starts):
                 def load(t):
-                    start = pl.multiple_of((first + low + t) * LANE, LANE)
-                    return joint[pl.ds(at_row, PACK), pl.ds(start, LANE)]
+                    return joint[first + low + t, pl.ds(at_row, PACK), :]
 
                 if back is None:
                     values = [load(t) for t in range(width)]
@@ -143,8 +143,9 @@
         return acc
 
     def products():
+        block = jnp.concatenate([aw[t] for t in range(tiles)], axis=1)
         return lax.dot_general(
-            aw[...], aw[pl.ds(0, members), :], (((1,), (1,)), ((), ())), preferred_element_type=F32)
+            block, block[:members], (((1,), (1,)), ((), ())), preferred_element_type=F32)
 
     def whiten_chunk(place, column, at):
         coefficients(column, at)
@@ -153,7 +154,7 @@
 
         def store_oldest():
             for at_row, tile, value in pending.pop(0):
-                aw[pl.ds(at_row, PACK), pl.ds(tile * LANE, LANE)] = value
+                aw[tile, pl.ds(at_row, PACK), :] = value
 
         acc = whiten_rows(steps, [members], 0, tiles)[0]
         row = lax.broadcasted_iota(jnp.int32, (PACK, LANE), 0)
@@ -187,9 +188,12 @@
     if edge:
         for copy in copies:
             copy.wait()
+        for place in range(6):
+            tile_wait(place, members + (PACK if place in (0, 5) else 0))
         for place in (0, 5):
-            pieces = raw[pl.ds(members, PACK), pl.ds(place * H, H)].astype(F32)
-            obs[:, pl.ds(place * H, H)] = pieces[0:1] + pieces[1:2] + pieces[2:3]
+            for t in range(tiles):
+                pieces = raw[place * tiles + t, pl.ds(members, PACK), :].astype(F32)
+                obs[:, pl.ds(place * H + t * LANE, LANE)] = pieces[0:1] + pieces[1:2] + pieces[2:3]
 
         def centre_step(place, carry):
             anomalies(place)
@@ -213,14 +217,20 @@
             copy.wait()
 
         def centre_step(place, carry):
-            chunk_copy(place).wait()
+            tile_wait(place, members)
             anomalies(place)
             return carry
 
         lax.fori_loop(0, 2, centre_step, 0)
 
         def chunk_step(place, carry):
-            chunk_copy(place + 1).wait()
+            tile_wait(place + 1, members)
+
+            @pl.when(place + AHEAD - 1 < chunks)
+            def _():
+                coming = place + AHEAD - 1
+                tile_copies(pred_ref, pl.multiple_of(coming * H, H), coming, members)
+
             added = products()
             anomalies(place + 1)
             column = pl.multiple_of(place * H, H)
@@ -258,6 +268,7 @@
     terms = band.shape[0]
     rows = members + PACK
     places = 6 if edge else columns // H
+    tiles = places * (H // LANE)
     vmem = pl.BlockSpec(memory_space=pltpu.VMEM)
     smem = pl.BlockSpec(memory_space=pltpu.SMEM)
     far = pl.BlockSpec(memory_space=pltpu.HBM)
@@ -265,9 +276,9 @@
     if edge:
         in_specs += [far, far, vmem, far]
     scratch = [
-        pltpu.VMEM((rows if edge else members, places * H), BF),
-        pltpu.VMEM((rows, places * H), BF),
-        pltpu.VMEM((rows, H), BF),
+        pltpu.VMEM((tiles, rows if edge else members, LANE), BF),
+        pltpu.VMEM((tiles, rows, LANE), BF),
+        pltpu.VMEM((H // LANE, rows, LANE), BF),
         pltpu.VMEM((SUB * terms, H), F32),
         pltpu.VMEM((rows, members), F32),
         pltpu.VMEM((1, places * H), F32),
@@ -387,7 +398,7 @@
         in_specs=[vmem, vmem],
         out_specs=vmem,
         scratch_shapes=[pltpu.VMEM((members, 2 * members), F32)],
-        compiler_params=pltpu.CompilerParams(vmem_limit_bytes=VMEM),
+        compiler_params=pltpu.CompilerParams(vmem_limit_bytes=VMEM // 4),
         name="update",
     )(total, params)
 
@@ -433,22 +444,13 @@
     )(predicted, observed)
 
 
-def scatter_sum(values, axis):
-    size, (rows, width) = lax.axis_size(axis), values.shape
-    parts = lax.all_to_all(values, axis, 0, 0, tiled=True)
-    return jnp.sum(parts.reshape(size, rows // size, width), axis=0)
-
-
-def gather_rows(values, axis):
-    size, (rows, width) = lax.axis_size(axis), values.shape
-    copies = jnp.broadcast_to(values[None], (size, rows, width)).reshape(size * rows, width)
-    return lax.all_to_all(copies, axis, 0, 0, tiled=True)
-
-
 def sum_over(values, axes):
-    outer, inner = axes
-    own = scatter_sum(scatter_sum(values, inner), outer)
-    return gather_rows(gather_rows(own, outer), inner)
+    shards = lax.axis_size(axes)
+    rows, width = values.shape
+    parts = lax.all_to_all(values, axes, 0, 0, tiled=True)
+    own = jnp.sum(parts.reshape(shards, rows // shards, width), axis=0)
+    copies = jnp.broadcast_to(own[None], (shards, rows // shards, width)).reshape(rows, width)
+    return lax.all_to_all(copies, axes, 0, 0, tiled=True)
 
 
 def body(predicted, observed, band, offsets, rows_count, params):

time: 122 us -> 94.5 us (0.77)
  Pallas kernels: 75.2 us -> 55.6 us
  blocking collectives: 40.5 us -> 31.4 us
    pallas_call x2, Pallas kernels: 59.4 us -> 40.8 us  [local_call(): pl.pallas_call(functools.partial(local_kernel, edge, columns, obs_total),...]
    all_to_all x4 -> x2, blocking collectives: 40.5 us -> 31.4 us  [the longest x1 18.5 us: sum_over(): parts = lax.all_to_all(values, axes, 0, 0, tiled=True)]
  transfers between devices with their start and end apart: 2 -> 2, of which waited for: 0 -> 0; matrix products, arithmetic and copies ran while one was open for 0% -> 0% of each run, Pallas kernels for 41% -> 36%
where the time goes in v6:
time: 94.5 us; the launch traced here: 93.7 us
  Pallas kernels  55.6 us (59%)
  blocking collectives  31.4 us (33%)
  starting transfers between devices  4.44 us (5%)
  between operations  1.34 us (1%)
  local copies, waits for them, and re-layouts  0.97 us (1%)
    pallas_call x2, Pallas kernels, local_call(): pl.pallas_call(functools.partial(local_kernel, edge, columns, obs_total),...  40.8 us
    all_to_all x1, blocking collectives, sum_over(): parts = lax.all_to_all(values, axes, 0, 0, tiled=True)  18.5 us
    all_to_all x1, blocking collectives, sum_over(): return lax.all_to_all(copies, axes, 0, 0, tiled=True)  12.8 us
    pallas_call x1, Pallas kernels, update(): pl.pallas_call(update_kernel, out_shape=jax.ShapeDtypeStruct(params.shape...  12.4 us
    ppermute x1, starting transfers between devices, body(): left = lax.ppermute(last, axes, up)  3.16 us
    pallas_call x1, Pallas kernels, halo_blocks(): pl.pallas_call(functools.partial(halo_kernel, columns), out_shape=(block,...  2.29 us
  transfers between devices with their start and end apart: 2, of which 0 were waited for; matrix products, arithmetic and copies ran while one was open for 0% of the time, Pallas kernels for 36%

profile of v6, /device:TPU:0, one launch (start us, length us, event | category | flops | bytes accessed | tf_op | source)
XLA Modules:
  0.0 93.7 jit_solution(3669336860403007600)
XLA Ops:
  0.6 2.3 %halos.1 = (bf16[272,1024]{1,0:T(8,128)(2,1)}, bf16[272,1024]{1,0:T(8,128)(2,1)}) custom-call(bf16[256,24576]{1,0:T(8,128)(2,1)} %refs_2_.3, f32[1,24576]{1,0:T(1,128)} %bitcast.5), custom_call_target="tpu_custom_call" | custom-call | tf_op jit(solution)/shard_map/halos/pallas_call | solution.py:436
  2.9 3.2 %collective-permute-start = (bf16[272,1024]{1,0:T(8,128)(2,1)}, bf16[272,1024]{1,0:T(8,128)(2,1)}, u32[]{:S(2)}, u32[]{:S(2)}) collective-permute-start(bf16[272,1024]{1,0:T(8,128)(2,1)} %get-tuple-element.8), channel_id=1, source_target_pairs={{0,1},{1,2},{2,3},{3,4},{4,5},{5,6},{6,7},{7,8},{8,9},{9,10},{10,1... | collective-permute-start | bytes 1671176 | tf_op jit(solution)/shard_map/ppermute | solution.py:465
  6.1 1.3 %collective-permute-start.1 = (bf16[272,1024]{1,0:T(8,128)(2,1)}, bf16[272,1024]{1,0:T(8,128)(2,1)}, u32[]{:S(2)}, u32[]{:S(2)}) collective-permute-start(bf16[272,1024]{1,0:T(8,128)(2,1)} %get-tuple-element.9), channel_id=1, source_target_pairs={{1,0},{2,1},{3,2},{4,3},{5,4},{6,5},{7,6},{8,7},{9,8},{10,9},{11,1... | collective-permute-start | bytes 1671176 | tf_op jit(solution)/shard_map/ppermute | solution.py:466
  8.0 33.4 %inner.1 = (f32[256,256]{1,0:T(8,128)}, f32[1,24576]{1,0:T(1,128)}) custom-call(s32[8]{0:T(128)} %refs_0_.3, s32[1]{0:T(128)S(6)} %copy.10.refs_1_, bf16[256,24576]{1,0:T(8,128)(2,1)} %refs_2_.3, f32[1,24576]{1,0:T(1,128)} %bitcast.6, f32[8,24576]{1,0:T(8,128)} %refs_4_.3), custom_call_target="tpu_custom_call" | custom-call | flops 6274678784 | bytes 12582912 | tf_op jit(solution)/shard_map/inner/pallas_call | solution.py:291
  41.4 0.0 collective-permute-done.refs_5_
  41.5 0.0 collective-permute-done.1.refs_6_
  41.5 7.4 %edges.1 = (f32[256,256]{1,0:T(8,128)}, f32[1,24576]{1,0:T(1,128)}) custom-call(s32[8]{0:T(128)} %refs_0_.3, s32[1]{0:T(128)S(6)} %copy.10.refs_1_, bf16[256,24576]{1,0:T(8,128)(2,1)} %refs_2_.3, f32[1,24576]{1,0:T(1,128)} %bitcast.7, f32[8,24576]{1,0:T(8,128)} %refs_4_.3, ...), custom_call_target="tpu_custom_call", output_to_operand_aliasing={{1}: (8, {})} | custom-call | flops 570425344 | bytes 3145728 | tf_op jit(solution)/shard_map/edges/pallas_call | solution.py:291
  48.9 18.5 %all_to_all.17 = f32[16,16,256]{2,1,0:T(8,128)S(1)} all-to-all(f32[16,16,256]{2,1,0:T(8,128)} %bitcast.8), channel_id=1, replica_groups=mesh['grp'=2,'obs'=4,'par'=4] {'obs','par'}, dimensions={0} | all-to-all | bytes 524288 | tf_op jit(solution)/shard_map/all_to_all | solution.py:450
  67.5 12.8 %all_to_all.18 = f32[16,16,256]{2,1,0:T(8,128)S(1)} all-to-all(f32[16,16,256]{2,1,0:T(8,128)S(1)} %broadcast_in_dim.10), channel_id=1, replica_groups=mesh['grp'=2,'obs'=4,'par'=4] {'obs','par'}, dimensions={0} | all-to-all | bytes 524288 | tf_op jit(solution)/shard_map/all_to_all | solution.py:453
  80.3 0.0 copy-start
  80.3 0.9 %copy-done = bf16[512,256]{1,0:T(8,128)(2,1)S(1)} copy-done((bf16[512,256]{1,0:T(8,128)(2,1)S(1)}, bf16[512,256]{1,0:T(8,128)(2,1)}, u32[]{:S(2)}) %copy-start) | copy-done | bytes 262168
  81.3 12.4 %update.1 = f32[512,256]{1,0:T(8,128)} custom-call(f32[256,256]{1,0:T(8,128)S(1)} %bitcast.4, bf16[512,256]{1,0:T(8,128)(2,1)S(1)} %copy-done), custom_call_target="tpu_custom_call" | custom-call | tf_op jit(solution)/shard_map/update/pallas_call | solution.py:395
  (2 shorter events, 0.0 us)
Async XLA Ops:
  2.9 38.5 %collective-permute-start = (bf16[272,1024]{1,0:T(8,128)(2,1)}, bf16[272,1024]{1,0:T(8,128)(2,1)}, u32[]{:S(2)}, u32[]{:S(2)}) collective-permute-start(bf16[272,1024]{1,0:T(8,128)(2,1)} %get-tuple-element.8), channel_id=1, source_target_pairs={{0,1},{1,2},{2,3},{3,4},{4,5},{5,6},{6,7},{7,8},{8,9},{9,10},{10,1... | collective-permute-start | bytes 1671176 | tf_op jit(solution)/shard_map/ppermute | solution.py:465
  6.1 35.4 %collective-permute-start.1 = (bf16[272,1024]{1,0:T(8,128)(2,1)}, bf16[272,1024]{1,0:T(8,128)(2,1)}, u32[]{:S(2)}, u32[]{:S(2)}) collective-permute-start(bf16[272,1024]{1,0:T(8,128)(2,1)} %get-tuple-element.9), channel_id=1, source_target_pairs={{1,0},{2,1},{3,2},{4,3},{5,4},{6,5},{7,6},{8,7},{9,8},{10,9},{11,1... | collective-permute-start | bytes 1671176 | tf_op jit(solution)/shard_map/ppermute | solution.py:466
  80.3 1.0 %copy-start = (bf16[512,256]{1,0:T(8,128)(2,1)S(1)}, bf16[512,256]{1,0:T(8,128)(2,1)}, u32[]{:S(2)}) copy-start(bf16[512,256]{1,0:T(8,128)(2,1)} %params_ref.1) | copy-start | bytes 786436

commit v7 on v6

--- a/solution.py
+++ b/solution.py
@@ -12,7 +12,8 @@
 LANE = 128
 SUB = 8
 PACK = 16
-LATE = 2
+TALL = 4
+LATE = 0
 AHEAD = 5
 BLOCK = 64
 PANEL = 8
@@ -171,8 +172,8 @@
         scale = math.sqrt(members - 1) * row_factor
         misfit = [acc[t][0:1] * scale for t in range(tiles)]
         width = tiles // 2
-        for group in range(members // (2 * PACK)):
-            starts = [group * 2 * PACK, group * 2 * PACK + PACK]
+        for group in range(members // (TALL * PACK)):
+            starts = [(group * TALL + r) * PACK for r in range(TALL)]
             for first in (0, width):
                 out = whiten_rows(steps, starts, first, width)
                 pending.append([
@@ -248,17 +249,22 @@
     tail = gram[pl.ds(members, 8), :]
     total = tail[0:1] + tail[1:2] + tail[2:3]
     both = gram[pl.ds(0, members), :]
-    top = lax.broadcasted_iota(jnp.int32, (half, half), 0)
-    corner = jnp.where(top == 0, total[:, :half], jnp.where(top == 1, total[:, half:], 0.0))
-    upper = jnp.concatenate([both[:half, :half], corner], 1)
-    lower = both[half:]
-    upper = upper * (1.0 / obs_total)
-    lower = lower * (1.0 / obs_total)
-    if edge:
-        upper = upper + gram_in[pl.ds(0, half), :]
-        lower = lower + gram_in[pl.ds(half, half), :]
-    gram_out[pl.ds(0, half), :] = upper
-    gram_out[pl.ds(half, half), :] = lower
+    down = lax.broadcasted_iota(jnp.int32, (half, half), 0)
+    across = lax.broadcasted_iota(jnp.int32, (half, half), 1)
+
+    def tuck(block, piece):
+        block = jnp.where((down == 1) & (across == half - 1), piece[:, :1], block)
+        return jnp.where((down == 0) & (across > 0), piece, block)
+
+    blocks = (
+        tuck(both[:half, :half], total[:, :half]),
+        both[half:, :half],
+        tuck(both[half:, half:], total[:, half:]),
+    )
+    for index, block in enumerate(blocks):
+        at = pl.ds(index * half, half)
+        block = block * (1.0 / obs_total)
+        gram_out[:, at] = block + gram_in[:, at] if edge else block
     for copy in out_copies:
         copy.wait()
 
@@ -291,7 +297,7 @@
     return pl.pallas_call(
         functools.partial(local_kernel, edge, columns, obs_total),
         out_shape=(
-            jax.ShapeDtypeStruct((members, members), F32),
+            jax.ShapeDtypeStruct((members // 2, members // 2 * 3), F32),
             jax.ShapeDtypeStruct((1, columns), F32),
         ),
         in_specs=in_specs,
@@ -312,9 +318,22 @@
     col_index = lax.broadcasted_iota(jnp.int32, (members, members), 1)
     identity = jnp.where(row_index == col_index, 1.0, 0.0).astype(F32)
     half = members // 2
-    work[:, pl.ds(0, half)] = sum_ref[:, pl.ds(0, half)] + identity[:, :half]
-    work[pl.ds(0, half), pl.ds(half, half)] = sum_ref[pl.ds(half, half), pl.ds(0, half)].T
-    work[pl.ds(half, half), pl.ds(half, half)] = sum_ref[pl.ds(half, half), pl.ds(half, half)] + identity[half:, half:]
+    eye_half = identity[:half, :half]
+    lower = row_index[:half, :half] >= col_index[:half, :half]
+
+    def mirrored(block):
+        return jnp.where(lower, block, block.T) + eye_half
+
+    def tucked(block):
+        first = lax.broadcasted_iota(jnp.int32, (1, half), 1) == 0
+        return jnp.where(first, block[1:2, half - 1:half], block[0:1, :])
+
+    blocks = [sum_ref[:, pl.ds(index * half, half)] for index in range(3)]
+    work[pl.ds(0, half), pl.ds(0, half)] = mirrored(blocks[0])
+    work[pl.ds(0, half), pl.ds(half, half)] = blocks[1].T
+    work[pl.ds(half, half), pl.ds(0, half)] = blocks[1]
+    work[pl.ds(half, half), pl.ds(half, half)] = mirrored(blocks[2])
+    projection = jnp.concatenate([tucked(blocks[0]), tucked(blocks[2])], 1)
     work[:, pl.ds(members, members)] = identity
     panels = BLOCK // PANEL
     sub = lax.broadcasted_iota(jnp.int32, (PANEL, LANE), 0)
@@ -337,23 +356,31 @@
             upper = tile
             full = tile
             cols = [across(tile, c0 + j) for j in range(PANEL)]
-            full_cols = list(cols)
             scale = jnp.zeros((PANEL, LANE), F32)
-            for k in range(PANEL):
-                pivot = down(cols[k], k)
-                inverse = 1.0 / pivot
-                scale = jnp.where(sub == k, pivot, scale)
-                below = jnp.where(sub > k, cols[k] * inverse, 0.0)
+            for k in range(0, PANEL, 2):
+                left, right = cols[k], cols[k + 1]
+                a, b, c = down(left, k), down(left, k + 1), down(right, k + 1)
+                det = a * c - b * b
+                inverse = 1.0 / det
+                ratio = b / a
+                scale = jnp.where(sub == k, a, jnp.where(sub == k + 1, c - b * ratio, scale))
+                from_left = c * left - b * right
+                from_right = a * right - b * left
+
+                def change_of(values):
+                    x, y = down(values, k), down(values, k + 1)
+                    return x, y, (from_left * x + from_right * y) * inverse
 
                 def clear(values):
-                    row = down(values, k) * inverse
-                    return jnp.where(sub == k, row, values - full_cols[k] * row)
-
-                for j in range(k + 1, PANEL):
-                    cols[j] = cols[j] - below * down(cols[j], k)
-                    full_cols[j] = clear(full_cols[j])
-                upper = upper - below * down(upper, k)
+                    x, y, change = change_of(values)
+                    own = jnp.where(sub == k, c * x - b * y, a * y - b * x) * inverse
+                    return jnp.where((sub == k) | (sub == k + 1), own, values - change)
+
+                x, y, change = change_of(upper)
+                upper = upper - jnp.where(sub > k + 1, change, jnp.where(sub == k + 1, ratio * x, 0.0))
                 full = clear(full)
+                for j in range(k + 2, PANEL):
+                    cols[j] = clear(cols[j])
             done.append(upper * lax.rsqrt(scale))
             rows_of = [down(full, k) for k in range(PANEL)]
             for t in range(p + 1, panels):
@@ -372,7 +399,6 @@
                 factor, solved, (((0,), (0,)), ((), ())), precision=highest, preferred_element_type=F32)
 
     inverse = jnp.where(row_index >= col_index, work[:, pl.ds(members, members)], 0.0)
-    projection = jnp.concatenate([sum_ref[pl.ds(r, 1), pl.ds(half, half)] for r in range(2)], 1)
     solved = jnp.sum(inverse * projection, axis=1, keepdims=True)
     weights = jnp.sum(inverse * solved, axis=0, keepdims=True)
     turned = inverse + weights

time: 94.5 us -> 90.9 us (0.962)
  blocking collectives: 31.4 us -> 29.1 us
  Pallas kernels: 55.6 us -> 54.6 us
    pallas_call x1, Pallas kernels: 12.4 us -> 10.8 us  [update(): pl.pallas_call(update_kernel, out_shape=jax.ShapeDtypeStruct(params.shape...]
    all_to_all x1, blocking collectives: 12.8 us -> 11.6 us  [sum_over(): return lax.all_to_all(copies, axes, 0, 0, tiled=True)]
    all_to_all x1, blocking collectives: 18.5 us -> 17.5 us  [sum_over(): parts = lax.all_to_all(values, axes, 0, 0, tiled=True)]
  transfers between devices with their start and end apart: 2 -> 2, of which waited for: 0 -> 0; matrix products, arithmetic and copies ran while one was open for 0% -> 0% of each run, Pallas kernels for 36% -> 38%
where the time goes in v7:
time: 90.9 us; the launch traced here: 90.4 us
  Pallas kernels  54.6 us (60%)
  blocking collectives  29.1 us (32%)
  starting transfers between devices  4.44 us (5%)
  between operations  1.34 us (1%)
  local copies, waits for them, and re-layouts  0.96 us (1%)
    pallas_call x2, Pallas kernels, local_call(): pl.pallas_call(functools.partial(local_kernel, edge, columns, obs_total),...  41.4 us
    all_to_all x1, blocking collectives, sum_over(): parts = lax.all_to_all(values, axes, 0, 0, tiled=True)  17.5 us
    all_to_all x1, blocking collectives, sum_over(): return lax.all_to_all(copies, axes, 0, 0, tiled=True)  11.6 us
    pallas_call x1, Pallas kernels, update(): pl.pallas_call(update_kernel, out_shape=jax.ShapeDtypeStruct(params.shape...  10.8 us
    ppermute x1, starting transfers between devices, body(): left = lax.ppermute(last, axes, up)  3.16 us
    pallas_call x1, Pallas kernels, halo_blocks(): pl.pallas_call(functools.partial(halo_kernel, columns), out_shape=(block,...  2.29 us
  transfers between devices with their start and end apart: 2, of which 0 were waited for; matrix products, arithmetic and copies ran while one was open for 0% of the time, Pallas kernels for 38%

profile of v7, /device:TPU:0, one launch (start us, length us, event | category | flops | bytes accessed | tf_op | source)
XLA Modules:
  0.0 90.4 jit_solution(15608482269472067573)
XLA Ops:
  0.6 2.3 %halos.1 = (bf16[272,1024]{1,0:T(8,128)(2,1)}, bf16[272,1024]{1,0:T(8,128)(2,1)}) custom-call(bf16[256,24576]{1,0:T(8,128)(2,1)} %refs_2_.3, f32[1,24576]{1,0:T(1,128)} %bitcast.5), custom_call_target="tpu_custom_call" | custom-call | tf_op jit(solution)/shard_map/halos/pallas_call | solution.py:462
  2.9 3.2 %collective-permute-start = (bf16[272,1024]{1,0:T(8,128)(2,1)}, bf16[272,1024]{1,0:T(8,128)(2,1)}, u32[]{:S(2)}, u32[]{:S(2)}) collective-permute-start(bf16[272,1024]{1,0:T(8,128)(2,1)} %get-tuple-element.8), channel_id=1, source_target_pairs={{0,1},{1,2},{2,3},{3,4},{4,5},{5,6},{6,7},{7,8},{8,9},{9,10},{10,1... | collective-permute-start | bytes 1671176 | tf_op jit(solution)/shard_map/ppermute | solution.py:491
  6.1 1.3 %collective-permute-start.1 = (bf16[272,1024]{1,0:T(8,128)(2,1)}, bf16[272,1024]{1,0:T(8,128)(2,1)}, u32[]{:S(2)}, u32[]{:S(2)}) collective-permute-start(bf16[272,1024]{1,0:T(8,128)(2,1)} %get-tuple-element.9), channel_id=1, source_target_pairs={{1,0},{2,1},{3,2},{4,3},{5,4},{6,5},{7,6},{8,7},{9,8},{10,9},{11,1... | collective-permute-start | bytes 1671176 | tf_op jit(solution)/shard_map/ppermute | solution.py:492
  8.0 34.1 %inner.1 = (f32[128,384]{1,0:T(8,128)}, f32[1,24576]{1,0:T(1,128)}) custom-call(s32[8]{0:T(128)} %refs_0_.3, s32[1]{0:T(128)S(6)} %copy.10.refs_1_, bf16[256,24576]{1,0:T(8,128)(2,1)} %refs_2_.3, f32[1,24576]{1,0:T(1,128)} %bitcast.6, f32[8,24576]{1,0:T(8,128)} %refs_4_.3), custom_call_target="tpu_custom_call" | custom-call | flops 6274678784 | bytes 12582912 | tf_op jit(solution)/shard_map/inner/pallas_call | solution.py:297
  42.1 0.0 collective-permute-done.refs_5_
  42.1 0.0 collective-permute-done.1.refs_6_
  42.1 7.4 %edges.1 = (f32[128,384]{1,0:T(8,128)}, f32[1,24576]{1,0:T(1,128)}) custom-call(s32[8]{0:T(128)} %refs_0_.3, s32[1]{0:T(128)S(6)} %copy.10.refs_1_, bf16[256,24576]{1,0:T(8,128)(2,1)} %refs_2_.3, f32[1,24576]{1,0:T(1,128)} %bitcast.7, f32[8,24576]{1,0:T(8,128)} %refs_4_.3, ...), custom_call_target="tpu_custom_call", output_to_operand_aliasing={{1}: (8, {})} | custom-call | flops 570425344 | bytes 3145728 | tf_op jit(solution)/shard_map/edges/pallas_call | solution.py:297
  49.5 17.5 %all_to_all.17 = f32[16,8,384]{2,1,0:T(8,128)S(1)} all-to-all(f32[16,8,384]{2,1,0:T(8,128)} %bitcast.8), channel_id=1, replica_groups=mesh['grp'=2,'obs'=4,'par'=4] {'obs','par'}, dimensions={0} | all-to-all | bytes 393216 | tf_op jit(solution)/shard_map/all_to_all | solution.py:476
  67.0 11.6 %all_to_all.18 = f32[16,8,384]{2,1,0:T(8,128)S(1)} all-to-all(f32[16,8,384]{2,1,0:T(8,128)S(1)} %broadcast_in_dim.10), channel_id=1, replica_groups=mesh['grp'=2,'obs'=4,'par'=4] {'obs','par'}, dimensions={0} | all-to-all | bytes 393216 | tf_op jit(solution)/shard_map/all_to_all | solution.py:479
  78.6 0.0 copy-start
  78.6 0.9 %copy-done = bf16[512,256]{1,0:T(8,128)(2,1)S(1)} copy-done((bf16[512,256]{1,0:T(8,128)(2,1)S(1)}, bf16[512,256]{1,0:T(8,128)(2,1)}, u32[]{:S(2)}) %copy-start) | copy-done | bytes 262168
  79.6 10.8 %update.1 = f32[512,256]{1,0:T(8,128)} custom-call(f32[128,384]{1,0:T(8,128)S(1)} %bitcast.4, bf16[512,256]{1,0:T(8,128)(2,1)S(1)} %copy-done), custom_call_target="tpu_custom_call" | custom-call | tf_op jit(solution)/shard_map/update/pallas_call | solution.py:421
  (2 shorter events, 0.0 us)
Async XLA Ops:
  2.9 39.2 %collective-permute-start = (bf16[272,1024]{1,0:T(8,128)(2,1)}, bf16[272,1024]{1,0:T(8,128)(2,1)}, u32[]{:S(2)}, u32[]{:S(2)}) collective-permute-start(bf16[272,1024]{1,0:T(8,128)(2,1)} %get-tuple-element.8), channel_id=1, source_target_pairs={{0,1},{1,2},{2,3},{3,4},{4,5},{5,6},{6,7},{7,8},{8,9},{9,10},{10,1... | collective-permute-start | bytes 1671176 | tf_op jit(solution)/shard_map/ppermute | solution.py:491
  6.1 36.0 %collective-permute-start.1 = (bf16[272,1024]{1,0:T(8,128)(2,1)}, bf16[272,1024]{1,0:T(8,128)(2,1)}, u32[]{:S(2)}, u32[]{:S(2)}) collective-permute-start(bf16[272,1024]{1,0:T(8,128)(2,1)} %get-tuple-element.9), channel_id=1, source_target_pairs={{1,0},{2,1},{3,2},{4,3},{5,4},{6,5},{7,6},{8,7},{9,8},{10,9},{11,1... | collective-permute-start | bytes 1671176 | tf_op jit(solution)/shard_map/ppermute | solution.py:492
  78.6 1.0 %copy-start = (bf16[512,256]{1,0:T(8,128)(2,1)S(1)}, bf16[512,256]{1,0:T(8,128)(2,1)}, u32[]{:S(2)}) copy-start(bf16[512,256]{1,0:T(8,128)(2,1)} %params_ref.1) | copy-start | bytes 786436

commit v8 on v7

--- a/solution.py
+++ b/solution.py
@@ -25,11 +25,11 @@
 def local_kernel(edge, columns, obs_total, *refs):
     if edge:
         (off_ref, count_ref, pred_ref, obs_ref, band_ref, left_ref, right_ref, gram_in, misfit_in,
-         gram_out, misfit_out, raw, joint, aw, coef, gram, obs, band, row_out, slots,
+         gram_out, misfit_out, raw, special, aw, coef, mean_white, gram, obs, band, row_out, slots,
          sems) = refs
     else:
         (off_ref, count_ref, pred_ref, obs_ref, band_ref,
-         gram_out, misfit_out, raw, joint, aw, coef, gram, obs, band, row_out, slots,
+         gram_out, misfit_out, raw, special, aw, coef, mean_white, gram, obs, band, row_out, slots,
          sems) = refs
     members = pred_ref.shape[0]
     terms = band_ref.shape[0]
@@ -86,17 +86,17 @@
     gram[...] = jnp.zeros_like(gram)
     aw[...] = jnp.zeros_like(aw)
 
-    def anomalies(place):
-        means = []
+    def mean_rows(place):
+        block = jnp.concatenate(
+            [raw[place * tiles + t, pl.ds(0, members), :] for t in range(tiles)], axis=1)
+        return jnp.dot(jnp.full((PACK, members), 1.0 / members, BF), block, preferred_element_type=F32)[:SUB]
+
+    def keep_special(place, mean):
+        seen = obs[:, pl.ds(pl.multiple_of(place * H, H), H)]
+        innovation = (seen - mean).astype(BF).astype(F32)
+        value = jnp.where(lax.broadcasted_iota(jnp.int32, (SUB, H), 0) == 0, innovation, mean)
         for t in range(tiles):
-            wide = raw[place * tiles + t, pl.ds(0, members), :].astype(F32)
-            means.append(jnp.sum(wide, axis=0, keepdims=True) * (1.0 / members))
-        for t, mean in enumerate(means):
-            tile = place * tiles + t
-            joint[tile, pl.ds(0, members), :] = (
-                raw[tile, pl.ds(0, members), :].astype(F32) - mean).astype(BF)
-            seen = obs[:, pl.ds(pl.multiple_of(place * H + t * LANE, LANE), LANE)]
-            joint[tile, pl.ds(members, PACK), :] = jnp.broadcast_to(seen - mean, (PACK, LANE)).astype(BF)
+            special[place * tiles + t] = value[:, t * LANE:(t + 1) * LANE]
 
     def coefficients(column, at):
         index = column + lax.broadcasted_iota(jnp.int32, (1, H), 1)
@@ -111,36 +111,48 @@
 
     def plan(place):
         lane = lax.broadcasted_iota(jnp.int32, (PACK, LANE), 1)
+        low_lane = lax.broadcasted_iota(jnp.int32, (SUB, LANE), 1)
         steps = []
         for slot in range(terms):
             if slot < 3:
-                steps.append((place * tiles + (0, -tiles, tiles)[slot], None, None))
+                steps.append((place * tiles + (0, -tiles, tiles)[slot], None, None, None))
             else:
                 offset = slots[slot, 1] + 8 * LANE
                 turn = lax.rem(offset, LANE)
                 first = place * tiles + lax.div(offset, LANE) - 8
-                steps.append((first, lax.rem(LANE - turn, LANE), lane < LANE - turn))
+                back = lax.rem(LANE - turn, LANE)
+                steps.append((first, back, lane < LANE - turn, low_lane < LANE - turn))
         return steps
 
+    def shifted(load, back, keep, width):
+        if back is None:
+            return [load(t) for t in range(width)]
+        rolled = [pltpu.roll(load(t), back, 1) for t in range(width + 1)]
+        return [jnp.where(keep, rolled[t], rolled[t + 1]) for t in range(width)]
+
+    def whiten_special(steps):
+        acc = [None] * tiles
+        for slot, (first, back, _, keep) in enumerate(steps):
+            values = shifted(lambda t: special[first + t], back, keep, tiles)
+            for t in range(tiles):
+                product = values[t] * coef[pl.ds(slot * SUB, SUB), pl.ds(t * LANE, LANE)]
+                acc[t] = product if acc[t] is None else acc[t] + product
+        return acc
+
     def whiten_rows(steps, starts, low, width):
-        acc = [[None] * width for _ in starts]
-        for slot, (first, back, keep) in enumerate(steps):
-            weights = []
-            for t in range(width):
-                weight = coef[pl.ds(slot * SUB, SUB), pl.ds((low + t) * LANE, LANE)]
-                weights.append(jnp.concatenate([weight, weight], 0))
+        def twice(ref, at_row, t):
+            value = ref[pl.ds(at_row, SUB), pl.ds((low + t) * LANE, LANE)]
+            return jnp.concatenate([value, value], 0)
+
+        off = [twice(mean_white, 0, t) for t in range(width)]
+        acc = [list(off) for _ in starts]
+        for slot, (first, back, keep, _) in enumerate(steps):
+            weights = [twice(coef, slot * SUB, t) for t in range(width)]
             for r, at_row in enumerate(starts):
-                def load(t):
-                    return joint[first + low + t, pl.ds(at_row, PACK), :]
-
-                if back is None:
-                    values = [load(t) for t in range(width)]
-                else:
-                    rolled = [pltpu.roll(load(t), back, 1) for t in range(width + 1)]
-                    values = [jnp.where(keep, rolled[t], rolled[t + 1]) for t in range(width)]
+                values = shifted(lambda t: raw[first + low + t, pl.ds(at_row, PACK), :], back, keep, width)
                 for t in range(width):
                     product = values[t].astype(F32) * weights[t]
-                    acc[r][t] = product if acc[r][t] is None else acc[r][t] + product
+                    acc[r][t] = product - acc[r][t] if slot == 0 else acc[r][t] + product
         return acc
 
     def products():
@@ -157,11 +169,12 @@
             for at_row, tile, value in pending.pop(0):
                 aw[tile, pl.ds(at_row, PACK), :] = value
 
-        acc = whiten_rows(steps, [members], 0, tiles)[0]
+        acc = whiten_special(steps)
         row = lax.broadcasted_iota(jnp.int32, (PACK, LANE), 0)
         parts = []
         for t in range(tiles):
-            wide = acc[t]
+            mean_white[:, pl.ds(t * LANE, LANE)] = jnp.broadcast_to(acc[t][1:2], (SUB, LANE))
+            wide = jnp.broadcast_to(acc[t][0:1], (PACK, LANE))
             high = wide.astype(BF).astype(F32)
             rest = wide - high
             middle = rest.astype(BF).astype(F32)
@@ -197,7 +210,7 @@
                 obs[:, pl.ds(place * H + t * LANE, LANE)] = pieces[0:1] + pieces[1:2] + pieces[2:3]
 
         def centre_step(place, carry):
-            anomalies(place)
+            keep_special(place, mean_rows(place))
             return carry
 
         lax.fori_loop(0, 6, centre_step, 0)
@@ -219,13 +232,17 @@
 
         def centre_step(place, carry):
             tile_wait(place, members)
-            anomalies(place)
+            keep_special(place, mean_rows(place))
             return carry
 
-        lax.fori_loop(0, 2, centre_step, 0)
+        lax.fori_loop(0, 3, centre_step, 0)
 
         def chunk_step(place, carry):
-            tile_wait(place + 1, members)
+            ahead = jnp.minimum(place + 2, chunks - 1)
+
+            @pl.when(place + 2 < chunks)
+            def _():
+                tile_wait(ahead, members)
 
             @pl.when(place + AHEAD - 1 < chunks)
             def _():
@@ -233,10 +250,11 @@
                 tile_copies(pred_ref, pl.multiple_of(coming * H, H), coming, members)
 
             added = products()
-            anomalies(place + 1)
+            mean = mean_rows(ahead)
             column = pl.multiple_of(place * H, H)
             whiten_chunk(place, column, column)
             gram[...] += added
+            keep_special(ahead, mean)
             return carry
 
         lax.fori_loop(1, chunks - 1, chunk_step, 0)
@@ -283,9 +301,10 @@
         in_specs += [far, far, vmem, far]
     scratch = [
         pltpu.VMEM((tiles, rows if edge else members, LANE), BF),
-        pltpu.VMEM((tiles, rows, LANE), BF),
+        pltpu.VMEM((tiles, SUB, LANE), F32),
         pltpu.VMEM((H // LANE, rows, LANE), BF),
         pltpu.VMEM((SUB * terms, H), F32),
+        pltpu.VMEM((SUB, H), F32),
         pltpu.VMEM((rows, members), F32),
         pltpu.VMEM((1, places * H), F32),
         pltpu.VMEM((terms, 2 * H if edge else columns), F32),

time: 90.9 us -> 86.4 us (0.950)
  Pallas kernels: 54.6 us -> 50.1 us
    pallas_call x2, Pallas kernels: 41.4 us -> 37 us  [local_call(): pl.pallas_call(functools.partial(local_kernel, edge, columns, obs_total),...]
  transfers between devices with their start and end apart: 2 -> 2, of which waited for: 0 -> 0; matrix products, arithmetic and copies ran while one was open for 0% -> 0% of each run, Pallas kernels for 38% -> 34%
where the time goes in v8:
time: 86.4 us; the launch traced here: 86 us
  Pallas kernels  50.1 us (58%)
  blocking collectives  29.1 us (34%)
  starting transfers between devices  4.44 us (5%)
  between operations  1.34 us (2%)
  local copies, waits for them, and re-layouts  0.96 us (1%)
    pallas_call x2, Pallas kernels, local_call(): pl.pallas_call(functools.partial(local_kernel, edge, columns, obs_total),...  37 us
    all_to_all x1, blocking collectives, sum_over(): parts = lax.all_to_all(values, axes, 0, 0, tiled=True)  17.5 us
    all_to_all x1, blocking collectives, sum_over(): return lax.all_to_all(copies, axes, 0, 0, tiled=True)  11.6 us
    pallas_call x1, Pallas kernels, update(): pl.pallas_call(update_kernel, out_shape=jax.ShapeDtypeStruct(params.shape...  10.8 us
    ppermute x1, starting transfers between devices, body(): left = lax.ppermute(last, axes, up)  3.16 us
    pallas_call x1, Pallas kernels, halo_blocks(): pl.pallas_call(functools.partial(halo_kernel, columns), out_shape=(block,...  2.29 us
  transfers between devices with their start and end apart: 2, of which 0 were waited for; matrix products, arithmetic and copies ran while one was open for 0% of the time, Pallas kernels for 34%

profile of v8, /device:TPU:0, one launch (start us, length us, event | category | flops | bytes accessed | tf_op | source)
XLA Modules:
  0.0 86.0 jit_solution(2216309353034587091)
XLA Ops:
  0.6 2.3 %halos.1 = (bf16[272,1024]{1,0:T(8,128)(2,1)}, bf16[272,1024]{1,0:T(8,128)(2,1)}) custom-call(bf16[256,24576]{1,0:T(8,128)(2,1)} %refs_2_.3, f32[1,24576]{1,0:T(1,128)} %bitcast.5), custom_call_target="tpu_custom_call" | custom-call | tf_op jit(solution)/shard_map/halos/pallas_call | solution.py:481
  2.9 3.2 %collective-permute-start = (bf16[272,1024]{1,0:T(8,128)(2,1)}, bf16[272,1024]{1,0:T(8,128)(2,1)}, u32[]{:S(2)}, u32[]{:S(2)}) collective-permute-start(bf16[272,1024]{1,0:T(8,128)(2,1)} %get-tuple-element.8), channel_id=1, source_target_pairs={{0,1},{1,2},{2,3},{3,4},{4,5},{5,6},{6,7},{7,8},{8,9},{9,10},{10,1... | collective-permute-start | bytes 1671176 | tf_op jit(solution)/shard_map/ppermute | solution.py:510
  6.1 1.3 %collective-permute-start.1 = (bf16[272,1024]{1,0:T(8,128)(2,1)}, bf16[272,1024]{1,0:T(8,128)(2,1)}, u32[]{:S(2)}, u32[]{:S(2)}) collective-permute-start(bf16[272,1024]{1,0:T(8,128)(2,1)} %get-tuple-element.9), channel_id=1, source_target_pairs={{1,0},{2,1},{3,2},{4,3},{5,4},{6,5},{7,6},{8,7},{9,8},{10,9},{11,1... | collective-permute-start | bytes 1671176 | tf_op jit(solution)/shard_map/ppermute | solution.py:511
  8.0 29.3 %inner.1 = (f32[128,384]{1,0:T(8,128)}, f32[1,24576]{1,0:T(1,128)}) custom-call(s32[8]{0:T(128)} %refs_0_.3, s32[1]{0:T(128)S(6)} %copy.10.refs_1_, bf16[256,24576]{1,0:T(8,128)(2,1)} %refs_2_.3, f32[1,24576]{1,0:T(1,128)} %bitcast.6, f32[8,24576]{1,0:T(8,128)} %refs_4_.3), custom_call_target="tpu_custom_call" | custom-call | flops 6274678784 | bytes 12582912 | tf_op jit(solution)/shard_map/inner/pallas_call | solution.py:316
  37.3 0.0 collective-permute-done.refs_5_
  37.3 0.0 collective-permute-done.1.refs_6_
  37.4 7.7 %edges.1 = (f32[128,384]{1,0:T(8,128)}, f32[1,24576]{1,0:T(1,128)}) custom-call(s32[8]{0:T(128)} %refs_0_.3, s32[1]{0:T(128)S(6)} %copy.10.refs_1_, bf16[256,24576]{1,0:T(8,128)(2,1)} %refs_2_.3, f32[1,24576]{1,0:T(1,128)} %bitcast.7, f32[8,24576]{1,0:T(8,128)} %refs_4_.3, ...), custom_call_target="tpu_custom_call", output_to_operand_aliasing={{1}: (8, {})} | custom-call | flops 570425344 | bytes 3145728 | tf_op jit(solution)/shard_map/edges/pallas_call | solution.py:316
  45.0 17.5 %all_to_all.17 = f32[16,8,384]{2,1,0:T(8,128)S(1)} all-to-all(f32[16,8,384]{2,1,0:T(8,128)} %bitcast.8), channel_id=1, replica_groups=mesh['grp'=2,'obs'=4,'par'=4] {'obs','par'}, dimensions={0} | all-to-all | bytes 393216 | tf_op jit(solution)/shard_map/all_to_all | solution.py:495
  62.6 11.6 %all_to_all.18 = f32[16,8,384]{2,1,0:T(8,128)S(1)} all-to-all(f32[16,8,384]{2,1,0:T(8,128)S(1)} %broadcast_in_dim.10), channel_id=1, replica_groups=mesh['grp'=2,'obs'=4,'par'=4] {'obs','par'}, dimensions={0} | all-to-all | bytes 393216 | tf_op jit(solution)/shard_map/all_to_all | solution.py:498
  74.2 0.0 copy-start
  74.2 0.9 %copy-done = bf16[512,256]{1,0:T(8,128)(2,1)S(1)} copy-done((bf16[512,256]{1,0:T(8,128)(2,1)S(1)}, bf16[512,256]{1,0:T(8,128)(2,1)}, u32[]{:S(2)}) %copy-start) | copy-done | bytes 262168
  75.1 10.8 %update.1 = f32[512,256]{1,0:T(8,128)} custom-call(f32[128,384]{1,0:T(8,128)S(1)} %bitcast.4, bf16[512,256]{1,0:T(8,128)(2,1)S(1)} %copy-done), custom_call_target="tpu_custom_call" | custom-call | tf_op jit(solution)/shard_map/update/pallas_call | solution.py:440
  (2 shorter events, 0.0 us)
Async XLA Ops:
  2.9 34.4 %collective-permute-start = (bf16[272,1024]{1,0:T(8,128)(2,1)}, bf16[272,1024]{1,0:T(8,128)(2,1)}, u32[]{:S(2)}, u32[]{:S(2)}) collective-permute-start(bf16[272,1024]{1,0:T(8,128)(2,1)} %get-tuple-element.8), channel_id=1, source_target_pairs={{0,1},{1,2},{2,3},{3,4},{4,5},{5,6},{6,7},{7,8},{8,9},{9,10},{10,1... | collective-permute-start | bytes 1671176 | tf_op jit(solution)/shard_map/ppermute | solution.py:510
  6.1 31.3 %collective-permute-start.1 = (bf16[272,1024]{1,0:T(8,128)(2,1)}, bf16[272,1024]{1,0:T(8,128)(2,1)}, u32[]{:S(2)}, u32[]{:S(2)}) collective-permute-start(bf16[272,1024]{1,0:T(8,128)(2,1)} %get-tuple-element.9), channel_id=1, source_target_pairs={{1,0},{2,1},{3,2},{4,3},{5,4},{6,5},{7,6},{8,7},{9,8},{10,9},{11,1... | collective-permute-start | bytes 1671176 | tf_op jit(solution)/shard_map/ppermute | solution.py:511
  74.2 1.0 %copy-start = (bf16[512,256]{1,0:T(8,128)(2,1)S(1)}, bf16[512,256]{1,0:T(8,128)(2,1)}, u32[]{:S(2)}) copy-start(bf16[512,256]{1,0:T(8,128)(2,1)} %params_ref.1) | copy-start | bytes 786436

commit v9 on v8

--- a/solution.py
+++ b/solution.py
@@ -13,7 +13,7 @@
 SUB = 8
 PACK = 16
 TALL = 4
-LATE = 0
+LATE = 1
 AHEAD = 5
 BLOCK = 64
 PANEL = 8
@@ -49,10 +49,6 @@
         pltpu.make_async_copy(whole, whole, sems.at[place]).wait()
 
     if edge:
-        tile_copies(left_ref, 0, 0, members + PACK)
-        for place, chunk in ((1, 0), (2, 1), (3, chunks - 2), (4, chunks - 1)):
-            tile_copies(pred_ref, chunk * H, place, members)
-        tile_copies(right_ref, 0, 5, members + PACK)
         copies = []
         for which in range(2):
             there = which * (columns - 2 * H)
@@ -66,10 +62,16 @@
             pltpu.make_async_copy(obs_ref, obs, sems.at[chunks]),
             pltpu.make_async_copy(band_ref, band, sems.at[chunks + 1]),
         ]
+    for copy in copies:
+        copy.start()
+    if edge:
+        tile_copies(left_ref, 0, 0, members + PACK)
+        for place, chunk in ((1, 0), (2, 1), (3, chunks - 2), (4, chunks - 1)):
+            tile_copies(pred_ref, chunk * H, place, members)
+        tile_copies(right_ref, 0, 5, members + PACK)
+    else:
         for place in range(AHEAD):
             tile_copies(pred_ref, place * H, place, members)
-    for copy in copies:
-        copy.start()
 
     slots[0, 0] = 0
     slots[0, 1] = 0
@@ -202,26 +204,20 @@
     if edge:
         for copy in copies:
             copy.wait()
-        for place in range(6):
-            tile_wait(place, members + (PACK if place in (0, 5) else 0))
-        for place in (0, 5):
+        for which in range(2):
+            near = range(3 * which, 3 * which + 3)
+            halo = 5 * which
+            for place in near:
+                tile_wait(place, members + (PACK if place == halo else 0))
+            if which == 1:
+                gram[...] += products()
+            means = [mean_rows(place) for place in near]
             for t in range(tiles):
-                pieces = raw[place * tiles + t, pl.ds(members, PACK), :].astype(F32)
-                obs[:, pl.ds(place * H + t * LANE, LANE)] = pieces[0:1] + pieces[1:2] + pieces[2:3]
-
-        def centre_step(place, carry):
-            keep_special(place, mean_rows(place))
-            return carry
-
-        lax.fori_loop(0, 6, centre_step, 0)
-
-        def chunk_step(which, carry):
-            added = products()
-            whiten_chunk(1 + 3 * which, which * (columns - H), pl.multiple_of(which * H, H))
-            gram[...] += added
-            return carry
-
-        lax.fori_loop(0, 2, chunk_step, 0)
+                pieces = raw[halo * tiles + t, pl.ds(members, PACK), :].astype(F32)
+                obs[:, pl.ds(halo * H + t * LANE, LANE)] = pieces[0:1] + pieces[1:2] + pieces[2:3]
+            for place, mean in zip(near, means):
+                keep_special(place, mean)
+            whiten_chunk(1 + 3 * which, which * (columns - H), which * H)
         out_copies = [
             pltpu.make_async_copy(row_out.at[:, pl.ds(0, H)], misfit_out.at[:, pl.ds(0, H)], sems.at[0]),
             pltpu.make_async_copy(row_out.at[:, pl.ds(H, H)], misfit_out.at[:, pl.ds(columns - H, H)], sems.at[1]),
@@ -330,8 +326,10 @@
     )(offsets, rows_count, predicted, observed, band, *more)
 
 
-def update_kernel(sum_ref, params_ref, out_ref, work):
+def update_kernel(sum_ref, params_ref, out_ref, work, params, sem):
     members = params_ref.shape[1]
+    fetch = pltpu.make_async_copy(params_ref, params, sem)
+    fetch.start()
     highest = lax.Precision.HIGHEST
     row_index = lax.broadcasted_iota(jnp.int32, (members, members), 0)
     col_index = lax.broadcasted_iota(jnp.int32, (members, members), 1)
@@ -409,12 +407,15 @@
                     change = [a + b for a, b in zip(change[::2], change[1::2])]
                 tiles[t] = tile_t - change[0]
         lower_inverse = jnp.concatenate(done, axis=0)[:, BLOCK:2 * BLOCK]
-        solved = jnp.dot(lower_inverse, work[pl.ds(r0, BLOCK), :], precision=highest, preferred_element_type=F32)
-        work[pl.ds(r0, BLOCK), :] = solved
+        begin = (r0 + BLOCK) // LANE * LANE
+        end = members + -(-(r0 + BLOCK) // LANE) * LANE
+        wide = pl.ds(begin, end - begin)
+        solved = jnp.dot(lower_inverse, work[pl.ds(r0, BLOCK), wide], precision=highest, preferred_element_type=F32)
+        work[pl.ds(r0, BLOCK), wide] = solved
         if r0 + BLOCK < members:
             rest = members - r0 - BLOCK
-            factor = solved[:, r0 + BLOCK:members]
-            work[pl.ds(r0 + BLOCK, rest), :] = work[pl.ds(r0 + BLOCK, rest), :] - lax.dot_general(
+            factor = solved[:, r0 + BLOCK - begin:members - begin]
+            work[pl.ds(r0 + BLOCK, rest), wide] = work[pl.ds(r0 + BLOCK, rest), wide] - lax.dot_general(
                 factor, solved, (((0,), (0,)), ((), ())), precision=highest, preferred_element_type=F32)
 
     inverse = jnp.where(row_index >= col_index, work[:, pl.ds(members, members)], 0.0)
@@ -426,10 +427,10 @@
     rest = turned - high.astype(F32)
     middle = rest.astype(BF)
     low = (rest - middle.astype(F32)).astype(BF)
-    params = params_ref[...]
+    fetch.wait()
 
     def times(part):
-        return lax.dot_general(params, part, (((1,), (1,)), ((), ())), preferred_element_type=F32)
+        return lax.dot_general(params[...], part, (((1,), (1,)), ((), ())), preferred_element_type=F32)
 
     out_ref[...] = times(high) + (times(middle) + times(low))
 
@@ -440,10 +441,11 @@
     return pl.pallas_call(
         update_kernel,
         out_shape=jax.ShapeDtypeStruct(params.shape, F32),
-        in_specs=[vmem, vmem],
+        in_specs=[vmem, pl.BlockSpec(memory_space=pltpu.HBM)],
         out_specs=vmem,
-        scratch_shapes=[pltpu.VMEM((members, 2 * members), F32)],
-        compiler_params=pltpu.CompilerParams(vmem_limit_bytes=VMEM // 4),
+        scratch_shapes=[
+            pltpu.VMEM((members, 2 * members), F32), pltpu.VMEM(params.shape, BF), pltpu.SemaphoreType.DMA],
+        compiler_params=pltpu.CompilerParams(vmem_limit_bytes=VMEM - 5 * total.size),
         name="update",
     )(total, params)
 

time: 86.4 us -> 85.5 us (0.990)
  local copies, waits for them, and re-layouts: 0.96 us -> 0.01 us
    pallas_call x2, Pallas kernels: 37 us -> 35 us  [local_call(): pl.pallas_call(functools.partial(local_kernel, edge, columns, obs_total),...]
    pallas_call x1, Pallas kernels: 10.8 us -> 12.1 us  [update(): pl.pallas_call(update_kernel, out_shape=jax.ShapeDtypeStruct(params.shape...]
    unnamed x2 -> x0, local copies, waits for them, and re-layouts: 0.95 us -> none
  transfers between devices with their start and end apart: 2 -> 2, of which waited for: 0 -> 0; matrix products, arithmetic and copies ran while one was open for 0% -> 0% of each run, Pallas kernels for 34% -> 33%
where the time goes in v9:
time: 85.5 us; the launch traced here: 85 us
  Pallas kernels  49.4 us (58%)
  blocking collectives  29.8 us (35%)
  starting transfers between devices  4.45 us (5%)
  between operations  1.34 us (2%)
    pallas_call x2, Pallas kernels, local_call(): pl.pallas_call(functools.partial(local_kernel, edge, columns, obs_total),...  35 us
    all_to_all x1, blocking collectives, sum_over(): parts = lax.all_to_all(values, axes, 0, 0, tiled=True)  17.5 us
    all_to_all x1, blocking collectives, sum_over(): return lax.all_to_all(copies, axes, 0, 0, tiled=True)  12.3 us
    pallas_call x1, Pallas kernels, update(): pl.pallas_call(update_kernel, out_shape=jax.ShapeDtypeStruct(params.shape...  12.1 us
    ppermute x1, starting transfers between devices, body(): left = lax.ppermute(last, axes, up)  3.17 us
    pallas_call x1, Pallas kernels, halo_blocks(): pl.pallas_call(functools.partial(halo_kernel, columns), out_shape=(block,...  2.29 us
  transfers between devices with their start and end apart: 2, of which 0 were waited for; matrix products, arithmetic and copies ran while one was open for 0% of the time, Pallas kernels for 33%

profile of v9, /device:TPU:0, one launch (start us, length us, event | category | flops | bytes accessed | tf_op | source)
XLA Modules:
  0.0 85.0 jit_solution(6848269248800237981)
XLA Ops:
  0.6 2.3 %halos.1 = (bf16[272,1024]{1,0:T(8,128)(2,1)}, bf16[272,1024]{1,0:T(8,128)(2,1)}) custom-call(bf16[256,24576]{1,0:T(8,128)(2,1)} %refs_2_.3, f32[1,24576]{1,0:T(1,128)} %bitcast.5), custom_call_target="tpu_custom_call" | custom-call | tf_op jit(solution)/shard_map/halos/pallas_call | solution.py:483
  2.9 3.2 %collective-permute-start = (bf16[272,1024]{1,0:T(8,128)(2,1)}, bf16[272,1024]{1,0:T(8,128)(2,1)}, u32[]{:S(2)}, u32[]{:S(2)}) collective-permute-start(bf16[272,1024]{1,0:T(8,128)(2,1)} %get-tuple-element.8), channel_id=1, source_target_pairs={{0,1},{1,2},{2,3},{3,4},{4,5},{5,6},{6,7},{7,8},{8,9},{9,10},{10,1... | collective-permute-start | bytes 1671176 | tf_op jit(solution)/shard_map/ppermute | solution.py:512
  6.1 1.3 %collective-permute-start.1 = (bf16[272,1024]{1,0:T(8,128)(2,1)}, bf16[272,1024]{1,0:T(8,128)(2,1)}, u32[]{:S(2)}, u32[]{:S(2)}) collective-permute-start(bf16[272,1024]{1,0:T(8,128)(2,1)} %get-tuple-element.9), channel_id=1, source_target_pairs={{1,0},{2,1},{3,2},{4,3},{5,4},{6,5},{7,6},{8,7},{9,8},{10,9},{11,1... | collective-permute-start | bytes 1671176 | tf_op jit(solution)/shard_map/ppermute | solution.py:513
  8.0 28.4 %inner.1 = (f32[128,384]{1,0:T(8,128)}, f32[1,24576]{1,0:T(1,128)}) custom-call(s32[8]{0:T(128)} %refs_0_.3, s32[1]{0:T(128)S(6)} %copy.10.refs_1_, bf16[256,24576]{1,0:T(8,128)(2,1)} %refs_2_.3, f32[1,24576]{1,0:T(1,128)} %bitcast.6, f32[8,24576]{1,0:T(8,128)} %refs_4_.3), custom_call_target="tpu_custom_call" | custom-call | flops 6274678784 | bytes 12582912 | tf_op jit(solution)/shard_map/inner/pallas_call | solution.py:312
  36.5 0.0 collective-permute-done.refs_5_
  36.5 0.0 collective-permute-done.1.refs_6_
  36.5 6.6 %edges.1 = (f32[128,384]{1,0:T(8,128)}, f32[1,24576]{1,0:T(1,128)}) custom-call(s32[8]{0:T(128)} %refs_0_.3, s32[1]{0:T(128)S(6)} %copy.10.refs_1_, bf16[256,24576]{1,0:T(8,128)(2,1)} %refs_2_.3, f32[1,24576]{1,0:T(1,128)} %bitcast.7, f32[8,24576]{1,0:T(8,128)} %refs_4_.3, ...), custom_call_target="tpu_custom_call", output_to_operand_aliasing={{1}: (8, {})} | custom-call | flops 570425344 | bytes 3145728 | tf_op jit(solution)/shard_map/edges/pallas_call | solution.py:312
  43.1 17.5 %all_to_all.17 = f32[16,8,384]{2,1,0:T(8,128)S(1)} all-to-all(f32[16,8,384]{2,1,0:T(8,128)} %bitcast.8), channel_id=1, replica_groups=mesh['grp'=2,'obs'=4,'par'=4] {'obs','par'}, dimensions={0} | all-to-all | bytes 393216 | tf_op jit(solution)/shard_map/all_to_all | solution.py:497
  60.6 12.3 %all_to_all.18 = f32[16,8,384]{2,1,0:T(8,128)} all-to-all(f32[16,8,384]{2,1,0:T(8,128)S(1)} %broadcast_in_dim.10), channel_id=1, replica_groups=mesh['grp'=2,'obs'=4,'par'=4] {'obs','par'}, dimensions={0} | all-to-all | bytes 393216 | tf_op jit(solution)/shard_map/all_to_all | solution.py:500
  72.9 12.1 %update.1 = f32[512,256]{1,0:T(8,128)} custom-call(f32[128,384]{1,0:T(8,128)} %bitcast.4, bf16[512,256]{1,0:T(8,128)(2,1)} %params_ref.1), custom_call_target="tpu_custom_call" | custom-call | tf_op jit(solution)/shard_map/update/pallas_call | solution.py:441
  (2 shorter events, 0.0 us)
Async XLA Ops:
  2.9 33.5 %collective-permute-start = (bf16[272,1024]{1,0:T(8,128)(2,1)}, bf16[272,1024]{1,0:T(8,128)(2,1)}, u32[]{:S(2)}, u32[]{:S(2)}) collective-permute-start(bf16[272,1024]{1,0:T(8,128)(2,1)} %get-tuple-element.8), channel_id=1, source_target_pairs={{0,1},{1,2},{2,3},{3,4},{4,5},{5,6},{6,7},{7,8},{8,9},{9,10},{10,1... | collective-permute-start | bytes 1671176 | tf_op jit(solution)/shard_map/ppermute | solution.py:512
  6.1 30.4 %collective-permute-start.1 = (bf16[272,1024]{1,0:T(8,128)(2,1)}, bf16[272,1024]{1,0:T(8,128)(2,1)}, u32[]{:S(2)}, u32[]{:S(2)}) collective-permute-start(bf16[272,1024]{1,0:T(8,128)(2,1)} %get-tuple-element.9), channel_id=1, source_target_pairs={{1,0},{2,1},{3,2},{4,3},{5,4},{6,5},{7,6},{8,7},{9,8},{10,9},{11,1... | collective-permute-start | bytes 1671176 | tf_op jit(solution)/shard_map/ppermute | solution.py:513

commit v10 on v9

--- a/solution.py
+++ b/solution.py
@@ -162,7 +162,7 @@
         return lax.dot_general(
             block, block[:members], (((1,), (1,)), ((), ())), preferred_element_type=F32)
 
-    def whiten_chunk(place, column, at):
+    def whiten_chunk(place, column, at, meanwhile=None):
         coefficients(column, at)
         steps = plan(place)
         pending = []
@@ -196,6 +196,8 @@
                     for r, at_row in enumerate(starts) for t in range(width)])
                 if len(pending) > LATE:
                     store_oldest()
+            if group == 0 and meanwhile is not None:
+                meanwhile()
         while pending:
             store_oldest()
         for t in range(tiles):
@@ -248,9 +250,12 @@
             added = products()
             mean = mean_rows(ahead)
             column = pl.multiple_of(place * H, H)
-            whiten_chunk(place, column, column)
-            gram[...] += added
-            keep_special(ahead, mean)
+
+            def meanwhile():
+                gram[...] += added
+                keep_special(ahead, mean)
+
+            whiten_chunk(place, column, column, meanwhile)
             return carry
 
         lax.fori_loop(1, chunks - 1, chunk_step, 0)
@@ -326,10 +331,8 @@
     )(offsets, rows_count, predicted, observed, band, *more)
 
 
-def update_kernel(sum_ref, params_ref, out_ref, work, params, sem):
+def update_kernel(sum_ref, params_ref, out_ref, work):
     members = params_ref.shape[1]
-    fetch = pltpu.make_async_copy(params_ref, params, sem)
-    fetch.start()
     highest = lax.Precision.HIGHEST
     row_index = lax.broadcasted_iota(jnp.int32, (members, members), 0)
     col_index = lax.broadcasted_iota(jnp.int32, (members, members), 1)
@@ -427,10 +430,8 @@
     rest = turned - high.astype(F32)
     middle = rest.astype(BF)
     low = (rest - middle.astype(F32)).astype(BF)
-    fetch.wait()
-
     def times(part):
-        return lax.dot_general(params[...], part, (((1,), (1,)), ((), ())), preferred_element_type=F32)
+        return lax.dot_general(params_ref[...], part, (((1,), (1,)), ((), ())), preferred_element_type=F32)
 
     out_ref[...] = times(high) + (times(middle) + times(low))
 
@@ -441,11 +442,10 @@
     return pl.pallas_call(
         update_kernel,
         out_shape=jax.ShapeDtypeStruct(params.shape, F32),
-        in_specs=[vmem, pl.BlockSpec(memory_space=pltpu.HBM)],
+        in_specs=[vmem, vmem],
         out_specs=vmem,
-        scratch_shapes=[
-            pltpu.VMEM((members, 2 * members), F32), pltpu.VMEM(params.shape, BF), pltpu.SemaphoreType.DMA],
-        compiler_params=pltpu.CompilerParams(vmem_limit_bytes=VMEM - 5 * total.size),
+        scratch_shapes=[pltpu.VMEM((members, 2 * members), F32)],
+        compiler_params=pltpu.CompilerParams(vmem_limit_bytes=VMEM // 4),
         name="update",
     )(total, params)
 

time: 85.5 us -> 84.2 us (0.985)
  Pallas kernels: 49.4 us -> 47.9 us
  local copies, waits for them, and re-layouts: 0.01 us -> 0.96 us
    pallas_call x1, Pallas kernels: 12.1 us -> 10.7 us  [update(): pl.pallas_call(update_kernel, out_shape=jax.ShapeDtypeStruct(params.shape...]
    unnamed x0 -> x2, local copies, waits for them, and re-layouts: none -> 0.95 us
  transfers between devices with their start and end apart: 2 -> 2, of which waited for: 0 -> 0; matrix products, arithmetic and copies ran while one was open for 0% -> 0% of each run, Pallas kernels for 33% -> 34%
where the time goes in v10:
time: 84.2 us; the launch traced here: 83.8 us
  Pallas kernels  47.9 us (57%)
  blocking collectives  29.1 us (35%)
  starting transfers between devices  4.44 us (5%)
  between operations  1.34 us (2%)
  local copies, waits for them, and re-layouts  0.96 us (1%)
    pallas_call x2, Pallas kernels, local_call(): pl.pallas_call(functools.partial(local_kernel, edge, columns, obs_total),...  35 us
    all_to_all x1, blocking collectives, sum_over(): parts = lax.all_to_all(values, axes, 0, 0, tiled=True)  17.5 us
    all_to_all x1, blocking collectives, sum_over(): return lax.all_to_all(copies, axes, 0, 0, tiled=True)  11.6 us
    pallas_call x1, Pallas kernels, update(): pl.pallas_call(update_kernel, out_shape=jax.ShapeDtypeStruct(params.shape...  10.7 us
    ppermute x1, starting transfers between devices, body(): left = lax.ppermute(last, axes, up)  3.16 us
    pallas_call x1, Pallas kernels, halo_blocks(): pl.pallas_call(functools.partial(halo_kernel, columns), out_shape=(block,...  2.29 us
  transfers between devices with their start and end apart: 2, of which 0 were waited for; matrix products, arithmetic and copies ran while one was open for 0% of the time, Pallas kernels for 34%

profile of v10, /device:TPU:0, one launch (start us, length us, event | category | flops | bytes accessed | tf_op | source)
XLA Modules:
  0.0 83.8 jit_solution(9182947453499779220)
XLA Ops:
  0.6 2.3 %halos.1 = (bf16[272,1024]{1,0:T(8,128)(2,1)}, bf16[272,1024]{1,0:T(8,128)(2,1)}) custom-call(bf16[256,24576]{1,0:T(8,128)(2,1)} %refs_2_.3, f32[1,24576]{1,0:T(1,128)} %bitcast.5), custom_call_target="tpu_custom_call" | custom-call | tf_op jit(solution)/shard_map/halos/pallas_call | solution.py:483
  2.9 3.2 %collective-permute-start = (bf16[272,1024]{1,0:T(8,128)(2,1)}, bf16[272,1024]{1,0:T(8,128)(2,1)}, u32[]{:S(2)}, u32[]{:S(2)}) collective-permute-start(bf16[272,1024]{1,0:T(8,128)(2,1)} %get-tuple-element.8), channel_id=1, source_target_pairs={{0,1},{1,2},{2,3},{3,4},{4,5},{5,6},{6,7},{7,8},{8,9},{9,10},{10,1... | collective-permute-start | bytes 1671176 | tf_op jit(solution)/shard_map/ppermute | solution.py:512
  6.1 1.3 %collective-permute-start.1 = (bf16[272,1024]{1,0:T(8,128)(2,1)}, bf16[272,1024]{1,0:T(8,128)(2,1)}, u32[]{:S(2)}, u32[]{:S(2)}) collective-permute-start(bf16[272,1024]{1,0:T(8,128)(2,1)} %get-tuple-element.9), channel_id=1, source_target_pairs={{1,0},{2,1},{3,2},{4,3},{5,4},{6,5},{7,6},{8,7},{9,8},{10,9},{11,1... | collective-permute-start | bytes 1671176 | tf_op jit(solution)/shard_map/ppermute | solution.py:513
  8.0 28.4 %inner.1 = (f32[128,384]{1,0:T(8,128)}, f32[1,24576]{1,0:T(1,128)}) custom-call(s32[8]{0:T(128)} %refs_0_.3, s32[1]{0:T(128)S(6)} %copy.10.refs_1_, bf16[256,24576]{1,0:T(8,128)(2,1)} %refs_2_.3, f32[1,24576]{1,0:T(1,128)} %bitcast.6, f32[8,24576]{1,0:T(8,128)} %refs_4_.3), custom_call_target="tpu_custom_call" | custom-call | flops 6274678784 | bytes 12582912 | tf_op jit(solution)/shard_map/inner/pallas_call | solution.py:317
  36.5 0.0 collective-permute-done.refs_5_
  36.5 0.0 collective-permute-done.1.refs_6_
  36.5 6.6 %edges.1 = (f32[128,384]{1,0:T(8,128)}, f32[1,24576]{1,0:T(1,128)}) custom-call(s32[8]{0:T(128)} %refs_0_.3, s32[1]{0:T(128)S(6)} %copy.10.refs_1_, bf16[256,24576]{1,0:T(8,128)(2,1)} %refs_2_.3, f32[1,24576]{1,0:T(1,128)} %bitcast.7, f32[8,24576]{1,0:T(8,128)} %refs_4_.3, ...), custom_call_target="tpu_custom_call", output_to_operand_aliasing={{1}: (8, {})} | custom-call | flops 570425344 | bytes 3145728 | tf_op jit(solution)/shard_map/edges/pallas_call | solution.py:317
  43.0 17.5 %all_to_all.17 = f32[16,8,384]{2,1,0:T(8,128)S(1)} all-to-all(f32[16,8,384]{2,1,0:T(8,128)} %bitcast.8), channel_id=1, replica_groups=mesh['grp'=2,'obs'=4,'par'=4] {'obs','par'}, dimensions={0} | all-to-all | bytes 393216 | tf_op jit(solution)/shard_map/all_to_all | solution.py:497
  60.6 11.6 %all_to_all.18 = f32[16,8,384]{2,1,0:T(8,128)S(1)} all-to-all(f32[16,8,384]{2,1,0:T(8,128)S(1)} %broadcast_in_dim.10), channel_id=1, replica_groups=mesh['grp'=2,'obs'=4,'par'=4] {'obs','par'}, dimensions={0} | all-to-all | bytes 393216 | tf_op jit(solution)/shard_map/all_to_all | solution.py:500
  72.2 0.0 copy-start
  72.2 0.9 %copy-done = bf16[512,256]{1,0:T(8,128)(2,1)S(1)} copy-done((bf16[512,256]{1,0:T(8,128)(2,1)S(1)}, bf16[512,256]{1,0:T(8,128)(2,1)}, u32[]{:S(2)}) %copy-start) | copy-done | bytes 262168
  73.1 10.7 %update.1 = f32[512,256]{1,0:T(8,128)} custom-call(f32[128,384]{1,0:T(8,128)S(1)} %bitcast.4, bf16[512,256]{1,0:T(8,128)(2,1)S(1)} %copy-done), custom_call_target="tpu_custom_call" | custom-call | tf_op jit(solution)/shard_map/update/pallas_call | solution.py:442
  (2 shorter events, 0.0 us)
Async XLA Ops:
  2.9 33.5 %collective-permute-start = (bf16[272,1024]{1,0:T(8,128)(2,1)}, bf16[272,1024]{1,0:T(8,128)(2,1)}, u32[]{:S(2)}, u32[]{:S(2)}) collective-permute-start(bf16[272,1024]{1,0:T(8,128)(2,1)} %get-tuple-element.8), channel_id=1, source_target_pairs={{0,1},{1,2},{2,3},{3,4},{4,5},{5,6},{6,7},{7,8},{8,9},{9,10},{10,1... | collective-permute-start | bytes 1671176 | tf_op jit(solution)/shard_map/ppermute | solution.py:512
  6.1 30.4 %collective-permute-start.1 = (bf16[272,1024]{1,0:T(8,128)(2,1)}, bf16[272,1024]{1,0:T(8,128)(2,1)}, u32[]{:S(2)}, u32[]{:S(2)}) collective-permute-start(bf16[272,1024]{1,0:T(8,128)(2,1)} %get-tuple-element.9), channel_id=1, source_target_pairs={{1,0},{2,1},{3,2},{4,3},{5,4},{6,5},{7,6},{8,7},{9,8},{10,9},{11,1... | collective-permute-start | bytes 1671176 | tf_op jit(solution)/shard_map/ppermute | solution.py:513
  72.2 1.0 %copy-start = (bf16[512,256]{1,0:T(8,128)(2,1)S(1)}, bf16[512,256]{1,0:T(8,128)(2,1)}, u32[]{:S(2)}) copy-start(bf16[512,256]{1,0:T(8,128)(2,1)} %params_ref.1) | copy-start | bytes 786436

commit v11 on v10

--- a/solution.py
+++ b/solution.py
@@ -12,8 +12,8 @@
 LANE = 128
 SUB = 8
 PACK = 16
-TALL = 4
-LATE = 1
+TALL = 2
+LATE = 2
 AHEAD = 5
 BLOCK = 64
 PANEL = 8
@@ -24,9 +24,9 @@
 
 def local_kernel(edge, columns, obs_total, *refs):
     if edge:
-        (off_ref, count_ref, pred_ref, obs_ref, band_ref, left_ref, right_ref, gram_in, misfit_in,
+        (off_ref, count_ref, pred_ref, obs_ref, band_ref, left_ref, right_ref, gram_before, misfit_in,
          gram_out, misfit_out, raw, special, aw, coef, mean_white, gram, obs, band, row_out, slots,
-         sems) = refs
+         sems, gram_in) = refs
     else:
         (off_ref, count_ref, pred_ref, obs_ref, band_ref,
          gram_out, misfit_out, raw, special, aw, coef, mean_white, gram, obs, band, row_out, slots,
@@ -65,6 +65,8 @@
     for copy in copies:
         copy.start()
     if edge:
+        gram_copy = pltpu.make_async_copy(gram_before, gram_in, sems.at[10])
+        gram_copy.start()
         tile_copies(left_ref, 0, 0, members + PACK)
         for place, chunk in ((1, 0), (2, 1), (3, chunks - 2), (4, chunks - 1)):
             tile_copies(pred_ref, chunk * H, place, members)
@@ -265,6 +267,8 @@
         copy.start()
     gram[...] += products()
 
+    if edge:
+        gram_copy.wait()
     tail = gram[pl.ds(members, 8), :]
     total = tail[0:1] + tail[1:2] + tail[2:3]
     both = gram[pl.ds(0, members), :]
@@ -299,7 +303,7 @@
     far = pl.BlockSpec(memory_space=pltpu.HBM)
     in_specs = [smem, smem, far, far, far]
     if edge:
-        in_specs += [far, far, vmem, far]
+        in_specs += [far, far, far, far]
     scratch = [
         pltpu.VMEM((tiles, rows if edge else members, LANE), BF),
         pltpu.VMEM((tiles, SUB, LANE), F32),
@@ -311,8 +315,10 @@
         pltpu.VMEM((terms, 2 * H if edge else columns), F32),
         pltpu.VMEM((1, 2 * H if edge else columns), F32),
         pltpu.SMEM((8, 2), jnp.int32),
-        pltpu.SemaphoreType.DMA((places + 4,)),
+        pltpu.SemaphoreType.DMA((places + 5,)),
     ]
+    if edge:
+        scratch.append(pltpu.VMEM((members // 2, members // 2 * 3), F32))
     work = 2 if edge else places - 2
     return pl.pallas_call(
         functools.partial(local_kernel, edge, columns, obs_total),
@@ -359,6 +365,12 @@
     sub = lax.broadcasted_iota(jnp.int32, (PANEL, LANE), 0)
     eye = identity[:BLOCK, :BLOCK]
 
+    def reciprocal(value):
+        guess = pl.reciprocal(value, approx=True)
+        for _ in range(2):
+            guess = guess * (2.0 - value * guess)
+        return guess
+
     def across(tile, column):
         return jnp.broadcast_to(tile[:, column:column + 1], (PANEL, LANE))
 
@@ -381,8 +393,8 @@
                 left, right = cols[k], cols[k + 1]
                 a, b, c = down(left, k), down(left, k + 1), down(right, k + 1)
                 det = a * c - b * b
-                inverse = 1.0 / det
-                ratio = b / a
+                inverse = reciprocal(det)
+                ratio = b * reciprocal(a)
                 scale = jnp.where(sub == k, a, jnp.where(sub == k + 1, c - b * ratio, scale))
                 from_left = c * left - b * right
                 from_right = a * right - b * left

time: 84.2 us -> 85.4 us (1.014)
  Pallas kernels: 47.9 us -> 49.1 us
    pallas_call x1, Pallas kernels: 10.7 us -> 12.2 us  [update(): pl.pallas_call(update_kernel, out_shape=jax.ShapeDtypeStruct(params.shape...]
  transfers between devices with their start and end apart: 2 -> 2, of which waited for: 0 -> 0; matrix products, arithmetic and copies ran while one was open for 0% -> 0% of each run, Pallas kernels for 34% -> 33%
where the time goes in v11:
time: 85.4 us; the launch traced here: 85 us
  Pallas kernels  49.1 us (57%)
  blocking collectives  29.1 us (34%)
  starting transfers between devices  4.44 us (5%)
  between operations  1.34 us (2%)
  local copies, waits for them, and re-layouts  0.96 us (1%)
    pallas_call x2, Pallas kernels, local_call(): pl.pallas_call(functools.partial(local_kernel, edge, columns, obs_total),...  34.6 us
    all_to_all x1, blocking collectives, sum_over(): parts = lax.all_to_all(values, axes, 0, 0, tiled=True)  17.5 us
    pallas_call x1, Pallas kernels, update(): pl.pallas_call(update_kernel, out_shape=jax.ShapeDtypeStruct(params.shape...  12.2 us
    all_to_all x1, blocking collectives, sum_over(): return lax.all_to_all(copies, axes, 0, 0, tiled=True)  11.6 us
    ppermute x1, starting transfers between devices, body(): left = lax.ppermute(last, axes, up)  3.16 us
    pallas_call x1, Pallas kernels, halo_blocks(): pl.pallas_call(functools.partial(halo_kernel, columns), out_shape=(block,...  2.29 us
  transfers between devices with their start and end apart: 2, of which 0 were waited for; matrix products, arithmetic and copies ran while one was open for 0% of the time, Pallas kernels for 33%

profile of v11, /device:TPU:0, one launch (start us, length us, event | category | flops | bytes accessed | tf_op | source)
XLA Modules:
  0.0 85.0 jit_solution(14505005931926831994)
XLA Ops:
  0.6 2.3 %halos.1 = (bf16[272,1024]{1,0:T(8,128)(2,1)}, bf16[272,1024]{1,0:T(8,128)(2,1)}) custom-call(bf16[256,24576]{1,0:T(8,128)(2,1)} %refs_2_.3, f32[1,24576]{1,0:T(1,128)} %bitcast.5), custom_call_target="tpu_custom_call" | custom-call | tf_op jit(solution)/shard_map/halos/pallas_call | solution.py:495
  2.9 3.2 %collective-permute-start = (bf16[272,1024]{1,0:T(8,128)(2,1)}, bf16[272,1024]{1,0:T(8,128)(2,1)}, u32[]{:S(2)}, u32[]{:S(2)}) collective-permute-start(bf16[272,1024]{1,0:T(8,128)(2,1)} %get-tuple-element.8), channel_id=1, source_target_pairs={{0,1},{1,2},{2,3},{3,4},{4,5},{5,6},{6,7},{7,8},{8,9},{9,10},{10,1... | collective-permute-start | bytes 1671176 | tf_op jit(solution)/shard_map/ppermute | solution.py:524
  6.1 1.3 %collective-permute-start.1 = (bf16[272,1024]{1,0:T(8,128)(2,1)}, bf16[272,1024]{1,0:T(8,128)(2,1)}, u32[]{:S(2)}, u32[]{:S(2)}) collective-permute-start(bf16[272,1024]{1,0:T(8,128)(2,1)} %get-tuple-element.9), channel_id=1, source_target_pairs={{1,0},{2,1},{3,2},{4,3},{5,4},{6,5},{7,6},{8,7},{9,8},{10,9},{11,1... | collective-permute-start | bytes 1671176 | tf_op jit(solution)/shard_map/ppermute | solution.py:525
  8.0 28.3 %inner.1 = (f32[128,384]{1,0:T(8,128)}, f32[1,24576]{1,0:T(1,128)}) custom-call(s32[8]{0:T(128)} %refs_0_.3, s32[1]{0:T(128)S(6)} %copy.10.refs_1_, bf16[256,24576]{1,0:T(8,128)(2,1)} %refs_2_.3, f32[1,24576]{1,0:T(1,128)} %bitcast.6, f32[8,24576]{1,0:T(8,128)} %refs_4_.3), custom_call_target="tpu_custom_call" | custom-call | flops 6274678784 | bytes 12582912 | tf_op jit(solution)/shard_map/inner/pallas_call | solution.py:323
  36.3 0.0 collective-permute-done.refs_5_
  36.3 0.0 collective-permute-done.1.refs_6_
  36.3 6.3 %edges.1 = (f32[128,384]{1,0:T(8,128)}, f32[1,24576]{1,0:T(1,128)}) custom-call(s32[8]{0:T(128)} %refs_0_.3, s32[1]{0:T(128)S(6)} %copy.10.refs_1_, bf16[256,24576]{1,0:T(8,128)(2,1)} %refs_2_.3, f32[1,24576]{1,0:T(1,128)} %bitcast.7, f32[8,24576]{1,0:T(8,128)} %refs_4_.3, ...), custom_call_target="tpu_custom_call", output_to_operand_aliasing={{1}: (8, {})} | custom-call | flops 570425344 | bytes 3145728 | tf_op jit(solution)/shard_map/edges/pallas_call | solution.py:323
  42.7 17.5 %all_to_all.17 = f32[16,8,384]{2,1,0:T(8,128)S(1)} all-to-all(f32[16,8,384]{2,1,0:T(8,128)} %bitcast.8), channel_id=1, replica_groups=mesh['grp'=2,'obs'=4,'par'=4] {'obs','par'}, dimensions={0} | all-to-all | bytes 393216 | tf_op jit(solution)/shard_map/all_to_all | solution.py:509
  60.2 11.6 %all_to_all.18 = f32[16,8,384]{2,1,0:T(8,128)S(1)} all-to-all(f32[16,8,384]{2,1,0:T(8,128)S(1)} %broadcast_in_dim.10), channel_id=1, replica_groups=mesh['grp'=2,'obs'=4,'par'=4] {'obs','par'}, dimensions={0} | all-to-all | bytes 393216 | tf_op jit(solution)/shard_map/all_to_all | solution.py:512
  71.8 0.0 copy-start
  71.8 0.9 %copy-done = bf16[512,256]{1,0:T(8,128)(2,1)S(1)} copy-done((bf16[512,256]{1,0:T(8,128)(2,1)S(1)}, bf16[512,256]{1,0:T(8,128)(2,1)}, u32[]{:S(2)}) %copy-start) | copy-done | bytes 262168
  72.8 12.2 %update.1 = f32[512,256]{1,0:T(8,128)} custom-call(f32[128,384]{1,0:T(8,128)S(1)} %bitcast.4, bf16[512,256]{1,0:T(8,128)(2,1)S(1)} %copy-done), custom_call_target="tpu_custom_call" | custom-call | tf_op jit(solution)/shard_map/update/pallas_call | solution.py:454
  (2 shorter events, 0.0 us)
Async XLA Ops:
  2.9 33.4 %collective-permute-start = (bf16[272,1024]{1,0:T(8,128)(2,1)}, bf16[272,1024]{1,0:T(8,128)(2,1)}, u32[]{:S(2)}, u32[]{:S(2)}) collective-permute-start(bf16[272,1024]{1,0:T(8,128)(2,1)} %get-tuple-element.8), channel_id=1, source_target_pairs={{0,1},{1,2},{2,3},{3,4},{4,5},{5,6},{6,7},{7,8},{8,9},{9,10},{10,1... | collective-permute-start | bytes 1671176 | tf_op jit(solution)/shard_map/ppermute | solution.py:524
  6.1 30.2 %collective-permute-start.1 = (bf16[272,1024]{1,0:T(8,128)(2,1)}, bf16[272,1024]{1,0:T(8,128)(2,1)}, u32[]{:S(2)}, u32[]{:S(2)}) collective-permute-start(bf16[272,1024]{1,0:T(8,128)(2,1)} %get-tuple-element.9), channel_id=1, source_target_pairs={{1,0},{2,1},{3,2},{4,3},{5,4},{6,5},{7,6},{8,7},{9,8},{10,9},{11,1... | collective-permute-start | bytes 1671176 | tf_op jit(solution)/shard_map/ppermute | solution.py:525
  71.8 1.0 %copy-start = (bf16[512,256]{1,0:T(8,128)(2,1)S(1)}, bf16[512,256]{1,0:T(8,128)(2,1)}, u32[]{:S(2)}) copy-start(bf16[512,256]{1,0:T(8,128)(2,1)} %params_ref.1) | copy-start | bytes 786436

commit v12 on v11

--- a/solution.py
+++ b/solution.py
@@ -365,12 +365,6 @@
     sub = lax.broadcasted_iota(jnp.int32, (PANEL, LANE), 0)
     eye = identity[:BLOCK, :BLOCK]
 
-    def reciprocal(value):
-        guess = pl.reciprocal(value, approx=True)
-        for _ in range(2):
-            guess = guess * (2.0 - value * guess)
-        return guess
-
     def across(tile, column):
         return jnp.broadcast_to(tile[:, column:column + 1], (PANEL, LANE))
 
@@ -393,8 +387,8 @@
                 left, right = cols[k], cols[k + 1]
                 a, b, c = down(left, k), down(left, k + 1), down(right, k + 1)
                 det = a * c - b * b
-                inverse = reciprocal(det)
-                ratio = b * reciprocal(a)
+                inverse = 1.0 / det
+                ratio = b / a
                 scale = jnp.where(sub == k, a, jnp.where(sub == k + 1, c - b * ratio, scale))
                 from_left = c * left - b * right
                 from_right = a * right - b * left

time: 85.4 us -> 83.9 us (0.982)
  Pallas kernels: 49.1 us -> 47.7 us
    pallas_call x1, Pallas kernels: 12.2 us -> 10.7 us  [update(): pl.pallas_call(update_kernel, out_shape=jax.ShapeDtypeStruct(params.shape...]
  transfers between devices with their start and end apart: 2 -> 2, of which waited for: 0 -> 0; matrix products, arithmetic and copies ran while one was open for 0% -> 0% of each run, Pallas kernels for 33% -> 34%
where the time goes in v12:
time: 83.9 us; the launch traced here: 83.5 us
  Pallas kernels  47.7 us (57%)
  blocking collectives  29.1 us (35%)
  starting transfers between devices  4.44 us (5%)
  between operations  1.34 us (2%)
  local copies, waits for them, and re-layouts  0.96 us (1%)
    pallas_call x2, Pallas kernels, local_call(): pl.pallas_call(functools.partial(local_kernel, edge, columns, obs_total),...  34.7 us
    all_to_all x1, blocking collectives, sum_over(): parts = lax.all_to_all(values, axes, 0, 0, tiled=True)  17.5 us
    all_to_all x1, blocking collectives, sum_over(): return lax.all_to_all(copies, axes, 0, 0, tiled=True)  11.6 us
    pallas_call x1, Pallas kernels, update(): pl.pallas_call(update_kernel, out_shape=jax.ShapeDtypeStruct(params.shape...  10.7 us
    ppermute x1, starting transfers between devices, body(): left = lax.ppermute(last, axes, up)  3.16 us
    pallas_call x1, Pallas kernels, halo_blocks(): pl.pallas_call(functools.partial(halo_kernel, columns), out_shape=(block,...  2.29 us
  transfers between devices with their start and end apart: 2, of which 0 were waited for; matrix products, arithmetic and copies ran while one was open for 0% of the time, Pallas kernels for 34%

profile of v12, /device:TPU:0, one launch (start us, length us, event | category | flops | bytes accessed | tf_op | source)
XLA Modules:
  0.0 83.5 jit_solution(7348351131198569953)
XLA Ops:
  0.6 2.3 %halos.1 = (bf16[272,1024]{1,0:T(8,128)(2,1)}, bf16[272,1024]{1,0:T(8,128)(2,1)}) custom-call(bf16[256,24576]{1,0:T(8,128)(2,1)} %refs_2_.3, f32[1,24576]{1,0:T(1,128)} %bitcast.5), custom_call_target="tpu_custom_call" | custom-call | tf_op jit(solution)/shard_map/halos/pallas_call | solution.py:489
  2.9 3.2 %collective-permute-start = (bf16[272,1024]{1,0:T(8,128)(2,1)}, bf16[272,1024]{1,0:T(8,128)(2,1)}, u32[]{:S(2)}, u32[]{:S(2)}) collective-permute-start(bf16[272,1024]{1,0:T(8,128)(2,1)} %get-tuple-element.8), channel_id=1, source_target_pairs={{0,1},{1,2},{2,3},{3,4},{4,5},{5,6},{6,7},{7,8},{8,9},{9,10},{10,1... | collective-permute-start | bytes 1671176 | tf_op jit(solution)/shard_map/ppermute | solution.py:518
  6.1 1.3 %collective-permute-start.1 = (bf16[272,1024]{1,0:T(8,128)(2,1)}, bf16[272,1024]{1,0:T(8,128)(2,1)}, u32[]{:S(2)}, u32[]{:S(2)}) collective-permute-start(bf16[272,1024]{1,0:T(8,128)(2,1)} %get-tuple-element.9), channel_id=1, source_target_pairs={{1,0},{2,1},{3,2},{4,3},{5,4},{6,5},{7,6},{8,7},{9,8},{10,9},{11,1... | collective-permute-start | bytes 1671176 | tf_op jit(solution)/shard_map/ppermute | solution.py:519
  8.0 28.3 %inner.1 = (f32[128,384]{1,0:T(8,128)}, f32[1,24576]{1,0:T(1,128)}) custom-call(s32[8]{0:T(128)} %refs_0_.3, s32[1]{0:T(128)S(6)} %copy.10.refs_1_, bf16[256,24576]{1,0:T(8,128)(2,1)} %refs_2_.3, f32[1,24576]{1,0:T(1,128)} %bitcast.6, f32[8,24576]{1,0:T(8,128)} %refs_4_.3), custom_call_target="tpu_custom_call" | custom-call | flops 6274678784 | bytes 12582912 | tf_op jit(solution)/shard_map/inner/pallas_call | solution.py:323
  36.3 0.0 collective-permute-done.refs_5_
  36.3 0.0 collective-permute-done.1.refs_6_
  36.3 6.4 %edges.1 = (f32[128,384]{1,0:T(8,128)}, f32[1,24576]{1,0:T(1,128)}) custom-call(s32[8]{0:T(128)} %refs_0_.3, s32[1]{0:T(128)S(6)} %copy.10.refs_1_, bf16[256,24576]{1,0:T(8,128)(2,1)} %refs_2_.3, f32[1,24576]{1,0:T(1,128)} %bitcast.7, f32[8,24576]{1,0:T(8,128)} %refs_4_.3, ...), custom_call_target="tpu_custom_call", output_to_operand_aliasing={{1}: (8, {})} | custom-call | flops 570425344 | bytes 3145728 | tf_op jit(solution)/shard_map/edges/pallas_call | solution.py:323
  42.8 17.5 %all_to_all.17 = f32[16,8,384]{2,1,0:T(8,128)S(1)} all-to-all(f32[16,8,384]{2,1,0:T(8,128)} %bitcast.8), channel_id=1, replica_groups=mesh['grp'=2,'obs'=4,'par'=4] {'obs','par'}, dimensions={0} | all-to-all | bytes 393216 | tf_op jit(solution)/shard_map/all_to_all | solution.py:503
  60.3 11.6 %all_to_all.18 = f32[16,8,384]{2,1,0:T(8,128)S(1)} all-to-all(f32[16,8,384]{2,1,0:T(8,128)S(1)} %broadcast_in_dim.10), channel_id=1, replica_groups=mesh['grp'=2,'obs'=4,'par'=4] {'obs','par'}, dimensions={0} | all-to-all | bytes 393216 | tf_op jit(solution)/shard_map/all_to_all | solution.py:506
  71.9 0.0 copy-start
  71.9 0.9 %copy-done = bf16[512,256]{1,0:T(8,128)(2,1)S(1)} copy-done((bf16[512,256]{1,0:T(8,128)(2,1)S(1)}, bf16[512,256]{1,0:T(8,128)(2,1)}, u32[]{:S(2)}) %copy-start) | copy-done | bytes 262168
  72.9 10.7 %update.1 = f32[512,256]{1,0:T(8,128)} custom-call(f32[128,384]{1,0:T(8,128)S(1)} %bitcast.4, bf16[512,256]{1,0:T(8,128)(2,1)S(1)} %copy-done), custom_call_target="tpu_custom_call" | custom-call | tf_op jit(solution)/shard_map/update/pallas_call | solution.py:448
  (2 shorter events, 0.0 us)
Async XLA Ops:
  2.9 33.4 %collective-permute-start = (bf16[272,1024]{1,0:T(8,128)(2,1)}, bf16[272,1024]{1,0:T(8,128)(2,1)}, u32[]{:S(2)}, u32[]{:S(2)}) collective-permute-start(bf16[272,1024]{1,0:T(8,128)(2,1)} %get-tuple-element.8), channel_id=1, source_target_pairs={{0,1},{1,2},{2,3},{3,4},{4,5},{5,6},{6,7},{7,8},{8,9},{9,10},{10,1... | collective-permute-start | bytes 1671176 | tf_op jit(solution)/shard_map/ppermute | solution.py:518
  6.1 30.2 %collective-permute-start.1 = (bf16[272,1024]{1,0:T(8,128)(2,1)}, bf16[272,1024]{1,0:T(8,128)(2,1)}, u32[]{:S(2)}, u32[]{:S(2)}) collective-permute-start(bf16[272,1024]{1,0:T(8,128)(2,1)} %get-tuple-element.9), channel_id=1, source_target_pairs={{1,0},{2,1},{3,2},{4,3},{5,4},{6,5},{7,6},{8,7},{9,8},{10,9},{11,1... | collective-permute-start | bytes 1671176 | tf_op jit(solution)/shard_map/ppermute | solution.py:519
  71.9 1.0 %copy-start = (bf16[512,256]{1,0:T(8,128)(2,1)S(1)}, bf16[512,256]{1,0:T(8,128)(2,1)}, u32[]{:S(2)}) copy-start(bf16[512,256]{1,0:T(8,128)(2,1)} %params_ref.1) | copy-start | bytes 786436

commit v13 on v12

--- a/solution.py
+++ b/solution.py
@@ -13,7 +13,7 @@
 SUB = 8
 PACK = 16
 TALL = 2
-LATE = 2
+LATE = 3
 AHEAD = 5
 BLOCK = 64
 PANEL = 8

time: 83.9 us -> 83.8 us (level)
  no operation moved by 1% of the time
where the time goes in v13:
time: 83.8 us; the launch traced here: 83.4 us
  Pallas kernels  47.6 us (57%)
  blocking collectives  29.1 us (35%)
  starting transfers between devices  4.44 us (5%)
  between operations  1.34 us (2%)
  local copies, waits for them, and re-layouts  0.96 us (1%)
    pallas_call x2, Pallas kernels, local_call(): pl.pallas_call(functools.partial(local_kernel, edge, columns, obs_total),...  34.6 us
    all_to_all x1, blocking collectives, sum_over(): parts = lax.all_to_all(values, axes, 0, 0, tiled=True)  17.5 us
    all_to_all x1, blocking collectives, sum_over(): return lax.all_to_all(copies, axes, 0, 0, tiled=True)  11.6 us
    pallas_call x1, Pallas kernels, update(): pl.pallas_call(update_kernel, out_shape=jax.ShapeDtypeStruct(params.shape...  10.7 us
    ppermute x1, starting transfers between devices, body(): left = lax.ppermute(last, axes, up)  3.16 us
    pallas_call x1, Pallas kernels, halo_blocks(): pl.pallas_call(functools.partial(halo_kernel, columns), out_shape=(block,...  2.29 us
  transfers between devices with their start and end apart: 2, of which 0 were waited for; matrix products, arithmetic and copies ran while one was open for 0% of the time, Pallas kernels for 34%

profile of v13, /device:TPU:0, one launch (start us, length us, event | category | flops | bytes accessed | tf_op | source)
XLA Modules:
  0.0 83.4 jit_solution(18439433462360103535)
XLA Ops:
  0.6 2.3 %halos.1 = (bf16[272,1024]{1,0:T(8,128)(2,1)}, bf16[272,1024]{1,0:T(8,128)(2,1)}) custom-call(bf16[256,24576]{1,0:T(8,128)(2,1)} %refs_2_.3, f32[1,24576]{1,0:T(1,128)} %bitcast.5), custom_call_target="tpu_custom_call" | custom-call | tf_op jit(solution)/shard_map/halos/pallas_call | solution.py:489
  2.9 3.2 %collective-permute-start = (bf16[272,1024]{1,0:T(8,128)(2,1)}, bf16[272,1024]{1,0:T(8,128)(2,1)}, u32[]{:S(2)}, u32[]{:S(2)}) collective-permute-start(bf16[272,1024]{1,0:T(8,128)(2,1)} %get-tuple-element.8), channel_id=1, source_target_pairs={{0,1},{1,2},{2,3},{3,4},{4,5},{5,6},{6,7},{7,8},{8,9},{9,10},{10,1... | collective-permute-start | bytes 1671176 | tf_op jit(solution)/shard_map/ppermute | solution.py:518
  6.1 1.3 %collective-permute-start.1 = (bf16[272,1024]{1,0:T(8,128)(2,1)}, bf16[272,1024]{1,0:T(8,128)(2,1)}, u32[]{:S(2)}, u32[]{:S(2)}) collective-permute-start(bf16[272,1024]{1,0:T(8,128)(2,1)} %get-tuple-element.9), channel_id=1, source_target_pairs={{1,0},{2,1},{3,2},{4,3},{5,4},{6,5},{7,6},{8,7},{9,8},{10,9},{11,1... | collective-permute-start | bytes 1671176 | tf_op jit(solution)/shard_map/ppermute | solution.py:519
  8.0 28.3 %inner.1 = (f32[128,384]{1,0:T(8,128)}, f32[1,24576]{1,0:T(1,128)}) custom-call(s32[8]{0:T(128)} %refs_0_.3, s32[1]{0:T(128)S(6)} %copy.10.refs_1_, bf16[256,24576]{1,0:T(8,128)(2,1)} %refs_2_.3, f32[1,24576]{1,0:T(1,128)} %bitcast.6, f32[8,24576]{1,0:T(8,128)} %refs_4_.3), custom_call_target="tpu_custom_call" | custom-call | flops 6274678784 | bytes 12582912 | tf_op jit(solution)/shard_map/inner/pallas_call | solution.py:323
  36.3 0.0 collective-permute-done.refs_5_
  36.3 0.0 collective-permute-done.1.refs_6_
  36.3 6.3 %edges.1 = (f32[128,384]{1,0:T(8,128)}, f32[1,24576]{1,0:T(1,128)}) custom-call(s32[8]{0:T(128)} %refs_0_.3, s32[1]{0:T(128)S(6)} %copy.10.refs_1_, bf16[256,24576]{1,0:T(8,128)(2,1)} %refs_2_.3, f32[1,24576]{1,0:T(1,128)} %bitcast.7, f32[8,24576]{1,0:T(8,128)} %refs_4_.3, ...), custom_call_target="tpu_custom_call", output_to_operand_aliasing={{1}: (8, {})} | custom-call | flops 570425344 | bytes 3145728 | tf_op jit(solution)/shard_map/edges/pallas_call | solution.py:323
  42.7 17.5 %all_to_all.17 = f32[16,8,384]{2,1,0:T(8,128)S(1)} all-to-all(f32[16,8,384]{2,1,0:T(8,128)} %bitcast.8), channel_id=1, replica_groups=mesh['grp'=2,'obs'=4,'par'=4] {'obs','par'}, dimensions={0} | all-to-all | bytes 393216 | tf_op jit(solution)/shard_map/all_to_all | solution.py:503
  60.2 11.6 %all_to_all.18 = f32[16,8,384]{2,1,0:T(8,128)S(1)} all-to-all(f32[16,8,384]{2,1,0:T(8,128)S(1)} %broadcast_in_dim.10), channel_id=1, replica_groups=mesh['grp'=2,'obs'=4,'par'=4] {'obs','par'}, dimensions={0} | all-to-all | bytes 393216 | tf_op jit(solution)/shard_map/all_to_all | solution.py:506
  71.8 0.0 copy-start
  71.8 0.9 %copy-done = bf16[512,256]{1,0:T(8,128)(2,1)S(1)} copy-done((bf16[512,256]{1,0:T(8,128)(2,1)S(1)}, bf16[512,256]{1,0:T(8,128)(2,1)}, u32[]{:S(2)}) %copy-start) | copy-done | bytes 262168
  72.8 10.7 %update.1 = f32[512,256]{1,0:T(8,128)} custom-call(f32[128,384]{1,0:T(8,128)S(1)} %bitcast.4, bf16[512,256]{1,0:T(8,128)(2,1)S(1)} %copy-done), custom_call_target="tpu_custom_call" | custom-call | tf_op jit(solution)/shard_map/update/pallas_call | solution.py:448
  (2 shorter events, 0.0 us)
Async XLA Ops:
  2.9 33.4 %collective-permute-start = (bf16[272,1024]{1,0:T(8,128)(2,1)}, bf16[272,1024]{1,0:T(8,128)(2,1)}, u32[]{:S(2)}, u32[]{:S(2)}) collective-permute-start(bf16[272,1024]{1,0:T(8,128)(2,1)} %get-tuple-element.8), channel_id=1, source_target_pairs={{0,1},{1,2},{2,3},{3,4},{4,5},{5,6},{6,7},{7,8},{8,9},{9,10},{10,1... | collective-permute-start | bytes 1671176 | tf_op jit(solution)/shard_map/ppermute | solution.py:518
  6.1 30.2 %collective-permute-start.1 = (bf16[272,1024]{1,0:T(8,128)(2,1)}, bf16[272,1024]{1,0:T(8,128)(2,1)}, u32[]{:S(2)}, u32[]{:S(2)}) collective-permute-start(bf16[272,1024]{1,0:T(8,128)(2,1)} %get-tuple-element.9), channel_id=1, source_target_pairs={{1,0},{2,1},{3,2},{4,3},{5,4},{6,5},{7,6},{8,7},{9,8},{10,9},{11,1... | collective-permute-start | bytes 1671176 | tf_op jit(solution)/shard_map/ppermute | solution.py:519
  71.8 1.0 %copy-start = (bf16[512,256]{1,0:T(8,128)(2,1)S(1)}, bf16[512,256]{1,0:T(8,128)(2,1)}, u32[]{:S(2)}) copy-start(bf16[512,256]{1,0:T(8,128)(2,1)} %params_ref.1) | copy-start | bytes 786436
